TPU v7x, 32 devices: a whole 2x2x4 slice. The times are simulated.
32 devices in a mesh: feature: 4 (over y, x), kvhead: 2 (over core), seq: 4 (over z).
Axes of the slice: x: 2, y: 2, z: 4, core: 2. Of those that a mesh axis runs over, the one named last changes fastest.
Arguments:
- queries: float32 [1024, 40, 128], P('seq', 'kvhead'), may hold values from -6 to 6
- keys: float32 [1024, 8, 128], P('seq', 'kvhead'), may hold values from -6 to 6
- values: float32 [1024, 8, 128], P('seq', 'kvhead'), may hold values from -6 to 6
- w_out: float32 [5120, 5120], P('kvhead', ('feature', 'seq')), may hold values from -0.078125 to 0.078125
Outputs:
- projected: float32 [1024, 5120], P(('seq', 'feature'), 'kvhead')
All inputs are finite; a program needn't handle non-finite values.
Results may differ from a plain program's by a relative error of at most 0.0003.
Values sent between devices are 32-bit elements; how exact they have to be, the bound alone decides.
No kernel may reach another device: no remote copies, remote signals or barrier semaphores. Data moves between devices by JAX's collectives and lax.ppermute only.
A program may use at most 192 MiB of HBM per device.

v0:
```python
import math

import jax
import jax.numpy as jnp
import numpy as np
from jax import lax
from jax.sharding import PartitionSpec as P


def prefix(part, axis, combine, identity):
    place = lax.axis_index(axis)
    gathered = jax.tree.map(lambda a: lax.all_gather(a, axis), part)
    state = jax.tree.map(lambda a, e: jnp.zeros_like(a) + jnp.asarray(e, a.dtype), part, identity)

    def one(lap, state):
        return combine(
            state, jax.tree.map(lambda a: lax.dynamic_index_in_dim(a, lap, 0, False), gathered)
        )

    return lax.fori_loop(0, place, one, state)


def expand(vectors, select_first, select_second, factor):
    highest = lax.Precision.HIGHEST
    left = jnp.einsum("...d,df->...f", vectors, select_first, precision=highest)
    right = jnp.einsum("...d,df->...f", vectors, select_second, precision=highest)
    return left * right * factor


def add_pair(earlier, later):
    return (earlier[0] + later[0], earlier[1] + later[1])


def local(queries, keys, values, w_out):
    rows, local_heads, head_size = queries.shape
    kv_local = keys.shape[1]
    group = local_heads // kv_local
    parts = lax.axis_size("feature")
    position = lax.axis_index("feature")
    width = head_size * (head_size + 1) // 2 // parts
    upper_i, upper_j = np.triu_indices(head_size)
    factor_table = np.where(upper_i == upper_j, 1.0, math.sqrt(2.0)).astype(np.float32)
    first = lax.dynamic_slice_in_dim(jnp.asarray(upper_i.astype(np.int32)), position * width, width)
    second = lax.dynamic_slice_in_dim(
        jnp.asarray(upper_j.astype(np.int32)), position * width, width
    )
    factor = lax.dynamic_slice_in_dim(jnp.asarray(factor_table), position * width, width)
    entries = jnp.arange(head_size, dtype=jnp.int32)
    select_first = (entries[:, None] == first[None, :]).astype(jnp.float32)
    select_second = (entries[:, None] == second[None, :]).astype(jnp.float32)
    quarter = rows // parts
    scaled = (queries * head_size ** (-0.5)).reshape(rows, kv_local, group, head_size)
    highest = lax.Precision.HIGHEST
    block_states = []
    block_norms = []
    for block in range(parts):
        key_part = keys[block * quarter : (block + 1) * quarter]
        lifted = expand(key_part, select_first, select_second, factor)
        block_states.append(
            jnp.einsum(
                "tkf,tkd->kfd",
                lifted,
                values[block * quarter : (block + 1) * quarter],
                precision=highest,
            )
        )
        block_norms.append(jnp.sum(lifted, axis=0))
    total_state = sum(block_states)
    total_norm = sum(block_norms)
    identity = (jnp.zeros_like(total_state), jnp.zeros_like(total_norm))
    prior_state, prior_norm = prefix((total_state, total_norm), "seq", add_pair, identity)
    running_state = prior_state
    running_norm = prior_norm
    numerators = []
    denominators = []
    for block in range(parts):
        lifted_query = expand(
            scaled[block * quarter : (block + 1) * quarter], select_first, select_second, factor
        )
        numerators.append(
            jnp.einsum("tkgf,kfd->tkgd", lifted_query, running_state, precision=highest)
        )
        denominators.append(
            jnp.einsum("tkgf,kf->tkg", lifted_query, running_norm, precision=highest)
        )
        running_state = running_state + block_states[block]
        running_norm = running_norm + block_norms[block]
    numerator = jnp.concatenate(numerators, axis=0)
    denominator = jnp.concatenate(denominators, axis=0)
    own_start = position * quarter
    own_query = lax.dynamic_slice_in_dim(scaled, own_start, quarter, 0)
    own_key = lax.dynamic_slice_in_dim(keys, own_start, quarter, 0)
    own_value = lax.dynamic_slice_in_dim(values, own_start, quarter, 0)
    scores = jnp.einsum("tkgd,skd->kgts", own_query, own_key, precision=highest)
    causal = jnp.tril(jnp.ones((quarter, quarter), jnp.bool_))
    squared = jnp.where(causal[None, None], scores * scores, jnp.float32(0.0))
    inner_numerator = jnp.einsum("kgts,skd->tkgd", squared, own_value, precision=highest)
    inner_denominator = jnp.transpose(jnp.sum(squared, axis=-1), (2, 0, 1))
    numerator = lax.dynamic_update_slice_in_dim(
        numerator,
        lax.dynamic_slice_in_dim(numerator, own_start, quarter, 0) + inner_numerator,
        own_start,
        0,
    )
    denominator = lax.dynamic_update_slice_in_dim(
        denominator,
        lax.dynamic_slice_in_dim(denominator, own_start, quarter, 0) + inner_denominator,
        own_start,
        0,
    )
    whole_numerator, whole_denominator = lax.psum((numerator, denominator), "feature")
    share_numerator = lax.dynamic_slice_in_dim(whole_numerator, own_start, quarter, 0)
    share_denominator = lax.dynamic_slice_in_dim(whole_denominator, own_start, quarter, 0)
    attended = (share_numerator / (share_denominator[..., None] + 1.0)).reshape(
        quarter, local_heads * head_size
    )
    partial_out = jnp.dot(
        attended,
        lax.all_gather(w_out, ("feature", "seq"), axis=1, tiled=True),
        precision=highest,
        preferred_element_type=jnp.float32,
    )
    return lax.psum_scatter(partial_out, "kvhead", scatter_dimension=1, tiled=True)


def solution(mesh):
    in_specs = (
        P("seq", "kvhead", None),
        P("seq", "kvhead", None),
        P("seq", "kvhead", None),
        P("kvhead", ("feature", "seq")),
    )
    out_specs = P(("seq", "feature"), "kvhead")
    return jax.shard_map(local, mesh=mesh, in_specs=in_specs, out_specs=out_specs, check_vma=False)
```

profile of v0, /device:TPU:0, one launch (start us, length us, event | category | flops | bytes accessed | tf_op | source)
XLA Modules:
  0.0 1027.6 jit_solution(5140327394291576662)
XLA Ops:
  9.7 1.4 constant_dynamic-slice_fusion
  20.2 1.4 fusion.110
  21.6 7.4 fusion.81
  29.0 6.9 fusion.83
  36.0 7.1 fusion.85
  43.1 1.9 copy-done.1
  45.0 8.6 convolution_add_fusion
  53.7 15.3 %all-gather.2 = f32[4,4,2064]{2,1,0:T(4,128)S(1)} all-gather(f32[1,4,2064]{2,1,0:T(4,128)S(1)} %add_bitcast_fusion.1), channel_id=3, replica_groups=mesh['feature'=4,'kvhead'=2,'seq'=4] {'seq'}, dimensions={0}, use_global_device_ids=true | all-gather | bytes 165120 | tf_op jit(solution)/shard_map/all_gather | solution.py:12
  69.3 3.2 fusion.112
  72.6 7.2 fusion.55
  79.9 7.7 fusion.57
  87.6 4.7 fusion.59
  92.3 4.8 fusion.61
  97.1 10.2 multiply_multiply_fusion
  107.3 10.8 %multiply_multiply_fusion.1 = f32[64,4,5,2064]{3,0,2,1:T(8,128)} fusion(f32[64,4,5,2064]{3,0,2,1:T(8,128)} %fusion.57, f32[64,4,5,128]{3,0,2,1:T(8,128)S(1)} %bitcast.168, f32[2064]{0:T(1024)S(1)} %dynamic_slice.40, s32[2064]{0:T(1024)S(1)} %dynamic_slice.39), kind=kOutput, calls=%fused_computation.3 | convolution fusion | flops 4063537152 | bytes 21807232 | tf_op jit(solution)/shard_map/...d,df->...f/dot_general | solution.py:26
  118.2 8.0 multiply_multiply_fusion.2
  126.1 8.0 multiply_multiply_fusion.3
  134.1 212.9 %all-gather.8.cloned.1.call-done = f32[16,2064,128]{2,1,0:T(8,128)} async-done(((f32[4,2064,128]{2,1,0:T(8,128)}), f32[16,2064,128]{2,1,0:T(8,128)}) %all-gather.8.cloned.1.call-update) | async-done | bytes 16908304 | tf_op jit(solution)/shard_map/all_gather | solution.py:12
  347.0 2.2 broadcast_in_dim.13
  349.2 15.3 %fusion.28 = f32[64,4,5,128]{3,0,2,1:T(8,128)S(1)} fusion(f32[64,4,5,2064]{3,0,2,1:T(8,128)} %multiply_multiply_fusion, f32[4,2064,128]{2,1,0:T(8,128)} %copy-done.3, f32[4,2064,128]{2,1,0:T(8,128)} %copy-done.2, f32[4,2064,128]{2,1,0:T(8,128)} %get-tuple-element.39, f32[4,2064,128]{2,1,0:T(8,128)} %copy-done.1), kind=kOutput, calls=%fused_computation.36 | convolution fusion | flops 4061159424 | bytes 28131328 | tf_op jit(solution)/shard_map/tkgf,kfd->tkgd/dot_general | solution.py:81
  364.5 14.7 %fusion.25 = f32[64,4,5,128]{3,0,2,1:T(8,128)S(1)} fusion(f32[64,4,5,2064]{3,0,2,1:T(8,128)} %multiply_multiply_fusion.1, f32[4,2064,128]{2,1,0:T(8,128)} %copy-done.2, f32[4,2064,128]{2,1,0:T(8,128)} %get-tuple-element.39, f32[4,2064,128]{2,1,0:T(8,128)} %copy-done.1), kind=kOutput, calls=%fused_computation.35 | convolution fusion | flops 4060102656 | bytes 23904256 | tf_op jit(solution)/shard_map/tkgf,kfd->tkgd/dot_general | solution.py:81
  379.3 13.6 %fusion.22 = f32[64,4,5,128]{3,0,2,1:T(8,128)S(1)} fusion(f32[64,4,5,2064]{3,0,2,1:T(8,128)} %multiply_multiply_fusion.2, f32[4,2064,128]{2,1,0:T(8,128)S(1)} %copy-done, f32[4,2064,128]{2,1,0:T(8,128)} %copy-done.1), kind=kOutput, calls=%fused_computation.34 | convolution fusion | flops 4059045888 | bytes 19677184 | tf_op jit(solution)/shard_map/tkgf,kfd->tkgd/dot_general | solution.py:81
  392.9 12.6 %fusion.19 = f32[64,4,5,128]{3,0,2,1:T(8,128)S(1)} fusion(f32[64,4,5,2064]{3,0,2,1:T(8,128)} %multiply_multiply_fusion.3, f32[4,2064,128]{2,1,0:T(8,128)S(1)} %copy-done), kind=kOutput, calls=%fused_computation.33 | convolution fusion | flops 4057989120 | bytes 15450112 | tf_op jit(solution)/shard_map/tkgf,kfd->tkgd/dot_general | solution.py:81
  409.9 12.2 %fusion.95 = f32[4,1,64,5]{1,2,3,0:T(8,128)S(1)} fusion(f32[64,4,5,2064]{3,0,2,1:T(8,128)} %multiply_multiply_fusion, f32[4,2064,1,1]{1,0,2,3:T(4,128)S(1)} %get-tuple-element.68), kind=kOutput, calls=%fused_computation.91 | convolution fusion | flops 31703040 | bytes 10605824 | tf_op jit(solution)/shard_map/tkgf,kf->tkg/dot_general | solution.py:84
  422.6 11.9 %fusion.97 = f32[4,1,64,5]{1,2,3,0:T(8,128)S(1)} fusion(f32[64,4,5,2064]{3,0,2,1:T(8,128)} %multiply_multiply_fusion.1, f32[4,2064,1,1]{1,0,2,3:T(4,128)S(1)} %get-tuple-element.67), kind=kOutput, calls=%fused_computation.93 | convolution fusion | flops 31703040 | bytes 10605824 | tf_op jit(solution)/shard_map/tkgf,kf->tkg/dot_general | solution.py:84
  434.8 12.4 %fusion.99 = f32[4,1,64,5]{1,2,3,0:T(8,128)S(1)} fusion(f32[64,4,5,2064]{3,0,2,1:T(8,128)} %multiply_multiply_fusion.2, f32[4,2064,1,1]{1,0,2,3:T(4,128)S(1)} %get-tuple-element.69), kind=kOutput, calls=%fused_computation.95 | convolution fusion | flops 31703040 | bytes 10605824 | tf_op jit(solution)/shard_map/tkgf,kf->tkg/dot_general | solution.py:84
  447.6 12.0 %fusion.101 = f32[4,1,64,5]{1,2,3,0:T(8,128)S(1)} fusion(f32[64,4,5,2064]{3,0,2,1:T(8,128)} %multiply_multiply_fusion.3, f32[4,2064,1,1]{1,0,2,3:T(4,128)S(1)} %bitcast.172), kind=kOutput, calls=%fused_computation.97 | convolution fusion | flops 31703040 | bytes 10605824 | tf_op jit(solution)/shard_map/tkgf,kf->tkg/dot_general | solution.py:84
  460.3 17.5 %psum.15 = f32[256,4,5]{0,2,1:T(8,128)S(1)} all-reduce(f32[256,4,5]{0,2,1:T(8,128)S(1)} %dynamic_update_slice.7), channel_id=1, replica_groups=mesh['feature'=4,'kvhead'=2,'seq'=4] {'feature'}, use_global_device_ids=true, to_apply=%region_8.9 | all-reduce | flops 5120 | bytes 40960 | tf_op jit(solution)/shard_map/psum | solution.py:111
  477.9 41.3 %all-reduce.2.cloned.1.call-done = f32[256,4,5,128]{3,0,2,1:T(8,128)} async-done(((f32[256,4,5,128]{3,0,2,1:T(8,128)}), f32[256,4,5,128]{3,0,2,1:T(8,128)}) %all-reduce.2.cloned.1.call-update) | async-done | bytes 2621456 | tf_op jit(solution)/shard_map/psum | solution.py:111
  521.2 437.0 %all-gather.6.cloned.1.call-done = f32[2560,5120]{0,1:T(8,128)} async-done(((f32[2560,320]{0,1:T(8,128)}), f32[2560,5120]{0,1:T(8,128)}) %all-gather.6.cloned.1.call-update) | async-done | bytes 52428816 | tf_op jit(solution)/shard_map/all_gather | solution.py:119
  958.2 54.8 %fusion.113 = f32[64,5120]{1,0:T(8,128)} fusion(f32[64,2560]{1,0:T(8,128)S(1)} %reshape.52, f32[2560,5120]{0,1:T(8,128)} %all-gather.6.cloned.1.call-done), kind=kOutput, calls=%fused_computation.119 | convolution fusion | flops 10066329600 | bytes 54394880 | tf_op jit(solution)/shard_map/dot_general | solution.py:117
  1013.1 7.1 reduce-scatter.2.cloned.1.call-done
  (53 shorter events, 20.1 us)
Async XLA Ops:
  7.4 339.6 %all-gather.8.cloned.1.call-start = ((), (), s32[]{:S(2)}) async-start(), calls=%async_computation.4 | async-start | bytes 21135360 | tf_op jit(solution)/shard_map/all_gather | solution.py:12
  29.0 14.0 %copy-start.3 = (f32[4,2064,128]{2,1,0:T(8,128)}, f32[4,2064,128]{2,1,0:T(8,128)S(1)}, u32[]{:S(2)}) copy-start(f32[4,2064,128]{2,1,0:T(8,128)S(1)} %fusion.81) | copy-start | bytes 12681220
  36.0 7.1 copy-start.2
  43.1 2.0 copy-start.1
  53.6 15.4 %copy-start.6 = (f32[256,20,128]{2,0,1:T(8,128)S(1)}, f32[256,20,128]{2,0,1:T(8,128)}, u32[]{:S(2)}) copy-start(f32[256,20,128]{2,0,1:T(8,128)} %param.9) | copy-start | bytes 7864324
  53.7 465.6 %all-reduce.2.cloned.1.call-start = ((), (), s32[]{:S(2)}) async-start(), calls=%async_computation.1 | async-start | bytes 5242880 | tf_op jit(solution)/shard_map/psum | solution.py:111
  364.5 14.8 %copy-start = (f32[4,2064,128]{2,1,0:T(8,128)S(1)}, f32[4,2064,128]{2,1,0:T(8,128)}, u32[]{:S(2)}) copy-start(f32[4,2064,128]{2,1,0:T(8,128)} %get-tuple-element.39) | copy-start | bytes 12681220
  405.5 1.1 copy-start.5
  407.8 1.4 copy-start.4
  409.3 549.0 %all-gather.6.cloned.1.call-start = ((), (), s32[]{:S(2)}) async-start(), calls=%async_computation.2 | async-start | bytes 55705600 | tf_op jit(solution)/shard_map/all_gather | solution.py:119
  409.9 610.3 %reduce-scatter.2.cloned.1.call-start = ((), (), s32[]{:S(2)}) async-start(), calls=%async_computation.3 | async-start | bytes 1966080 | tf_op jit(solution)/shard_map/reduce_scatter | solution.py:123
  447.6 12.4 %copy-start.7 = (f32[4,5,64]{2,1,0:T(8,128)S(1)}, f32[4,5,64]{2,1,0:T(8,128)}, u32[]{:S(2)}) copy-start(f32[4,5,64]{2,1,0:T(8,128)} %get-tuple-element.78) | copy-start | bytes 15364
Sparse Core Ops, SparseCore 0:
  53.8 293.1 all-gather.7
  409.4 109.8 all-reduce.1
  1013.2 6.9 reduce-scatter.1
Sparse Core Ops, SparseCore 1:
  412.8 545.4 all-gather.5
where the time goes:
time: 1040 us; the launch traced here: 1030 us
  waiting for transfers between devices  699 us (67%)
  matrix products  266 us (26%)
  blocking collectives  32.8 us (3%)
  between operations  15.1 us (1%)
  local copies, waits for them, and re-layouts  12.8 us (1%)
    all_gather x1, waiting for transfers between devices, local(): lax.all_gather(w_out, ('feature', 'seq'), axis=1, tiled=True)  437 us
    all_gather x1, waiting for transfers between devices, prefix(): gathered = jax.tree.map(lambda a: lax.all_gather(a, axis), part)  213 us
    dot_general x4, matrix products, local(): jnp.einsum('tkgf,kfd->tkgd', lifted_query, running_state, precision=highest)  56.2 us
    dot_general x1, matrix products, local(): jnp.dot(attended, lax.all_gather(w_out, ('feature', 'seq'), axis=1, tiled...  54.8 us
    dot_general x4, matrix products, local(): jnp.einsum('tkgf,kf->tkg', lifted_query, running_norm, precision=highest)  48.5 us
    dot_general x8, matrix products, expand(): jnp.einsum('...d,df->...f', vectors, select_second, precision=highest)  42.8 us
    psum x1, waiting for transfers between devices, local(): lax.psum((numerator, denominator), 'feature')  41.3 us
    dot_general x4, matrix products, local(): jnp.einsum('tkf,tkd->kfd', lifted, values[block * quarter:(block + 1) * q...  30 us
  transfers between devices with their start and end apart: 4, of which 4 were waited for; matrix products, arithmetic and copies ran while one was open for 11% of the time, Pallas kernels for 0%

commit v1 on v0

v1 whole, which is shorter than its diff:
```python
import functools

import jax
import jax.numpy as jnp
from jax import lax
from jax.experimental import pallas as pl
from jax.experimental.pallas import tpu as pltpu
from jax.sharding import PartitionSpec as P

F32 = jnp.float32
BF16 = jnp.bfloat16
VMEM_LIMIT = 48 * 1024 * 1024
NT = (((1,), (1,)), ((), ()))


def split(a):
    high = a.astype(BF16)
    return high, (a - high.astype(F32)).astype(BF16)


def mm(a, b):
    return jnp.dot(a, b, preferred_element_type=F32)


def params():
    return pltpu.CompilerParams(vmem_limit_bytes=VMEM_LIMIT)


def smem():
    return pl.BlockSpec(memory_space=pltpu.SMEM)


def vmem(n):
    return [pl.BlockSpec(memory_space=pltpu.VMEM)] * n


def ring_at(place, n):
    half = (n + 1) // 2
    return jnp.where(place < half, 2 * place, 2 * (n - place) - 1)


def ring_place(index, n):
    return jnp.where(index % 2 == 0, index // 2, n - 1 - index // 2)


def ring_perm(n, step):
    order = list(range(0, n, 2)) + list(range(1, n, 2))[::-1]
    return [(order[i], order[(i + step) % n]) for i in range(n)]


def prepare_keys(pairs):
    n = len(pairs)
    _, rows, d = pairs[0].shape

    def kernel(*refs):
        kt, vv = refs[n:]
        for j in range(n):
            at = pl.ds(j * rows, rows)
            k_high, k_low = split(refs[j][0].T)
            kt[0:d, at] = k_high
            kt[d : 2 * d, at] = k_high
            kt[2 * d : 3 * d, at] = k_low
            v_high, v_low = split(refs[j][1])
            vv[at, 0:d] = v_high
            vv[at, d : 2 * d] = v_low
            below = pl.ds((n + j) * rows, rows)
            vv[below, 0:d] = v_high
            vv[below, d : 2 * d] = jnp.zeros((rows, d), BF16)

    return pl.pallas_call(
        kernel,
        out_shape=(
            jax.ShapeDtypeStruct((3 * d, n * rows), BF16),
            jax.ShapeDtypeStruct((2 * n * rows, 2 * d), BF16),
        ),
        in_specs=vmem(n),
        out_specs=tuple(vmem(2)),
        compiler_params=params(),
        cost_estimate=pl.CostEstimate(flops=0, bytes_accessed=6 * n * rows * d * 4, transcendentals=0),
        name="prepare_keys",
    )(*pairs)


def attend(meta, blocks, slots, kt, vv):
    group, rows, d = blocks[0].shape
    count = kt.shape[1] // rows
    n = len(blocks)
    scale = d ** (-0.5)

    def kernel(meta_ref, *refs):
        kt_ref, vv_ref, out = refs[n:]
        key_row = lax.broadcasted_iota(jnp.int32, (1, rows), 1)
        key_at = jnp.concatenate([key_row + meta_ref[j] * rows for j in range(count)], axis=1)
        row = lax.broadcasted_iota(jnp.int32, (rows, 1), 0)
        for i in range(n):
            allowed = key_at <= row + meta_ref[slots[i]] * rows

            def one(h, carry):
                q_high, q_low = split(refs[i][h] * scale)
                scores = mm(jnp.concatenate([q_high, q_low, q_high], axis=1), kt_ref[...])
                squared = jnp.where(allowed, scores * scores, 0.0)
                total = jnp.sum(squared, axis=1, keepdims=True)
                s_high, s_low = split(squared)
                both = mm(jnp.concatenate([s_high, s_low], axis=1), vv_ref[...])
                numerator = both[:, 0:d] + both[:, d : 2 * d]
                at = pl.ds(pl.multiple_of(h * d, d), d)
                out[pl.ds(i * rows, rows), at] = numerator / (total + 1.0)
                return carry

            lax.fori_loop(0, group, one, 0)

    return pl.pallas_call(
        kernel,
        out_shape=jax.ShapeDtypeStruct((n * rows, group * d), F32),
        in_specs=[smem()] + vmem(n + 2),
        out_specs=vmem(1)[0],
        compiler_params=params(),
        cost_estimate=pl.CostEstimate(
            flops=2 * n * group * rows * count * rows * d * 10,
            bytes_accessed=n * group * rows * d * 8 + kt.size * 2 + vv.size * 2,
            transcendentals=0,
        ),
        name="attend",
    )(meta, *blocks, kt, vv)


def prepare_weights(meta, pieces):
    n = len(pieces)
    columns, k = pieces[0].shape

    def kernel(meta_ref, *refs):
        high, low = refs[n:]
        for i in range(n):
            group, block = meta_ref[2 * i], meta_ref[2 * i + 1]
            at = pl.ds(pl.multiple_of(block * columns, 16), columns)
            w_high, w_low = split(refs[i][...])
            high[group, at] = w_high
            low[group, at] = w_low

    shape = jax.ShapeDtypeStruct((2, n // 2 * columns, k), BF16)
    return pl.pallas_call(
        kernel,
        out_shape=(shape, shape),
        in_specs=[smem()] + vmem(n),
        out_specs=tuple(vmem(2)),
        compiler_params=params(),
        cost_estimate=pl.CostEstimate(flops=0, bytes_accessed=n * columns * k * 8, transcendentals=0),
        name="prepare_weights",
    )(meta, *pieces)


def project(meta, own, other, high, low, parts, blocks):
    rows = own.shape[0] // blocks
    columns = high.shape[1]
    cut = rows // parts

    def kernel(meta_ref, own_ref, other_ref, high_ref, low_ref, *rest):
        outs, total = rest[:parts], rest[parts]
        core, place = meta_ref[0], meta_ref[1]
        acc = None
        for ref, group in ((own_ref, core), (other_ref, 1 - core)):
            a_high, a_low = split(ref[...])
            w_high, w_low = high_ref[group], low_ref[group]
            dot = functools.partial(lax.dot_general, dimension_numbers=NT, preferred_element_type=F32)
            term = dot(a_high, w_high) + dot(a_low, w_high) + dot(a_high, w_low)
            acc = term if acc is None else acc + term
        total[...] = acc
        for e in range(parts):
            for b in range(blocks):
                start = pl.multiple_of(b * rows + (place ^ e) * cut, 8)
                outs[e][b] = total[pl.ds(start, cut)]

    shape = jax.ShapeDtypeStruct((blocks, cut, columns), F32)
    return pl.pallas_call(
        kernel,
        out_shape=(shape,) * parts,
        in_specs=[smem()] + vmem(4),
        out_specs=tuple(vmem(parts)),
        scratch_shapes=[pltpu.VMEM((blocks * rows, columns), F32)],
        compiler_params=params(),
        cost_estimate=pl.CostEstimate(
            flops=2 * blocks * rows * columns * own.shape[1] * 6,
            bytes_accessed=high.size * 4 + own.size * 8 + blocks * rows * columns * 4,
            transcendentals=0,
        ),
        name="project",
    )(meta, own, other, high, low)


def assemble(meta, parts, halves):
    n = len(parts)
    rows, columns = parts[0].shape
    width = columns // halves

    def kernel(meta_ref, *refs):
        out, held = refs[n:]
        for j in range(n):
            held[meta_ref[j]] = refs[j][...]
        pieces = [
            held[z][:, h * width : (h + 1) * width] for h in range(halves) for z in range(n)
        ]
        out[...] = jnp.concatenate(pieces, axis=1)

    return pl.pallas_call(
        kernel,
        out_shape=jax.ShapeDtypeStruct((rows, n * columns), F32),
        in_specs=[smem()] + vmem(n),
        out_specs=vmem(1)[0],
        scratch_shapes=[pltpu.VMEM((n, rows, columns), F32)],
        compiler_params=params(),
        cost_estimate=pl.CostEstimate(flops=0, bytes_accessed=8 * n * rows * columns, transcendentals=0),
        name="assemble",
    )(meta, *parts)


def by_heads(queries, keys, values, w_out):
    rows, local_heads, d = queries.shape
    kv_local = keys.shape[1]
    group = local_heads // kv_local
    parts, planes = lax.axis_size("feature"), lax.axis_size("seq")
    f, c, s = (lax.axis_index(a) for a in ("feature", "kvhead", "seq"))
    at = ring_place(s, planes)
    ints = lambda *xs: jnp.stack([jnp.asarray(x, jnp.int32) for x in xs])
    held = [ring_at((at - j) % planes, planes) for j in range(planes)]
    sender = [ring_at((at + j) % planes, planes) for j in range(planes)]

    kv = jnp.stack(
        [lax.dynamic_index_in_dim(a, f, 1, False) for a in (keys, values)]
    )
    q = lax.dynamic_slice_in_dim(queries, f * group, group, 1).transpose(1, 0, 2)
    pairs, blocks = [kv], [q]
    for _ in range(planes - 1):
        pairs.append(lax.ppermute(pairs[-1], "seq", ring_perm(planes, 1)))
        blocks.append(lax.ppermute(blocks[-1], "seq", ring_perm(planes, 1)))

    k_rows = group * d
    pieces, places = [], []
    half = parts // 2
    b = f % half
    for k in range(parts):
        k1, k0 = k // 2, k % 2
        target = half * (b ^ k1) + (c ^ k0)
        piece = lax.dynamic_slice_in_dim(w_out, target * k_rows, k_rows, 0).T
        perm = []
        for fs in range(parts):
            for cs in range(2):
                perm.append((fs * 2 + cs, (half * ((fs % half) ^ k1) + (cs ^ k0)) * 2 + fs // half))
        pieces.append(lax.ppermute(piece, ("feature", "kvhead"), perm))
        places += [(f % 2) ^ k0, (f // half) ^ k1]
    high, low = prepare_weights(ints(*places), pieces)

    kt, vv = prepare_keys(pairs)
    meta = ints(*held)
    swap = [(0, 1), (1, 0)]
    results = [None] * planes
    for slots in ((0, 1), (2,), (3,)):
        own = attend(meta, [blocks[j] for j in slots], slots, kt, vv)
        other = lax.ppermute(own, "kvhead", swap)
        out = project(ints(c, f), own, other, high, low, parts, len(slots))
        total = out[0]
        for e in range(1, parts):
            total = total + lax.ppermute(out[e], "feature", [(i, i ^ e) for i in range(parts)])
        for i, j in enumerate(slots):
            piece = total[i]
            if j:
                piece = lax.ppermute(piece, "seq", ring_perm(planes, -j))
            results[j] = piece
    return assemble(ints(*sender), results, half)


def plain(queries, keys, values, w_out):
    highest = lax.Precision.HIGHEST
    rows, local_heads, d = queries.shape
    kv_local = keys.shape[1]
    parts, planes = lax.axis_size("feature"), lax.axis_size("seq")
    f, c, s = (lax.axis_index(a) for a in ("feature", "kvhead", "seq"))
    cut = rows // parts
    q = lax.dynamic_slice_in_dim(queries, f * cut, cut, 0) * d ** (-0.5)
    q = q.reshape(cut, kv_local, local_heads // kv_local, d)
    k = lax.all_gather(keys, "seq", axis=0, tiled=True)
    v = lax.all_gather(values, "seq", axis=0, tiled=True)
    scores = jnp.einsum("tkgd,skd->kgts", q, k, precision=highest)
    row = s * rows + f * cut + jnp.arange(cut)
    allowed = jnp.arange(k.shape[0])[None, :] <= row[:, None]
    squared = jnp.where(allowed, scores * scores, 0.0)
    numerator = jnp.einsum("kgts,skd->tkgd", squared, v, precision=highest)
    denominator = jnp.transpose(jnp.sum(squared, axis=-1), (2, 0, 1))
    attended = (numerator / (denominator[..., None] + 1.0)).reshape(cut, local_heads * d)
    attended = lax.all_gather(attended, ("seq", "feature"), axis=0, tiled=True)
    partial = jnp.dot(attended, w_out, precision=highest, preferred_element_type=F32)
    whole = lax.psum(partial, "kvhead")
    mine = lax.all_to_all(whole, ("seq", "feature"), 0, 1, tiled=True)
    columns = w_out.shape[1]
    mine = mine.reshape(cut, planes, parts, columns).transpose(0, 2, 1, 3).reshape(cut, -1)
    width = mine.shape[1] // lax.axis_size("kvhead")
    return lax.dynamic_slice_in_dim(mine, c * width, width, 1)


def solution(mesh):
    in_specs = (
        P("seq", "kvhead", None),
        P("seq", "kvhead", None),
        P("seq", "kvhead", None),
        P("kvhead", ("feature", "seq")),
    )
    out_specs = P(("seq", "feature"), "kvhead")

    def local(queries, keys, values, w_out):
        parts, groups = mesh.shape["feature"], mesh.shape["kvhead"]
        body = by_heads if (groups, parts, keys.shape[1]) == (2, 4, parts) else plain
        return body(queries, keys, values, w_out)

    return jax.shard_map(local, mesh=mesh, in_specs=in_specs, out_specs=out_specs, check_vma=False)
```

time: 1040 us -> 143 us (0.14); the launches traced: 1030 us -> 142 us
  waiting for transfers between devices: 699 us -> 48.4 us
  matrix products: 266 us -> 0 us
  Pallas kernels: 0 us -> 44.2 us
  starting transfers between devices: 0.13 us -> 42.2 us
  blocking collectives: 32.8 us -> 0 us
  between operations: 15.1 us -> 0.18 us
    all_gather x2 -> x0, waiting for transfers between devices: 650 us -> none  [the longest x1 437 us: local(): lax.all_gather(w_out, ('feature', 'seq'), axis=1, tiled=True)]
    dot_general x31 -> x0, matrix products: 266 us -> none  [the longest x4 56.2 us: local(): jnp.einsum('tkgf,kfd->tkgd', lifted_query, running_state, precision=highest)]
    ppermute x0 -> x25, waiting for transfers between devices: none -> 48.4 us  [the longest x3 20.2 us: by_heads(): pairs.append(lax.ppermute(pairs[-1], 'seq', ring_perm(planes, 1)))]
    pallas_call x0 -> x9, Pallas kernels: none -> 44.2 us  [the longest x3 25.8 us: attend(): pl.pallas_call(kernel, out_shape=jax.ShapeDtypeStruct((n * rows, group *...]
    ppermute x0 -> x25, starting transfers between devices: none -> 42.2 us  [the longest x4 12.6 us: by_heads(): pieces.append(lax.ppermute(piece, ('feature', 'kvhead'), perm))]
    psum x1 -> x0, waiting for transfers between devices: 41.3 us -> none  [local(): lax.psum((numerator, denominator), 'feature')]
    psum x1 -> x0, blocking collectives: 17.5 us -> none  [local(): lax.psum((numerator, denominator), 'feature')]
    all_gather x1 -> x0, blocking collectives: 15.3 us -> none  [prefix(): gathered = jax.tree.map(lambda a: lax.all_gather(a, axis), part)]
  transfers between devices with their start and end apart: 4 -> 25, of which waited for: 4 -> 9; matrix products, arithmetic and copies ran while one was open for 11% -> 4% of each run, Pallas kernels for 0% -> 30%
where the time goes in v1:
time: 143 us; the launch traced here: 142 us
  waiting for transfers between devices  48.4 us (34%)
  Pallas kernels  44.2 us (31%)
  starting transfers between devices  42.2 us (30%)
  local copies, waits for them, and re-layouts  5.52 us (4%)
  other arithmetic  1.72 us (1%)
    pallas_call x3, Pallas kernels, attend(): pl.pallas_call(kernel, out_shape=jax.ShapeDtypeStruct((n * rows, group *...  25.8 us
    ppermute x3, waiting for transfers between devices, by_heads(): pairs.append(lax.ppermute(pairs[-1], 'seq', ring_perm(planes, 1)))  20.2 us
    ppermute x9, waiting for transfers between devices, by_heads(): lax.ppermute(out[e], 'feature', [(i, i ^ e) for i in range(parts)])  15.9 us
    ppermute x4, starting transfers between devices, by_heads(): pieces.append(lax.ppermute(piece, ('feature', 'kvhead'), perm))  12.6 us
    pallas_call x3, Pallas kernels, project(): pl.pallas_call(kernel, out_shape=(shape,) * parts, in_specs=[smem()] + vm...  12.1 us
    ppermute x3, starting transfers between devices, by_heads(): pairs.append(lax.ppermute(pairs[-1], 'seq', ring_perm(planes, 1)))  11 us
    ppermute x9, starting transfers between devices, by_heads(): lax.ppermute(out[e], 'feature', [(i, i ^ e) for i in range(parts)])  10.6 us
    ppermute x4, waiting for transfers between devices, by_heads(): pieces.append(lax.ppermute(piece, ('feature', 'kvhead'), perm))  8.08 us
  transfers between devices with their start and end apart: 25, of which 9 were waited for; matrix products, arithmetic and copies ran while one was open for 4% of the time, Pallas kernels for 30%

profile of v1, /device:TPU:0, one launch (start us, length us, event | category | flops | bytes accessed | tf_op | source)
XLA Modules:
  0.0 142.2 jit_solution(8749614277272840909)
XLA Ops:
  0.0 1.6 %constant_dynamic-slice_fusion = (f32[256,1,128]{2,1,0:T(1,128)S(1)}, f32[256,1,128]{2,1,0:T(1,128)S(1)}) fusion(f32[256,4,128]{2,1,0:T(4,128)} %param.6, s32[]{:T(128)S(6)} %select_n.123, f32[256,4,128]{2,1,0:T(4,128)} %param.5), kind=kLoop, calls=%fused_computation.11 | loop fusion | bytes 524292 | tf_op jit(solution)/shard_map/jit(dynamic_index_in_dim)/dynamic_slice | solution.py:228
  1.7 4.1 %collective-permute-start.1 = (f32[2,256,128]{2,1,0:T(8,128)S(1)}, f32[2,256,128]{2,1,0:T(8,128)}, u32[]{:S(2)}, u32[]{:S(2)}) collective-permute-start(f32[2,256,128]{2,1,0:T(8,128)S(1)} %pad_maximum_fusion.refs_0_), channel_id=1, source_target_pairs={{0,2},{2,3},{3,1},{1,0},{4,6},{6,7},{7,5},{5,4},{8,10},{10,11},{11... | collective-permute-start | bytes 786440 | tf_op jit(solution)/shard_map/ppermute | solution.py:233
  5.8 1.6 %collective-permute-start = (f32[5,256,128]{2,1,0:T(8,128)S(1)}, f32[5,256,128]{2,1,0:T(8,128)}, u32[]{:S(2)}, u32[]{:S(2)}) collective-permute-start(f32[5,256,128]{2,1,0:T(8,128)S(1)} %dynamic-slice_bitcast_fusion.4.refs_0_), channel_id=1, source_target_pairs={{0,2},{2,3},{3,1},{1,0},{4,6},{6,7},{7,5},{5,4},{8,10},{10,11},{11... | collective-permute-start | bytes 1966088 | tf_op jit(solution)/shard_map/ppermute | solution.py:234
  7.4 5.0 %collective-permute-done.1.refs_1_ = f32[2,256,128]{2,1,0:T(8,128)} collective-permute-done((f32[2,256,128]{2,1,0:T(8,128)S(1)}, f32[2,256,128]{2,1,0:T(8,128)}, u32[]{:S(2)}, u32[]{:S(2)}) %collective-permute-start.1) | collective-permute-done | bytes 262176 | tf_op jit(solution)/shard_map/ppermute | solution.py:233
  12.5 3.5 %collective-permute-start.2 = (f32[2,256,128]{2,1,0:T(8,128)}, f32[2,256,128]{2,1,0:T(8,128)}, u32[]{:S(2)}, u32[]{:S(2)}) collective-permute-start(f32[2,256,128]{2,1,0:T(8,128)} %collective-permute-done.1.refs_1_), channel_id=1, source_target_pairs={{0,2},{2,3},{3,1},{1,0},{4,6},{6,7},{7,5},{5,4},{8,10},{10,11},{11... | collective-permute-start | bytes 786440 | tf_op jit(solution)/shard_map/ppermute | solution.py:233
  15.9 15.1 %collective-permute-done.2.refs_2_ = f32[2,256,128]{2,1,0:T(8,128)} collective-permute-done((f32[2,256,128]{2,1,0:T(8,128)}, f32[2,256,128]{2,1,0:T(8,128)}, u32[]{:S(2)}, u32[]{:S(2)}) %collective-permute-start.2) | collective-permute-done | bytes 262176 | tf_op jit(solution)/shard_map/ppermute | solution.py:233
  31.1 3.4 %collective-permute-start.3 = (f32[2,256,128]{2,1,0:T(8,128)}, f32[2,256,128]{2,1,0:T(8,128)}, u32[]{:S(2)}, u32[]{:S(2)}) collective-permute-start(f32[2,256,128]{2,1,0:T(8,128)} %collective-permute-done.2.refs_2_), channel_id=1, source_target_pairs={{0,2},{2,3},{3,1},{1,0},{4,6},{6,7},{7,5},{5,4},{8,10},{10,11},{11... | collective-permute-start | bytes 786440 | tf_op jit(solution)/shard_map/ppermute | solution.py:233
  34.5 3.7 %dynamic-slice_bitcast_fusion = (f32[320,640]{1,0:T(8,128)}, f32[320,640]{1,0:T(8,128)}, f32[320,640]{1,0:T(8,128)}, f32[320,640]{1,0:T(8,128)}) fusion(f32[2560,320]{0,1:T(8,128)} %param.7, s32[]{:T(128)S(6)} %select_n.129, s32[]{:T(128)S(6)} %select_n.127, s32[]{:T(128)S(6)} %select_n.126, s32[]{:T(128)S(6)} %select_n.128), kind=kLoop, calls=%fused_computation | loop fusion | bytes 6553616 | tf_op jit(solution)/shard_map/transpose | solution.py:243
  38.2 7.9 %collective-permute-start.5 = (f32[320,640]{1,0:T(8,128)}, f32[320,640]{1,0:T(8,128)}, u32[]{:S(2)}, u32[]{:S(2)}) collective-permute-start(f32[320,640]{1,0:T(8,128)} %get-tuple-element.39), channel_id=1, source_target_pairs={{0,0},{4,8},{8,16},{12,24},{16,4},{20,12},{24,20},{28,28},{1,1},{5... | collective-permute-start | bytes 2457608 | tf_op jit(solution)/shard_map/ppermute | solution.py:248
  46.8 1.4 prepare_keys.1
  48.3 12.7 %attend.3.own_ref = f32[512,640]{1,0:T(8,128)} custom-call(s32[4]{0:T(128)S(1)} %pad_add_fusion.2.meta_ref, f32[5,256,128]{2,1,0:T(8,128)S(1)} %dynamic-slice_bitcast_fusion.4.refs_0_, f32[5,256,128]{2,1,0:T(8,128)} %collective-permute-done.refs_1_, bf16[384,1024]{1,0:T(8,128)(2,1)S(1)} %get-tuple-element.21.refs_2_.refs_1_, ...), custom_call_target="tpu_custom_call" | custom-call | flops 6710886400 | bytes 4456448 | tf_op jit(solution)/shard_map/attend/pallas_call | solution.py:112
  61.1 4.7 %collective-permute-start.8 = (f32[320,640]{1,0:T(8,128)}, f32[320,640]{1,0:T(8,128)}, u32[]{:S(2)}, u32[]{:S(2)}) collective-permute-start(f32[320,640]{1,0:T(8,128)} %get-tuple-element.37), channel_id=1, source_target_pairs={{0,24},{4,16},{8,8},{12,0},{16,28},{20,20},{24,12},{28,4},{1,25},{... | collective-permute-start | bytes 2457608 | tf_op jit(solution)/shard_map/ppermute | solution.py:248
  65.9 1.5 %collective-permute-start.19 = (f32[5,256,128]{2,1,0:T(8,128)}, f32[5,256,128]{2,1,0:T(8,128)}, u32[]{:S(2)}, u32[]{:S(2)}) collective-permute-start(f32[5,256,128]{2,1,0:T(8,128)} %collective-permute-done.13.refs_0_), channel_id=1, source_target_pairs={{0,2},{2,3},{3,1},{1,0},{4,6},{6,7},{7,5},{5,4},{8,10},{10,11},{11... | collective-permute-start | bytes 1966088 | tf_op jit(solution)/shard_map/ppermute | solution.py:234
  67.4 7.0 %attend.4.own_ref = f32[256,640]{1,0:T(8,128)} custom-call(s32[4]{0:T(128)S(1)} %pad_add_fusion.2.meta_ref, f32[5,256,128]{2,1,0:T(8,128)} %collective-permute-done.13.refs_0_, bf16[384,1024]{1,0:T(8,128)(2,1)S(1)} %get-tuple-element.21.refs_2_.refs_1_, bf16[2048,256]{1,0:T(8,128)(2,1)S(1)} %get-tuple-element.22.refs_3_.refs_2_), custom_call_target="tpu_custom_call" | custom-call | flops 3355443200 | bytes 3145728 | tf_op jit(solution)/shard_map/attend/pallas_call | solution.py:112
  74.5 6.6 %collective-permute-done.7.refs_2_ = f32[320,640]{1,0:T(8,128)S(1)} collective-permute-done((f32[320,640]{1,0:T(8,128)}, f32[320,640]{1,0:T(8,128)S(1)}, u32[]{:S(2)}, u32[]{:S(2)}) %collective-permute-start.7) | collective-permute-done | bytes 819232 | tf_op jit(solution)/shard_map/ppermute | solution.py:248
  81.1 1.5 %collective-permute-done.8.refs_3_ = f32[320,640]{1,0:T(8,128)} collective-permute-done((f32[320,640]{1,0:T(8,128)}, f32[320,640]{1,0:T(8,128)}, u32[]{:S(2)}, u32[]{:S(2)}) %collective-permute-start.8) | collective-permute-done | bytes 819232 | tf_op jit(solution)/shard_map/ppermute | solution.py:248
  82.6 3.3 %prepare_weights.1 = (bf16[2,640,640]{2,1,0:T(8,128)(2,1)S(1)}, bf16[2,640,640]{2,1,0:T(8,128)(2,1)}) custom-call(s32[8]{0:T(128)S(1)} %stack.90.meta_ref, f32[320,640]{1,0:T(8,128)} %collective-permute-done.5.refs_0_, f32[320,640]{1,0:T(8,128)} %collective-permute-done.6.refs_1_, f32[320,640]{1,0:T(8,128)S(1)} %collective-permute-done.7.refs_2_, ...), custom_call_target="tpu_custom_call" | custom-call | bytes 6553600 | tf_op jit(solution)/shard_map/prepare_weights/pallas_call | solution.py:141
  85.9 6.2 %attend.5.own_ref = f32[256,640]{1,0:T(8,128)S(1)} custom-call(s32[4]{0:T(128)S(1)} %pad_add_fusion.2.meta_ref, f32[5,256,128]{2,1,0:T(8,128)} %collective-permute-done.19.refs_0_, bf16[384,1024]{1,0:T(8,128)(2,1)S(1)} %copy-done.6, bf16[2048,256]{1,0:T(8,128)(2,1)S(1)} %copy-done.4), custom_call_target="tpu_custom_call" | custom-call | flops 3355443200 | bytes 3145728 | tf_op jit(solution)/shard_map/attend/pallas_call | solution.py:112
  92.8 3.4 %project.4 = (f32[1,64,640]{2,1,0:T(8,128)S(1)}, f32[1,64,640]{2,1,0:T(8,128)S(1)}, f32[1,64,640]{2,1,0:T(8,128)S(1)}, f32[1,64,640]{2,1,0:T(8,128)S(1)}) custom-call(s32[2]{0:T(128)S(1)} %pad_add_fusion.1.meta_ref, f32[256,640]{1,0:T(8,128)} %attend.4.own_ref, f32[256,640]{1,0:T(8,128)} %collective-permute-done.14.other_ref, ...), custom_call_target="tpu_custom_call" | custom-call | flops 1258291200 | bytes 5242880 | tf_op jit(solution)/shard_map/project/pallas_call | solution.py:174
  97.5 2.3 %collective-permute-start.17 = (f32[1,64,640]{2,1,0:T(8,128)S(1)}, f32[1,64,640]{2,1,0:T(8,128)S(1)}, u32[]{:S(2)}, u32[]{:S(2)}) collective-permute-start(f32[1,64,640]{2,1,0:T(8,128)S(1)} %get-tuple-element.32), channel_id=1, source_target_pairs={{0,24},{8,16},{16,8},{24,0},{1,25},{9,17},{17,9},{25,1},{2,26},{10... | collective-permute-start | bytes 491528 | tf_op jit(solution)/shard_map/ppermute | solution.py:262
  99.8 6.0 %project.3 = (f32[2,64,640]{2,1,0:T(8,128)S(1)}, f32[2,64,640]{2,1,0:T(8,128)S(1)}, f32[2,64,640]{2,1,0:T(8,128)S(1)}, f32[2,64,640]{2,1,0:T(8,128)S(1)}) custom-call(s32[2]{0:T(128)S(1)} %pad_add_fusion.1.meta_ref, f32[512,640]{1,0:T(8,128)} %attend.3.own_ref, f32[512,640]{1,0:T(8,128)} %collective-permute-done.4.other_ref, ...), custom_call_target="tpu_custom_call" | custom-call | flops 2516582400 | bytes 7208960 | tf_op jit(solution)/shard_map/project/pallas_call | solution.py:174
  105.9 1.5 %collective-permute-start.11 = (f32[2,64,640]{2,1,0:T(8,128)S(1)}, f32[2,64,640]{2,1,0:T(8,128)S(1)}, u32[]{:S(2)}, u32[]{:S(2)}) collective-permute-start(f32[2,64,640]{2,1,0:T(8,128)S(1)} %get-tuple-element.28), channel_id=1, source_target_pairs={{0,24},{8,16},{16,8},{24,0},{1,25},{9,17},{17,9},{25,1},{2,26},{10... | collective-permute-start | bytes 983048 | tf_op jit(solution)/shard_map/ppermute | solution.py:262
  107.4 1.9 %collective-permute-start.9 = (f32[2,64,640]{2,1,0:T(8,128)S(1)}, f32[2,64,640]{2,1,0:T(8,128)S(1)}, u32[]{:S(2)}, u32[]{:S(2)}) collective-permute-start(f32[2,64,640]{2,1,0:T(8,128)S(1)} %get-tuple-element.26), channel_id=1, source_target_pairs={{0,8},{8,0},{16,24},{24,16},{1,9},{9,1},{17,25},{25,17},{2,10},{10... | collective-permute-start | bytes 983048 | tf_op jit(solution)/shard_map/ppermute | solution.py:262
  110.8 10.9 %collective-permute-done.10 = f32[2,64,640]{2,1,0:T(8,128)S(1)} collective-permute-done((f32[2,64,640]{2,1,0:T(8,128)S(1)}, f32[2,64,640]{2,1,0:T(8,128)S(1)}, u32[]{:S(2)}, u32[]{:S(2)}) %collective-permute-start.10) | collective-permute-done | bytes 327712 | tf_op jit(solution)/shard_map/ppermute | solution.py:262
  123.0 2.7 %project.5 = (f32[1,64,640]{2,1,0:T(8,128)S(1)}, f32[1,64,640]{2,1,0:T(8,128)S(1)}, f32[1,64,640]{2,1,0:T(8,128)S(1)}, f32[1,64,640]{2,1,0:T(8,128)S(1)}) custom-call(s32[2]{0:T(128)S(1)} %pad_add_fusion.1.meta_ref, f32[256,640]{1,0:T(8,128)S(1)} %attend.5.own_ref, f32[256,640]{1,0:T(8,128)S(1)} %collective-permute-done.20.other_ref, ...), custom_call_target="tpu_custom_call" | custom-call | flops 1258291200 | bytes 5242880 | tf_op jit(solution)/shard_map/project/pallas_call | solution.py:174
  126.1 1.3 collective-permute-start.22
  127.4 1.8 %collective-permute-start.23 = (f32[1,64,640]{2,1,0:T(8,128)S(1)}, f32[1,64,640]{2,1,0:T(8,128)S(1)}, u32[]{:S(2)}, u32[]{:S(2)}) collective-permute-start(f32[1,64,640]{2,1,0:T(8,128)S(1)} %get-tuple-element.36), channel_id=1, source_target_pairs={{0,24},{8,16},{16,8},{24,0},{1,25},{9,17},{17,9},{25,1},{2,26},{10... | collective-permute-start | bytes 491528 | tf_op jit(solution)/shard_map/ppermute | solution.py:262
  129.3 1.4 collective-permute-start.12
  131.7 2.7 %collective-permute-done.22 = f32[1,64,640]{2,1,0:T(8,128)S(1)} collective-permute-done((f32[1,64,640]{2,1,0:T(8,128)S(1)}, f32[1,64,640]{2,1,0:T(8,128)S(1)}, u32[]{:S(2)}, u32[]{:S(2)}) %collective-permute-start.22) | collective-permute-done | bytes 163872 | tf_op jit(solution)/shard_map/ppermute | solution.py:262
  135.1 1.2 collective-permute-start.24
  136.4 4.2 %collective-permute-done.24.refs_3_ = f32[64,640]{1,0:T(8,128)S(1)} collective-permute-done((f32[64,640]{1,0:T(8,128)}, f32[64,640]{1,0:T(8,128)S(1)}, u32[]{:S(2)}, u32[]{:S(2)}) %collective-permute-start.24) | collective-permute-done | bytes 163872 | tf_op jit(solution)/shard_map/ppermute | solution.py:266
  140.6 1.6 %assemble.1 = f32[64,2560]{1,0:T(8,128)} custom-call(s32[4]{0:T(128)S(1)} %pad_add_fusion.meta_ref, f32[64,640]{1,0:T(8,128)S(1)} %get-tuple-element.42.refs_0_, f32[64,640]{1,0:T(8,128)S(1)} %collective-permute-done.12.refs_1_, f32[64,640]{1,0:T(8,128)S(1)} %collective-permute-done.18.refs_2_, f32[64,640]{1,0:T(8,128)S(1)} %collective-permute-done.24.refs_3_), custom_call_target="tpu_custom_call" | custom-call | bytes 1310720 | tf_op jit(solution)/shard_map/assemble/pallas_call | solution.py:204
  (53 shorter events, 8.2 us)
Async XLA Ops:
  0.0 5.7 %copy-start = (f32[256,20,128]{2,0,1:T(8,128)S(1)}, f32[256,20,128]{2,0,1:T(8,128)}, u32[]{:S(2)}) copy-start(f32[256,20,128]{2,0,1:T(8,128)} %param.4) | copy-start | bytes 7864324
  1.7 10.8 %collective-permute-start.1 = (f32[2,256,128]{2,1,0:T(8,128)S(1)}, f32[2,256,128]{2,1,0:T(8,128)}, u32[]{:S(2)}, u32[]{:S(2)}) collective-permute-start(f32[2,256,128]{2,1,0:T(8,128)S(1)} %pad_maximum_fusion.refs_0_), channel_id=1, source_target_pairs={{0,2},{2,3},{3,1},{1,0},{4,6},{6,7},{7,5},{5,4},{8,10},{10,11},{11... | collective-permute-start | bytes 786440 | tf_op jit(solution)/shard_map/ppermute | solution.py:233
  5.8 40.3 %collective-permute-start = (f32[5,256,128]{2,1,0:T(8,128)S(1)}, f32[5,256,128]{2,1,0:T(8,128)}, u32[]{:S(2)}, u32[]{:S(2)}) collective-permute-start(f32[5,256,128]{2,1,0:T(8,128)S(1)} %dynamic-slice_bitcast_fusion.4.refs_0_), channel_id=1, source_target_pairs={{0,2},{2,3},{3,1},{1,0},{4,6},{6,7},{7,5},{5,4},{8,10},{10,11},{11... | collective-permute-start | bytes 1966088 | tf_op jit(solution)/shard_map/ppermute | solution.py:234
  12.5 18.6 %collective-permute-start.2 = (f32[2,256,128]{2,1,0:T(8,128)}, f32[2,256,128]{2,1,0:T(8,128)}, u32[]{:S(2)}, u32[]{:S(2)}) collective-permute-start(f32[2,256,128]{2,1,0:T(8,128)} %collective-permute-done.1.refs_1_), channel_id=1, source_target_pairs={{0,2},{2,3},{3,1},{1,0},{4,6},{6,7},{7,5},{5,4},{8,10},{10,11},{11... | collective-permute-start | bytes 786440 | tf_op jit(solution)/shard_map/ppermute | solution.py:233
  31.1 15.7 %collective-permute-start.3 = (f32[2,256,128]{2,1,0:T(8,128)}, f32[2,256,128]{2,1,0:T(8,128)}, u32[]{:S(2)}, u32[]{:S(2)}) collective-permute-start(f32[2,256,128]{2,1,0:T(8,128)} %collective-permute-done.2.refs_2_), channel_id=1, source_target_pairs={{0,2},{2,3},{3,1},{1,0},{4,6},{6,7},{7,5},{5,4},{8,10},{10,11},{11... | collective-permute-start | bytes 786440 | tf_op jit(solution)/shard_map/ppermute | solution.py:233
  38.2 23.0 %collective-permute-start.5 = (f32[320,640]{1,0:T(8,128)}, f32[320,640]{1,0:T(8,128)}, u32[]{:S(2)}, u32[]{:S(2)}) collective-permute-start(f32[320,640]{1,0:T(8,128)} %get-tuple-element.39), channel_id=1, source_target_pairs={{0,0},{4,8},{8,16},{12,24},{16,4},{20,12},{24,20},{28,28},{1,1},{5... | collective-permute-start | bytes 2457608 | tf_op jit(solution)/shard_map/ppermute | solution.py:248
  46.0 28.3 %collective-permute-start.6 = (f32[320,640]{1,0:T(8,128)}, f32[320,640]{1,0:T(8,128)}, u32[]{:S(2)}, u32[]{:S(2)}) collective-permute-start(f32[320,640]{1,0:T(8,128)} %get-tuple-element.38), channel_id=1, source_target_pairs={{0,8},{4,0},{8,24},{12,16},{16,12},{20,4},{24,28},{28,20},{1,9},{5... | collective-permute-start | bytes 2457608 | tf_op jit(solution)/shard_map/ppermute | solution.py:248
  46.1 19.7 %collective-permute-start.13 = (f32[5,256,128]{2,1,0:T(8,128)}, f32[5,256,128]{2,1,0:T(8,128)}, u32[]{:S(2)}, u32[]{:S(2)}) collective-permute-start(f32[5,256,128]{2,1,0:T(8,128)} %collective-permute-done.refs_1_), channel_id=1, source_target_pairs={{0,2},{2,3},{3,1},{1,0},{4,6},{6,7},{7,5},{5,4},{8,10},{10,11},{11... | collective-permute-start | bytes 1966088 | tf_op jit(solution)/shard_map/ppermute | solution.py:234
  48.2 19.1 %copy-start.3 = (bf16[2048,256]{1,0:T(8,128)(2,1)}, bf16[2048,256]{1,0:T(8,128)(2,1)S(1)}, u32[]{:S(2)}) copy-start(bf16[2048,256]{1,0:T(8,128)(2,1)S(1)} %get-tuple-element.22.refs_3_.refs_2_) | copy-start | bytes 3145732
  48.2 19.1 %copy-start.5 = (bf16[384,1024]{1,0:T(8,128)(2,1)}, bf16[384,1024]{1,0:T(8,128)(2,1)S(1)}, u32[]{:S(2)}) copy-start(bf16[384,1024]{1,0:T(8,128)(2,1)S(1)} %get-tuple-element.21.refs_2_.refs_1_) | copy-start | bytes 2359300
  60.9 38.9 %collective-permute-start.4 = (f32[512,640]{1,0:T(8,128)}, f32[512,640]{1,0:T(8,128)}, u32[]{:S(2)}, u32[]{:S(2)}) collective-permute-start(f32[512,640]{1,0:T(8,128)} %attend.3.own_ref), channel_id=1, source_target_pairs={{0,4},{4,0},{1,5},{5,1},{2,6},{6,2},{3,7},{7,3},{8,12},{12,8},{9,1... | collective-permute-start | bytes 3932168 | tf_op jit(solution)/shard_map/ppermute | solution.py:258
  61.1 20.0 %collective-permute-start.7 = (f32[320,640]{1,0:T(8,128)}, f32[320,640]{1,0:T(8,128)S(1)}, u32[]{:S(2)}, u32[]{:S(2)}) collective-permute-start(f32[320,640]{1,0:T(8,128)} %get-tuple-element.40), channel_id=1, source_target_pairs={{0,16},{4,24},{8,0},{12,8},{16,20},{20,28},{24,4},{28,12},{1,17},{... | collective-permute-start | bytes 2457608 | tf_op jit(solution)/shard_map/ppermute | solution.py:248
  61.1 21.4 %collective-permute-start.8 = (f32[320,640]{1,0:T(8,128)}, f32[320,640]{1,0:T(8,128)}, u32[]{:S(2)}, u32[]{:S(2)}) collective-permute-start(f32[320,640]{1,0:T(8,128)} %get-tuple-element.37), channel_id=1, source_target_pairs={{0,24},{4,16},{8,8},{12,0},{16,28},{20,20},{24,12},{28,4},{1,25},{... | collective-permute-start | bytes 2457608 | tf_op jit(solution)/shard_map/ppermute | solution.py:248
  65.9 20.0 %collective-permute-start.19 = (f32[5,256,128]{2,1,0:T(8,128)}, f32[5,256,128]{2,1,0:T(8,128)}, u32[]{:S(2)}, u32[]{:S(2)}) collective-permute-start(f32[5,256,128]{2,1,0:T(8,128)} %collective-permute-done.13.refs_0_), channel_id=1, source_target_pairs={{0,2},{2,3},{3,1},{1,0},{4,6},{6,7},{7,5},{5,4},{8,10},{10,11},{11... | collective-permute-start | bytes 1966088 | tf_op jit(solution)/shard_map/ppermute | solution.py:234
  74.3 18.4 %collective-permute-start.14 = (f32[256,640]{1,0:T(8,128)}, f32[256,640]{1,0:T(8,128)}, u32[]{:S(2)}, u32[]{:S(2)}) collective-permute-start(f32[256,640]{1,0:T(8,128)} %attend.4.own_ref), channel_id=1, source_target_pairs={{0,4},{4,0},{1,5},{5,1},{2,6},{6,2},{3,7},{7,3},{8,12},{12,8},{9,1... | collective-permute-start | bytes 1966088 | tf_op jit(solution)/shard_map/ppermute | solution.py:258
  74.4 11.4 %copy-start.4 = (bf16[2048,256]{1,0:T(8,128)(2,1)S(1)}, bf16[2048,256]{1,0:T(8,128)(2,1)}, u32[]{:S(2)}) copy-start(bf16[2048,256]{1,0:T(8,128)(2,1)} %copy-done.3) | copy-start | bytes 3145732
  74.4 11.5 %copy-start.6 = (bf16[384,1024]{1,0:T(8,128)(2,1)S(1)}, bf16[384,1024]{1,0:T(8,128)(2,1)}, u32[]{:S(2)}) copy-start(bf16[384,1024]{1,0:T(8,128)(2,1)} %copy-done.5) | copy-start | bytes 2359300
  85.9 6.9 %copy-start.1 = (bf16[2,640,640]{2,1,0:T(8,128)(2,1)S(1)}, bf16[2,640,640]{2,1,0:T(8,128)(2,1)}, u32[]{:S(2)}) copy-start(bf16[2,640,640]{2,1,0:T(8,128)(2,1)} %get-tuple-element.24.low_ref) | copy-start | bytes 4915204
  92.1 30.9 %collective-permute-start.20 = (f32[256,640]{1,0:T(8,128)S(1)}, f32[256,640]{1,0:T(8,128)S(1)}, u32[]{:S(2)}, u32[]{:S(2)}) collective-permute-start(f32[256,640]{1,0:T(8,128)S(1)} %attend.5.own_ref), channel_id=1, source_target_pairs={{0,4},{4,0},{1,5},{5,1},{2,6},{6,2},{3,7},{7,3},{8,12},{12,8},{9,1... | collective-permute-start | bytes 1966088 | tf_op jit(solution)/shard_map/ppermute | solution.py:258
  96.2 9.7 %collective-permute-start.15 = (f32[1,64,640]{2,1,0:T(8,128)S(1)}, f32[1,64,640]{2,1,0:T(8,128)S(1)}, u32[]{:S(2)}, u32[]{:S(2)}) collective-permute-start(f32[1,64,640]{2,1,0:T(8,128)S(1)} %get-tuple-element.30), channel_id=1, source_target_pairs={{0,8},{8,0},{16,24},{24,16},{1,9},{9,1},{17,25},{25,17},{2,10},{10... | collective-permute-start | bytes 491528 | tf_op jit(solution)/shard_map/ppermute | solution.py:262
  96.3 11.1 %collective-permute-start.16 = (f32[1,64,640]{2,1,0:T(8,128)S(1)}, f32[1,64,640]{2,1,0:T(8,128)S(1)}, u32[]{:S(2)}, u32[]{:S(2)}) collective-permute-start(f32[1,64,640]{2,1,0:T(8,128)S(1)} %get-tuple-element.31), channel_id=1, source_target_pairs={{0,16},{8,24},{16,0},{24,8},{1,17},{9,25},{17,1},{25,9},{2,18},{10... | collective-permute-start | bytes 491528 | tf_op jit(solution)/shard_map/ppermute | solution.py:262
  97.5 25.5 %copy-start.2 = (bf16[2,640,640]{2,1,0:T(8,128)(2,1)S(1)}, bf16[2,640,640]{2,1,0:T(8,128)(2,1)}, u32[]{:S(2)}) copy-start(bf16[2,640,640]{2,1,0:T(8,128)(2,1)} %get-tuple-element.24.low_ref) | copy-start | bytes 4915204
  97.5 11.9 %collective-permute-start.17 = (f32[1,64,640]{2,1,0:T(8,128)S(1)}, f32[1,64,640]{2,1,0:T(8,128)S(1)}, u32[]{:S(2)}, u32[]{:S(2)}) collective-permute-start(f32[1,64,640]{2,1,0:T(8,128)S(1)} %get-tuple-element.32), channel_id=1, source_target_pairs={{0,24},{8,16},{16,8},{24,0},{1,25},{9,17},{17,9},{25,1},{2,26},{10... | collective-permute-start | bytes 491528 | tf_op jit(solution)/shard_map/ppermute | solution.py:262
  105.8 15.9 %collective-permute-start.10 = (f32[2,64,640]{2,1,0:T(8,128)S(1)}, f32[2,64,640]{2,1,0:T(8,128)S(1)}, u32[]{:S(2)}, u32[]{:S(2)}) collective-permute-start(f32[2,64,640]{2,1,0:T(8,128)S(1)} %get-tuple-element.27), channel_id=1, source_target_pairs={{0,16},{8,24},{16,0},{24,8},{1,17},{9,25},{17,1},{25,9},{2,18},{10... | collective-permute-start | bytes 983048 | tf_op jit(solution)/shard_map/ppermute | solution.py:262
  105.9 15.8 %collective-permute-start.11 = (f32[2,64,640]{2,1,0:T(8,128)S(1)}, f32[2,64,640]{2,1,0:T(8,128)S(1)}, u32[]{:S(2)}, u32[]{:S(2)}) collective-permute-start(f32[2,64,640]{2,1,0:T(8,128)S(1)} %get-tuple-element.28), channel_id=1, source_target_pairs={{0,24},{8,16},{16,8},{24,0},{1,25},{9,17},{17,9},{25,1},{2,26},{10... | collective-permute-start | bytes 983048 | tf_op jit(solution)/shard_map/ppermute | solution.py:262
  107.4 15.5 %collective-permute-start.9 = (f32[2,64,640]{2,1,0:T(8,128)S(1)}, f32[2,64,640]{2,1,0:T(8,128)S(1)}, u32[]{:S(2)}, u32[]{:S(2)}) collective-permute-start(f32[2,64,640]{2,1,0:T(8,128)S(1)} %get-tuple-element.26), channel_id=1, source_target_pairs={{0,8},{8,0},{16,24},{24,16},{1,9},{9,1},{17,25},{25,17},{2,10},{10... | collective-permute-start | bytes 983048 | tf_op jit(solution)/shard_map/ppermute | solution.py:262
  110.1 26.3 %collective-permute-start.18 = (f32[64,640]{1,0:T(8,128)}, f32[64,640]{1,0:T(8,128)S(1)}, u32[]{:S(2)}, u32[]{:S(2)}) collective-permute-start(f32[64,640]{1,0:T(8,128)} %add_bitcast_fusion.1), channel_id=1, source_target_pairs={{0,3},{2,1},{3,0},{1,2},{4,7},{6,5},{7,4},{5,6},{8,11},{10,9},{11,... | collective-permute-start | bytes 491528 | tf_op jit(solution)/shard_map/ppermute | solution.py:266
  125.7 6.0 %collective-permute-start.21 = (f32[1,64,640]{2,1,0:T(8,128)S(1)}, f32[1,64,640]{2,1,0:T(8,128)S(1)}, u32[]{:S(2)}, u32[]{:S(2)}) collective-permute-start(f32[1,64,640]{2,1,0:T(8,128)S(1)} %get-tuple-element.34), channel_id=1, source_target_pairs={{0,8},{8,0},{16,24},{24,16},{1,9},{9,1},{17,25},{25,17},{2,10},{10... | collective-permute-start | bytes 491528 | tf_op jit(solution)/shard_map/ppermute | solution.py:262
  126.1 8.3 %collective-permute-start.22 = (f32[1,64,640]{2,1,0:T(8,128)S(1)}, f32[1,64,640]{2,1,0:T(8,128)S(1)}, u32[]{:S(2)}, u32[]{:S(2)}) collective-permute-start(f32[1,64,640]{2,1,0:T(8,128)S(1)} %get-tuple-element.35), channel_id=1, source_target_pairs={{0,16},{8,24},{16,0},{24,8},{1,17},{9,25},{17,1},{25,9},{2,18},{10... | collective-permute-start | bytes 491528 | tf_op jit(solution)/shard_map/ppermute | solution.py:262
  127.4 7.0 %collective-permute-start.23 = (f32[1,64,640]{2,1,0:T(8,128)S(1)}, f32[1,64,640]{2,1,0:T(8,128)S(1)}, u32[]{:S(2)}, u32[]{:S(2)}) collective-permute-start(f32[1,64,640]{2,1,0:T(8,128)S(1)} %get-tuple-element.36), channel_id=1, source_target_pairs={{0,24},{8,16},{16,8},{24,0},{1,25},{9,17},{17,9},{25,1},{2,26},{10... | collective-permute-start | bytes 491528 | tf_op jit(solution)/shard_map/ppermute | solution.py:262
  129.3 7.1 %collective-permute-start.12 = (f32[64,640]{1,0:T(8,128)S(1)}, f32[64,640]{1,0:T(8,128)S(1)}, u32[]{:S(2)}, u32[]{:S(2)}) collective-permute-start(f32[64,640]{1,0:T(8,128)S(1)} %get-tuple-element.41), channel_id=1, source_target_pairs={{0,1},{2,0},{3,2},{1,3},{4,5},{6,4},{7,6},{5,7},{8,9},{10,8},{11,1... | collective-permute-start | bytes 491528 | tf_op jit(solution)/shard_map/ppermute | solution.py:266
  135.1 5.5 %collective-permute-start.24 = (f32[64,640]{1,0:T(8,128)}, f32[64,640]{1,0:T(8,128)S(1)}, u32[]{:S(2)}, u32[]{:S(2)}) collective-permute-start(f32[64,640]{1,0:T(8,128)} %add_bitcast_fusion), channel_id=1, source_target_pairs={{0,2},{2,3},{3,1},{1,0},{4,6},{6,7},{7,5},{5,4},{8,10},{10,11},{11... | collective-permute-start | bytes 491528 | tf_op jit(solution)/shard_map/ppermute | solution.py:266

commit v2 on v1

v2 whole, which is shorter than its diff:
```python
import functools

import jax
import jax.numpy as jnp
from jax import lax
from jax.experimental import pallas as pl
from jax.experimental.pallas import tpu as pltpu
from jax.sharding import PartitionSpec as P

F32 = jnp.float32
BF16 = jnp.bfloat16
VMEM_LIMIT = 20 * 1024 * 1024
NT = (((1,), (1,)), ((), ()))


def split(a):
    high = a.astype(BF16)
    return high, (a - high.astype(F32)).astype(BF16)


def mm(a, b):
    return jnp.dot(a, b, preferred_element_type=F32)


def after(*arrays):
    return lax.optimization_barrier(arrays)


def brief(micros=0):
    return pl.CostEstimate(flops=1 + micros * 10**9, bytes_accessed=1, transcendentals=0)


def params():
    return pltpu.CompilerParams(vmem_limit_bytes=VMEM_LIMIT)


def smem():
    return pl.BlockSpec(memory_space=pltpu.SMEM)


def vmem(n):
    return [pl.BlockSpec(memory_space=pltpu.VMEM)] * n


def ring_at(place, n):
    half = (n + 1) // 2
    return jnp.where(place < half, 2 * place, 2 * (n - place) - 1)


def ring_place(index, n):
    return jnp.where(index % 2 == 0, index // 2, n - 1 - index // 2)


def ring_perm(n, step):
    order = list(range(0, n, 2)) + list(range(1, n, 2))[::-1]
    return [(order[i], order[(i + step) % n]) for i in range(n)]


def prepare_keys(pairs):
    n = len(pairs)
    _, rows, d = pairs[0].shape

    def kernel(*refs):
        kt, vv, held, sems = refs[n:]
        copies = [pltpu.make_async_copy(refs[j], held.at[j], sems.at[j]) for j in range(n)]
        for copy in copies:
            copy.start()
        for j in range(n):
            copies[j].wait()
            at = pl.ds(j * rows, rows)
            k_high, k_low = split(held[j, 0].T)
            kt[0:d, at] = k_high
            kt[d : 2 * d, at] = k_high
            kt[2 * d : 3 * d, at] = k_low
            v_high, v_low = split(held[j, 1])
            upper, lower = pl.ds(2 * j * rows, rows), pl.ds((2 * j + 1) * rows, rows)
            vv[upper, 0:d] = v_high
            vv[upper, d : 2 * d] = v_low
            vv[lower, 0:d] = v_high
            vv[lower, d : 2 * d] = jnp.zeros((rows, d), BF16)

    return pl.pallas_call(
        kernel,
        out_shape=(
            jax.ShapeDtypeStruct((3 * d, n * rows), BF16),
            jax.ShapeDtypeStruct((2 * n * rows, 2 * d), BF16),
        ),
        in_specs=[pl.BlockSpec(memory_space=pltpu.MemorySpace.HBM)] * n,
        out_specs=tuple(vmem(2)),
        scratch_shapes=[pltpu.VMEM((n, 2, rows, d), F32), pltpu.SemaphoreType.DMA((n,))],
        compiler_params=params(),
        cost_estimate=brief(0),
        name="prepare_keys",
    )(*pairs)


def attend(meta, blocks, slots, kt, vv):
    group, rows, d = blocks[0].shape
    count = kt.shape[1] // rows
    n = len(blocks)
    scale = d ** (-0.5)

    def kernel(meta_ref, *refs):
        kt_ref, vv_ref, out, parts, acc, den = refs[n:]
        shape = (rows, rows)
        keep = lax.broadcasted_iota(jnp.int32, shape, 1) <= lax.broadcasted_iota(jnp.int32, shape, 0)

        def chunk(j, own):
            for h in range(group):
                at = pl.ds(h * rows, rows)
                scores = mm(parts[at], kt_ref[:, pl.ds(j * rows, rows)])
                squared = scores * scores
                if own:
                    squared = jnp.where(keep, squared, 0.0)
                high, low = split(squared)
                both = mm(jnp.concatenate([high, low], axis=1), vv_ref[pl.ds(2 * j * rows, 2 * rows)])
                total = jnp.broadcast_to(jnp.sum(squared, axis=1, keepdims=True), (rows, d))
                if own:
                    acc[at], den[at] = both, total
                else:
                    acc[at] += both
                    den[at] += total

        for i, slot in enumerate(slots):
            high, low = split(refs[i][...].reshape(group * rows, d) * scale)
            parts[:, 0:d] = high
            parts[:, d : 2 * d] = low
            parts[:, 2 * d : 3 * d] = high
            chunk(slot, True)
            for j in range(count):
                if j != slot:
                    pl.when(meta_ref[j] < meta_ref[slot])(functools.partial(chunk, j, False))
            for h in range(group):
                at = pl.ds(h * rows, rows)
                numerator = acc[at, 0:d] + acc[at, d : 2 * d]
                out[pl.ds(i * rows, rows), h * d : (h + 1) * d] = numerator / (den[at] + 1.0)

    return pl.pallas_call(
        kernel,
        out_shape=jax.ShapeDtypeStruct((n * rows, group * d), F32),
        in_specs=[smem()] + vmem(n + 2),
        out_specs=vmem(1)[0],
        scratch_shapes=[
            pltpu.VMEM((group * rows, 3 * d), BF16),
            pltpu.VMEM((group * rows, 2 * d), F32),
            pltpu.VMEM((group * rows, d), F32),
        ],
        compiler_params=params(),
        cost_estimate=brief(),
        name="attend",
    )(meta, *blocks, kt, vv)


def prepare_weights(meta, pieces):
    n = len(pieces)
    columns, k = pieces[0].shape

    def kernel(meta_ref, *refs):
        high, low = refs[n:]
        for i in range(n):
            at = pl.ds(pl.multiple_of(meta_ref[2 * i + 1] * columns, 16), columns)
            w_high, w_low = split(refs[i][...])
            high[meta_ref[2 * i], at] = w_high
            low[meta_ref[2 * i], at] = w_low

    shape = jax.ShapeDtypeStruct((2, n // 2 * columns, k), BF16)
    return pl.pallas_call(
        kernel,
        out_shape=(shape, shape),
        in_specs=[smem()] + vmem(n),
        out_specs=tuple(vmem(2)),
        compiler_params=params(),
        cost_estimate=brief(),
        name="prepare_weights",
    )(meta, *pieces)


def project(blocks, high, low):
    n = len(blocks)
    rows = blocks[0].shape[0]
    columns = high.shape[1]

    def kernel(*refs):
        high_ref, low_ref = refs[n : n + 2]
        a_high, a_low = split(jnp.concatenate([ref[...] for ref in refs[:n]], axis=0))
        dot = functools.partial(lax.dot_general, dimension_numbers=NT, preferred_element_type=F32)
        for half, out in ((1, refs[-1]), (0, refs[-2])):
            w_high, w_low = high_ref[half], low_ref[half]
            out[...] = dot(a_high, w_high) + dot(a_low, w_high) + dot(a_high, w_low)

    shape = jax.ShapeDtypeStruct((n * rows, columns), F32)
    return pl.pallas_call(
        kernel,
        out_shape=(shape, shape),
        in_specs=vmem(n + 2),
        out_specs=tuple(vmem(2)),
        compiler_params=params(),
        cost_estimate=brief(),
        name="project",
    )(*blocks, high, low)


def fold(meta, kept, got, blocks, order):
    rows = kept.shape[0] // blocks
    cut = rows // sum(len(group) for group in order)
    columns = kept.shape[1]

    def kernel(meta_ref, kept_ref, got_ref, *outs):
        for out, group in zip(outs, order):
            for i, e in enumerate(group):
                for b in range(blocks):
                    at = pl.ds(pl.multiple_of(b * rows + (meta_ref[0] ^ e) * cut, 8), cut)
                    out[i, b] = kept_ref[at] + got_ref[at]

    return pl.pallas_call(
        kernel,
        out_shape=tuple(
            jax.ShapeDtypeStruct((len(group), blocks, cut, columns), F32) for group in order
        ),
        in_specs=[smem()] + vmem(2),
        out_specs=tuple(vmem(len(order))),
        compiler_params=params(),
        cost_estimate=brief(),
        name="fold",
    )(meta, kept, got)


def assemble(meta, parts, halves):
    n = len(parts)
    rows, columns = parts[0].shape
    width = columns // halves

    def kernel(meta_ref, *refs):
        out, held = refs[n:]
        for j in range(n):
            held[meta_ref[j]] = refs[j][...]
        pieces = [
            held[z][:, h * width : (h + 1) * width] for h in range(halves) for z in range(n)
        ]
        out[...] = jnp.concatenate(pieces, axis=1)

    return pl.pallas_call(
        kernel,
        out_shape=jax.ShapeDtypeStruct((rows, n * columns), F32),
        in_specs=[smem()] + vmem(n),
        out_specs=vmem(1)[0],
        scratch_shapes=[pltpu.VMEM((n, rows, columns), F32)],
        compiler_params=params(),
        cost_estimate=brief(),
        name="assemble",
    )(meta, *parts)


def by_heads(queries, keys, values, w_out):
    rows, local_heads, d = queries.shape
    kv_local = keys.shape[1]
    group = local_heads // kv_local
    parts, planes = lax.axis_size("feature"), lax.axis_size("seq")
    f, c, s = (lax.axis_index(a) for a in ("feature", "kvhead", "seq"))
    at = ring_place(s, planes)
    ints = lambda *xs: jnp.stack([jnp.asarray(x, jnp.int32) for x in xs])
    held = [ring_at((at - j) % planes, planes) for j in range(planes)]
    sender = [ring_at((at + j) % planes, planes) for j in range(planes)]

    ring = lambda x, step: lax.ppermute(x, "seq", ring_perm(planes, step))
    swap = lambda x: lax.ppermute(x, "kvhead", [(0, 1), (1, 0)])

    kv = jnp.stack([lax.dynamic_index_in_dim(a, f, 1, False) for a in (keys, values)])
    pairs = [ring(kv, j) if j else kv for j in range(planes)]

    k_rows = group * d
    half = parts // 2
    turn = lambda x: lax.dynamic_slice_in_dim(w_out, x * k_rows, k_rows, 0).T
    cross = lambda x, e: lax.ppermute(x, "feature", [(i, i ^ e) for i in range(parts)])
    pieces = [cross(turn(f ^ e), e) for e in range(1, parts)]
    places = []
    for e in range(parts):
        places += [jnp.where((f ^ e) // half == c, 0, 1), (f ^ e) % half]

    q = lax.dynamic_slice_in_dim(queries, f * group, group, 1).transpose(1, 0, 2)
    *pairs, sent = after(*pairs, q)
    sent = ring(sent, 1)
    kt, vv = prepare_keys(pairs)
    meta = ints(*held)
    owns = {0: attend(meta, [q], (0,), kt, vv)}
    sent, back, *pieces = after(sent, owns[0], *pieces)
    owns[planes - 1] = ring(back, -1)
    owns[1] = attend(meta, [sent], (1,), kt, vv)
    owns[1], mine = after(owns[1], f)
    owns[2] = ring(owns[1], 1)
    high, low = prepare_weights(ints(*places), [turn(mine)] + pieces)

    results = [None] * planes
    place = ints(f)
    last, crossed = None, None
    for slots, way in (((0, 1), 1), ((3,), 2), ((2,), 0)):
        blocks = [owns[j] for j in slots]
        if last is not None:
            *blocks, _ = after(*blocks, last)
        kept, given = project(blocks, high, low)
        if slots[0] == 0:
            given, owns[planes - 1] = after(given, owns[planes - 1])
        got = swap(given)
        if way:
            keep, send = fold(place, kept, got, len(slots), ((0, 3 - way), (way, 3)))
            last, send = after(keep, send)
            both = last + cross(send, way)
            crossed = both if crossed is None else crossed
            total = both[0] + cross(both[1], 3 - way)
        else:
            got, _ = after(got, crossed)
            outs = fold(place, kept, got, len(slots), tuple((e,) for e in range(parts)))
            total = outs[0]
            for e in range(1, parts):
                total = total + cross(outs[e], e)
            total = total[0]
        for i, j in enumerate(slots):
            results[j] = ring(total[i], -j) if j else total[i]
    return assemble(ints(*sender), [results[j] for j in range(planes)], half)


def plain(queries, keys, values, w_out):
    highest = lax.Precision.HIGHEST
    rows, local_heads, d = queries.shape
    kv_local = keys.shape[1]
    parts, planes = lax.axis_size("feature"), lax.axis_size("seq")
    f, c, s = (lax.axis_index(a) for a in ("feature", "kvhead", "seq"))
    cut = rows // parts
    q = lax.dynamic_slice_in_dim(queries, f * cut, cut, 0) * d ** (-0.5)
    q = q.reshape(cut, kv_local, local_heads // kv_local, d)
    k = lax.all_gather(keys, "seq", axis=0, tiled=True)
    v = lax.all_gather(values, "seq", axis=0, tiled=True)
    scores = jnp.einsum("tkgd,skd->kgts", q, k, precision=highest)
    row = s * rows + f * cut + jnp.arange(cut)
    allowed = jnp.arange(k.shape[0])[None, :] <= row[:, None]
    squared = jnp.where(allowed, scores * scores, 0.0)
    numerator = jnp.einsum("kgts,skd->tkgd", squared, v, precision=highest)
    denominator = jnp.transpose(jnp.sum(squared, axis=-1), (2, 0, 1))
    attended = (numerator / (denominator[..., None] + 1.0)).reshape(cut, local_heads * d)
    attended = lax.all_gather(attended, ("seq", "feature"), axis=0, tiled=True)
    partial = jnp.dot(attended, w_out, precision=highest, preferred_element_type=F32)
    whole = lax.psum(partial, "kvhead")
    mine = lax.all_to_all(whole, ("seq", "feature"), 0, 1, tiled=True)
    columns = w_out.shape[1]
    mine = mine.reshape(cut, planes, parts, columns).transpose(0, 2, 1, 3).reshape(cut, -1)
    width = mine.shape[1] // lax.axis_size("kvhead")
    return lax.dynamic_slice_in_dim(mine, c * width, width, 1)


def solution(mesh):
    in_specs = (
        P("seq", "kvhead", None),
        P("seq", "kvhead", None),
        P("seq", "kvhead", None),
        P("kvhead", ("feature", "seq")),
    )
    out_specs = P(("seq", "feature"), "kvhead")

    def local(queries, keys, values, w_out):
        parts, groups = mesh.shape["feature"], mesh.shape["kvhead"]
        body = by_heads if (groups, parts, keys.shape[1]) == (2, 4, parts) else plain
        return body(queries, keys, values, w_out)

    return jax.shard_map(local, mesh=mesh, in_specs=in_specs, out_specs=out_specs, check_vma=False)
```

time: 143 us -> 120 us (0.84)
  Pallas kernels: 44.2 us -> 21.6 us
  starting transfers between devices: 42.2 us -> 25.5 us
  waiting for transfers between devices: 48.4 us -> 56.8 us
  local copies, waits for them, and re-layouts: 5.52 us -> 13.6 us
    pallas_call x3 -> x2, Pallas kernels: 25.8 us -> 6.52 us  [attend(): pl.pallas_call(kernel, out_shape=jax.ShapeDtypeStruct((n * rows, group *...]
    ppermute x25 -> x22, starting transfers between devices: 42.2 us -> 25.5 us  [the longest x9 13 us: by_heads(): ring = lambda x, step: lax.ppermute(x, 'seq', ring_perm(planes, step))]
    ppermute x25 -> x22, waiting for transfers between devices: 48.4 us -> 56.8 us  [the longest x10 33.3 us: by_heads(): lax.ppermute(x, 'feature', [(i, i ^ e) for i in range(parts)])]
    unnamed x14 -> x22, local copies, waits for them, and re-layouts: 0.03 us -> 6.61 us
    pallas_call x3 -> x6, Pallas kernels: 12.1 us -> 10.2 us  [the longest x3 9.96 us: project(): pl.pallas_call(kernel, out_shape=(shape, shape), in_specs=vmem(n + 2), ou...]
    transpose x1 -> x2, local copies, waits for them, and re-layouts: 3.72 us -> 4.37 us  [by_heads(): turn = lambda x: lax.dynamic_slice_in_dim(w_out, x * k_rows, k_rows, 0).T]
  transfers between devices with their start and end apart: 25 -> 22, of which waited for: 9 -> 10; matrix products, arithmetic and copies ran while one was open for 4% -> 6% of each run, Pallas kernels for 30% -> 14%
where the time goes in v2:
time: 120 us; the launch traced here: 119 us
  waiting for transfers between devices  56.8 us (47%)
  starting transfers between devices  25.5 us (21%)
  Pallas kernels  21.6 us (18%)
  local copies, waits for them, and re-layouts  13.6 us (11%)
  other arithmetic  1.69 us (1%)
    ppermute x10, waiting for transfers between devices, by_heads(): lax.ppermute(x, 'feature', [(i, i ^ e) for i in range(parts)])  33.3 us
    ppermute x9, waiting for transfers between devices, by_heads(): ring = lambda x, step: lax.ppermute(x, 'seq', ring_perm(planes, step))  20.5 us
    ppermute x9, starting transfers between devices, by_heads(): ring = lambda x, step: lax.ppermute(x, 'seq', ring_perm(planes, step))  13 us
    ppermute x10, starting transfers between devices, by_heads(): lax.ppermute(x, 'feature', [(i, i ^ e) for i in range(parts)])  12.2 us
    pallas_call x3, Pallas kernels, project(): pl.pallas_call(kernel, out_shape=(shape, shape), in_specs=vmem(n + 2), ou...  9.96 us
    unnamed x22, local copies, waits for them, and re-layouts  6.61 us
    pallas_call x2, Pallas kernels, attend(): pl.pallas_call(kernel, out_shape=jax.ShapeDtypeStruct((n * rows, group *...  6.52 us
    transpose x2, local copies, waits for them, and re-layouts, by_heads(): turn = lambda x: lax.dynamic_slice_in_dim(w_out, x * k_rows, k_rows, 0).T  4.37 us
  transfers between devices with their start and end apart: 22, of which 10 were waited for; matrix products, arithmetic and copies ran while one was open for 6% of the time, Pallas kernels for 14%

profile of v2, /device:TPU:0, one launch (start us, length us, event | category | flops | bytes accessed | tf_op | source)
XLA Modules:
  0.0 119.4 jit_solution(14044520849508366864)
XLA Ops:
  0.0 1.6 %constant_dynamic-slice_fusion = (f32[256,1,128]{2,1,0:T(1,128)S(1)}, f32[256,1,128]{2,1,0:T(1,128)S(1)}) fusion(f32[256,4,128]{2,1,0:T(4,128)} %param.6, s32[]{:T(128)S(6)} %select_n.146, f32[256,4,128]{2,1,0:T(4,128)} %param.5), kind=kLoop, calls=%fused_computation.16 | loop fusion | bytes 524292 | tf_op jit(solution)/shard_map/jit(dynamic_index_in_dim)/dynamic_slice | solution.py:268
  1.7 4.1 %collective-permute-start = (f32[2,256,128]{2,1,0:T(8,128)S(1)}, f32[2,256,128]{2,1,0:T(8,128)S(1)}, u32[]{:S(2)}, u32[]{:S(2)}) collective-permute-start(f32[2,256,128]{2,1,0:T(8,128)S(1)} %pad_maximum_fusion.refs_0_), channel_id=1, source_target_pairs={{0,2},{2,3},{3,1},{1,0},{4,6},{6,7},{7,5},{5,4},{8,10},{10,11},{11... | collective-permute-start | bytes 786440 | tf_op jit(solution)/shard_map/ppermute | solution.py:265
  5.8 1.3 %collective-permute-start.1 = (f32[2,256,128]{2,1,0:T(8,128)S(1)}, f32[2,256,128]{2,1,0:T(8,128)S(1)}, u32[]{:S(2)}, u32[]{:S(2)}) collective-permute-start(f32[2,256,128]{2,1,0:T(8,128)S(1)} %pad_maximum_fusion.refs_0_), channel_id=1, source_target_pairs={{0,3},{2,1},{3,0},{1,2},{4,7},{6,5},{7,4},{5,6},{8,11},{10,9},{11,... | collective-permute-start | bytes 786440 | tf_op jit(solution)/shard_map/ppermute | solution.py:265
  7.9 3.1 %dynamic-slice_bitcast_fusion.1 = (f32[320,640]{1,0:T(8,128)}, f32[320,640]{1,0:T(8,128)}, f32[320,640]{1,0:T(8,128)}) fusion(f32[2560,320]{0,1:T(8,128)} %param.7, s32[]{:T(128)S(6)} %select_n.149, s32[]{:T(128)S(6)} %select_n.148, s32[]{:T(128)S(6)} %select_n.147), kind=kLoop, calls=%fused_computation.1 | loop fusion | bytes 4915212 | tf_op jit(solution)/shard_map/transpose | solution.py:273
  11.0 1.5 %collective-permute-start.4 = (f32[320,640]{1,0:T(8,128)}, f32[320,640]{1,0:T(8,128)}, u32[]{:S(2)}, u32[]{:S(2)}) collective-permute-start(f32[320,640]{1,0:T(8,128)} %get-tuple-element.77), channel_id=1, source_target_pairs={{0,8},{8,0},{16,24},{24,16},{1,9},{9,1},{17,25},{25,17},{2,10},{10... | collective-permute-start | bytes 2457608 | tf_op jit(solution)/shard_map/ppermute | solution.py:274
  12.5 1.5 %collective-permute-start.5 = (f32[320,640]{1,0:T(8,128)}, f32[320,640]{1,0:T(8,128)}, u32[]{:S(2)}, u32[]{:S(2)}) collective-permute-start(f32[320,640]{1,0:T(8,128)} %get-tuple-element.76), channel_id=1, source_target_pairs={{0,16},{8,24},{16,0},{24,8},{1,17},{9,25},{17,1},{25,9},{2,18},{10... | collective-permute-start | bytes 2457608 | tf_op jit(solution)/shard_map/ppermute | solution.py:274
  15.8 4.1 %collective-permute-done.1.refs_2_ = f32[2,256,128]{2,1,0:T(8,128)S(1)} collective-permute-done((f32[2,256,128]{2,1,0:T(8,128)S(1)}, f32[2,256,128]{2,1,0:T(8,128)S(1)}, u32[]{:S(2)}, u32[]{:S(2)}) %collective-permute-start.1) | collective-permute-done | bytes 262176 | tf_op jit(solution)/shard_map/ppermute | solution.py:265
  20.6 9.5 %collective-permute-done.2.refs_3_ = f32[2,256,128]{2,1,0:T(8,128)} collective-permute-done((f32[2,256,128]{2,1,0:T(8,128)S(1)}, f32[2,256,128]{2,1,0:T(8,128)}, u32[]{:S(2)}, u32[]{:S(2)}) %collective-permute-start.2) | collective-permute-done | bytes 262176 | tf_op jit(solution)/shard_map/ppermute | solution.py:265
  33.0 1.2 prepare_keys.1
  34.2 3.1 %attend.2.refs_0_ = f32[256,640]{1,0:T(8,128)} custom-call(s32[4]{0:T(128)S(1)} %pad_add_fusion.1.meta_ref, f32[5,256,128]{2,1,0:T(8,128)} %dynamic-slice_bitcast_fusion.4.refs_0_, bf16[384,1024]{1,0:T(8,128)(2,1)S(1)} %get-tuple-element.44.refs_1_, bf16[2048,256]{1,0:T(8,128)(2,1)S(1)} %get-tuple-element.45.refs_2_), custom_call_target="tpu_custom_call" | custom-call | flops 1 | bytes 1 | tf_op jit(solution)/shard_map/attend/pallas_call | solution.py:138
  38.3 11.0 %collective-permute-done.5.refs_2_ = f32[320,640]{1,0:T(8,128)} collective-permute-done((f32[320,640]{1,0:T(8,128)}, f32[320,640]{1,0:T(8,128)}, u32[]{:S(2)}, u32[]{:S(2)}) %collective-permute-start.5) | collective-permute-done | bytes 819232 | tf_op jit(solution)/shard_map/ppermute | solution.py:274
  49.2 2.2 %collective-permute-start.7 = (f32[256,640]{1,0:T(8,128)}, f32[256,640]{1,0:T(8,128)}, u32[]{:S(2)}, u32[]{:S(2)}) collective-permute-start(f32[256,640]{1,0:T(8,128)} %attend.2.refs_0_), channel_id=1, source_target_pairs={{0,1},{2,0},{3,2},{1,3},{4,5},{6,4},{7,6},{5,7},{8,9},{10,8},{11,1... | collective-permute-start | bytes 1966088 | tf_op jit(solution)/shard_map/ppermute | solution.py:265
  51.6 1.2 %copy-done.2 = bf16[2048,256]{1,0:T(8,128)(2,1)S(1)} copy-done((bf16[2048,256]{1,0:T(8,128)(2,1)S(1)}, bf16[2048,256]{1,0:T(8,128)(2,1)}, u32[]{:S(2)}) %copy-start.2) | copy-done | bytes 1048600
  52.8 3.4 %attend.3.refs_1_ = f32[256,640]{1,0:T(8,128)S(1)} custom-call(s32[4]{0:T(128)S(1)} %pad_add_fusion.1.meta_ref, f32[5,256,128]{2,1,0:T(8,128)} %collective-permute-done.3.refs_0_, bf16[384,1024]{1,0:T(8,128)(2,1)S(1)} %get-tuple-element.44.refs_1_, bf16[2048,256]{1,0:T(8,128)(2,1)S(1)} %copy-done.2), custom_call_target="tpu_custom_call" | custom-call | flops 1 | bytes 1 | tf_op jit(solution)/shard_map/attend/pallas_call | solution.py:138
  57.1 1.3 %dynamic-slice_bitcast_fusion.refs_0_ = f32[320,640]{1,0:T(8,128)S(1)} fusion(f32[2560,320]{0,1:T(8,128)} %param.7, s32[]{:T(128)S(6)} %select_n.162), kind=kLoop, calls=%fused_computation | loop fusion | bytes 1638404 | tf_op jit(solution)/shard_map/transpose | solution.py:273
  58.4 2.1 %prepare_weights.1 = (bf16[2,640,640]{2,1,0:T(8,128)(2,1)S(1)}, bf16[2,640,640]{2,1,0:T(8,128)(2,1)S(1)}) custom-call(s32[8]{0:T(128)S(1)} %stack.88.meta_ref, f32[320,640]{1,0:T(8,128)S(1)} %dynamic-slice_bitcast_fusion.refs_0_, f32[320,640]{1,0:T(8,128)} %collective-permute-done.4.refs_1_, f32[320,640]{1,0:T(8,128)} %collective-permute-done.5.refs_2_, ...), custom_call_target="tpu_custom_call" | custom-call | flops 1 | bytes 1 | tf_op jit(solution)/shard_map/prepare_weights/pallas_call | solution.py:167
  60.5 4.8 %project.3 = (f32[512,640]{1,0:T(8,128)S(1)}, f32[512,640]{1,0:T(8,128)S(1)}) custom-call(f32[256,640]{1,0:T(8,128)} %attend.2.refs_0_, f32[256,640]{1,0:T(8,128)S(1)} %copy-done.4, bf16[2,640,640]{2,1,0:T(8,128)(2,1)S(1)} %get-tuple-element.53.refs_2_.refs_1_, bf16[2,640,640]{2,1,0:T(8,128)(2,1)S(1)} %get-tuple-element.54.refs_3_.refs_2_), custom_call_target="tpu_custom_call" | custom-call | flops 1 | bytes 1 | tf_op jit(solution)/shard_map/project/pallas_call | solution.py:192
  65.3 3.0 %collective-permute-done.8.got_ref = f32[512,640]{1,0:T(8,128)S(1)} collective-permute-done((f32[512,640]{1,0:T(8,128)S(1)}, f32[512,640]{1,0:T(8,128)S(1)}, u32[]{:S(2)}, u32[]{:S(2)}) %collective-permute-start.8) | collective-permute-done | bytes 1310752 | tf_op jit(solution)/shard_map/ppermute | solution.py:266
  68.5 3.1 %project.4 = (f32[256,640]{1,0:T(8,128)S(1)}, f32[256,640]{1,0:T(8,128)S(1)}) custom-call(f32[256,640]{1,0:T(8,128)} %collective-permute-done.7.refs_0_, bf16[2,640,640]{2,1,0:T(8,128)(2,1)S(1)} %get-tuple-element.53.refs_2_.refs_1_, bf16[2,640,640]{2,1,0:T(8,128)(2,1)S(1)} %get-tuple-element.54.refs_3_.refs_2_), custom_call_target="tpu_custom_call" | custom-call | flops 1 | bytes 1 | tf_op jit(solution)/shard_map/project/pallas_call | solution.py:192
  71.8 1.3 %collective-permute-start.9 = (f32[2,2,64,640]{3,2,1,0:T(8,128)S(1)}, f32[2,2,64,640]{3,2,1,0:T(8,128)S(1)}, u32[]{:S(2)}, u32[]{:S(2)}) collective-permute-start(f32[2,2,64,640]{3,2,1,0:T(8,128)S(1)} %get-tuple-element.60), channel_id=1, source_target_pairs={{0,8},{8,0},{16,24},{24,16},{1,9},{9,1},{17,25},{25,17},{2,10},{10... | collective-permute-start | bytes 1966088 | tf_op jit(solution)/shard_map/ppermute | solution.py:274
  74.3 1.2 collective-permute-start.19
  75.5 13.4 %collective-permute-done.9 = f32[2,2,64,640]{3,2,1,0:T(8,128)S(1)} collective-permute-done((f32[2,2,64,640]{3,2,1,0:T(8,128)S(1)}, f32[2,2,64,640]{3,2,1,0:T(8,128)S(1)}, u32[]{:S(2)}, u32[]{:S(2)}) %collective-permute-start.9) | collective-permute-done | bytes 655392 | tf_op jit(solution)/shard_map/ppermute | solution.py:274
  88.9 1.6 %collective-permute-start.10 = (f32[2,64,640]{2,1,0:T(8,128)S(1)}, f32[2,64,640]{2,1,0:T(8,128)S(1)}, u32[]{:S(2)}, u32[]{:S(2)}) collective-permute-start(f32[2,64,640]{2,1,0:T(8,128)S(1)} %slice_bitcast_fusion), channel_id=1, source_target_pairs={{0,16},{8,24},{16,0},{24,8},{1,17},{9,25},{17,1},{25,9},{2,18},{10... | collective-permute-start | bytes 983048 | tf_op jit(solution)/shard_map/ppermute | solution.py:274
  90.5 2.1 %project.5 = (f32[256,640]{1,0:T(8,128)S(1)}, f32[256,640]{1,0:T(8,128)S(1)}) custom-call(f32[256,640]{1,0:T(8,128)S(1)} %collective-permute-done.12.refs_0_, bf16[2,640,640]{2,1,0:T(8,128)(2,1)S(1)} %get-tuple-element.53.refs_2_.refs_1_, bf16[2,640,640]{2,1,0:T(8,128)(2,1)S(1)} %get-tuple-element.54.refs_3_.refs_2_), custom_call_target="tpu_custom_call" | custom-call | flops 1 | bytes 1 | tf_op jit(solution)/shard_map/project/pallas_call | solution.py:192
  93.5 4.7 %collective-permute-done.10 = f32[2,64,640]{2,1,0:T(8,128)S(1)} collective-permute-done((f32[2,64,640]{2,1,0:T(8,128)S(1)}, f32[2,64,640]{2,1,0:T(8,128)S(1)}, u32[]{:S(2)}, u32[]{:S(2)}) %collective-permute-start.10) | collective-permute-done | bytes 327712 | tf_op jit(solution)/shard_map/ppermute | solution.py:274
  98.2 2.4 %collective-permute-start.11 = (f32[64,640]{1,0:T(8,128)S(1)}, f32[64,640]{1,0:T(8,128)S(1)}, u32[]{:S(2)}, u32[]{:S(2)}) collective-permute-start(f32[64,640]{1,0:T(8,128)S(1)} %get-tuple-element.78), channel_id=1, source_target_pairs={{0,1},{2,0},{3,2},{1,3},{4,5},{6,4},{7,6},{5,7},{8,9},{10,8},{11,1... | collective-permute-start | bytes 491528 | tf_op jit(solution)/shard_map/ppermute | solution.py:265
  100.7 1.6 %collective-permute-start.17 = (f32[1,1,64,640]{3,2,1,0:T(8,128)S(1)}, f32[1,1,64,640]{3,2,1,0:T(8,128)S(1)}, u32[]{:S(2)}, u32[]{:S(2)}) collective-permute-start(f32[1,1,64,640]{3,2,1,0:T(8,128)S(1)} %get-tuple-element.73), channel_id=1, source_target_pairs={{0,24},{8,16},{16,8},{24,0},{1,25},{9,17},{17,9},{25,1},{2,26},{10... | collective-permute-start | bytes 491528 | tf_op jit(solution)/shard_map/ppermute | solution.py:274
  102.3 1.2 collective-permute-start.16
  105.5 2.5 %collective-permute-done.17 = f32[1,1,64,640]{3,2,1,0:T(8,128)S(1)} collective-permute-done((f32[1,1,64,640]{3,2,1,0:T(8,128)S(1)}, f32[1,1,64,640]{3,2,1,0:T(8,128)S(1)}, u32[]{:S(2)}, u32[]{:S(2)}) %collective-permute-start.17) | collective-permute-done | bytes 163872 | tf_op jit(solution)/shard_map/ppermute | solution.py:274
  108.0 1.7 %collective-permute-done.16 = f32[1,1,64,640]{3,2,1,0:T(8,128)S(1)} collective-permute-done((f32[1,1,64,640]{3,2,1,0:T(8,128)S(1)}, f32[1,1,64,640]{3,2,1,0:T(8,128)S(1)}, u32[]{:S(2)}, u32[]{:S(2)}) %collective-permute-start.16) | collective-permute-done | bytes 163872 | tf_op jit(solution)/shard_map/ppermute | solution.py:274
  110.9 6.9 %collective-permute-done.18.refs_2_ = f32[64,640]{1,0:T(8,128)S(1)} collective-permute-done((f32[64,640]{1,0:T(8,128)}, f32[64,640]{1,0:T(8,128)S(1)}, u32[]{:S(2)}, u32[]{:S(2)}) %collective-permute-start.18) | collective-permute-done | bytes 163872 | tf_op jit(solution)/shard_map/ppermute | solution.py:265
  117.8 1.6 %assemble.1 = f32[64,2560]{1,0:T(8,128)} custom-call(s32[4]{0:T(128)S(1)} %pad_add_fusion.meta_ref, f32[64,640]{1,0:T(8,128)S(1)} %get-tuple-element.79.refs_0_, f32[64,640]{1,0:T(8,128)S(1)} %collective-permute-done.11.refs_1_, f32[64,640]{1,0:T(8,128)S(1)} %collective-permute-done.18.refs_2_, f32[64,640]{1,0:T(8,128)S(1)} %collective-permute-done.21.refs_3_), custom_call_target="tpu_custom_call" | custom-call | flops 1 | bytes 1 | tf_op jit(solution)/shard_map/assemble/pallas_call | solution.py:242
  (61 shorter events, 14.2 us)
Async XLA Ops:
  0.0 15.0 %copy-start = (f32[256,20,128]{2,0,1:T(8,128)S(1)}, f32[256,20,128]{2,0,1:T(8,128)}, u32[]{:S(2)}) copy-start(f32[256,20,128]{2,0,1:T(8,128)} %param.4) | copy-start | bytes 7864324
  1.7 14.2 %copy-start.5 = (f32[2,256,128]{2,1,0:T(8,128)}, f32[2,256,128]{2,1,0:T(8,128)S(1)}, u32[]{:S(2)}) copy-start(f32[2,256,128]{2,1,0:T(8,128)S(1)} %pad_maximum_fusion.refs_0_) | copy-start | bytes 786436
  1.7 12.3 %collective-permute-start = (f32[2,256,128]{2,1,0:T(8,128)S(1)}, f32[2,256,128]{2,1,0:T(8,128)S(1)}, u32[]{:S(2)}, u32[]{:S(2)}) collective-permute-start(f32[2,256,128]{2,1,0:T(8,128)S(1)} %pad_maximum_fusion.refs_0_), channel_id=1, source_target_pairs={{0,2},{2,3},{3,1},{1,0},{4,6},{6,7},{7,5},{5,4},{8,10},{10,11},{11... | collective-permute-start | bytes 786440 | tf_op jit(solution)/shard_map/ppermute | solution.py:265
  5.8 14.2 %collective-permute-start.1 = (f32[2,256,128]{2,1,0:T(8,128)S(1)}, f32[2,256,128]{2,1,0:T(8,128)S(1)}, u32[]{:S(2)}, u32[]{:S(2)}) collective-permute-start(f32[2,256,128]{2,1,0:T(8,128)S(1)} %pad_maximum_fusion.refs_0_), channel_id=1, source_target_pairs={{0,3},{2,1},{3,0},{1,2},{4,7},{6,5},{7,4},{5,6},{8,11},{10,9},{11,... | collective-permute-start | bytes 786440 | tf_op jit(solution)/shard_map/ppermute | solution.py:265
  7.1 23.0 %collective-permute-start.2 = (f32[2,256,128]{2,1,0:T(8,128)S(1)}, f32[2,256,128]{2,1,0:T(8,128)}, u32[]{:S(2)}, u32[]{:S(2)}) collective-permute-start(f32[2,256,128]{2,1,0:T(8,128)S(1)} %pad_maximum_fusion.refs_0_), channel_id=1, source_target_pairs={{0,1},{2,0},{3,2},{1,3},{4,5},{6,4},{7,6},{5,7},{8,9},{10,8},{11,1... | collective-permute-start | bytes 786440 | tf_op jit(solution)/shard_map/ppermute | solution.py:265
  11.0 27.3 %collective-permute-start.4 = (f32[320,640]{1,0:T(8,128)}, f32[320,640]{1,0:T(8,128)}, u32[]{:S(2)}, u32[]{:S(2)}) collective-permute-start(f32[320,640]{1,0:T(8,128)} %get-tuple-element.77), channel_id=1, source_target_pairs={{0,8},{8,0},{16,24},{24,16},{1,9},{9,1},{17,25},{25,17},{2,10},{10... | collective-permute-start | bytes 2457608 | tf_op jit(solution)/shard_map/ppermute | solution.py:274
  12.5 36.7 %collective-permute-start.5 = (f32[320,640]{1,0:T(8,128)}, f32[320,640]{1,0:T(8,128)}, u32[]{:S(2)}, u32[]{:S(2)}) collective-permute-start(f32[320,640]{1,0:T(8,128)} %get-tuple-element.76), channel_id=1, source_target_pairs={{0,16},{8,24},{16,0},{24,8},{1,17},{9,25},{17,1},{25,9},{2,18},{10... | collective-permute-start | bytes 2457608 | tf_op jit(solution)/shard_map/ppermute | solution.py:274
  14.0 16.1 %copy-start.7 = (f32[2,256,128]{2,1,0:T(8,128)}, f32[2,256,128]{2,1,0:T(8,128)S(1)}, u32[]{:S(2)}) copy-start(f32[2,256,128]{2,1,0:T(8,128)S(1)} %collective-permute-done.refs_1_) | copy-start | bytes 786436
  14.0 35.2 %collective-permute-start.6 = (f32[320,640]{1,0:T(8,128)}, f32[320,640]{1,0:T(8,128)}, u32[]{:S(2)}, u32[]{:S(2)}) collective-permute-start(f32[320,640]{1,0:T(8,128)} %get-tuple-element.75), channel_id=1, source_target_pairs={{0,24},{8,16},{16,8},{24,0},{1,25},{9,17},{17,9},{25,1},{2,26},{10... | collective-permute-start | bytes 2457608 | tf_op jit(solution)/shard_map/ppermute | solution.py:274
  30.1 19.2 %collective-permute-start.3 = (f32[5,256,128]{2,1,0:T(8,128)}, f32[5,256,128]{2,1,0:T(8,128)}, u32[]{:S(2)}, u32[]{:S(2)}) collective-permute-start(f32[5,256,128]{2,1,0:T(8,128)} %dynamic-slice_bitcast_fusion.4.refs_0_), channel_id=1, source_target_pairs={{0,2},{2,3},{3,1},{1,0},{4,6},{6,7},{7,5},{5,4},{8,10},{10,11},{11... | collective-permute-start | bytes 1966088 | tf_op jit(solution)/shard_map/ppermute | solution.py:265
  30.2 1.0 copy-start.6
  31.1 0.9 copy-start.8
  32.1 0.9 copy-start.10
  37.3 1.0 copy-start.1
  49.2 16.0 %collective-permute-start.7 = (f32[256,640]{1,0:T(8,128)}, f32[256,640]{1,0:T(8,128)}, u32[]{:S(2)}, u32[]{:S(2)}) collective-permute-start(f32[256,640]{1,0:T(8,128)} %attend.2.refs_0_), channel_id=1, source_target_pairs={{0,1},{2,0},{3,2},{1,3},{4,5},{6,4},{7,6},{5,7},{8,9},{10,8},{11,1... | collective-permute-start | bytes 1966088 | tf_op jit(solution)/shard_map/ppermute | solution.py:265
  51.6 1.2 %copy-start.2 = (bf16[2048,256]{1,0:T(8,128)(2,1)S(1)}, bf16[2048,256]{1,0:T(8,128)(2,1)}, u32[]{:S(2)}) copy-start(bf16[2048,256]{1,0:T(8,128)(2,1)} %copy-done.1) | copy-start | bytes 3145732
  56.2 0.8 copy-start.3
  57.1 3.4 %copy-start.4 = (f32[256,640]{1,0:T(8,128)S(1)}, f32[256,640]{1,0:T(8,128)}, u32[]{:S(2)}) copy-start(f32[256,640]{1,0:T(8,128)} %copy-done.3) | copy-start | bytes 1966084
  65.3 3.1 %collective-permute-start.8 = (f32[512,640]{1,0:T(8,128)S(1)}, f32[512,640]{1,0:T(8,128)S(1)}, u32[]{:S(2)}, u32[]{:S(2)}) collective-permute-start(f32[512,640]{1,0:T(8,128)S(1)} %get-tuple-element.58), channel_id=1, source_target_pairs={{0,4},{4,0},{1,5},{5,1},{2,6},{6,2},{3,7},{7,3},{8,12},{12,8},{9,1... | collective-permute-start | bytes 3932168 | tf_op jit(solution)/shard_map/ppermute | solution.py:266
  71.6 2.6 %collective-permute-start.13 = (f32[256,640]{1,0:T(8,128)S(1)}, f32[256,640]{1,0:T(8,128)S(1)}, u32[]{:S(2)}, u32[]{:S(2)}) collective-permute-start(f32[256,640]{1,0:T(8,128)S(1)} %get-tuple-element.64), channel_id=1, source_target_pairs={{0,4},{4,0},{1,5},{5,1},{2,6},{6,2},{3,7},{7,3},{8,12},{12,8},{9,1... | collective-permute-start | bytes 1966088 | tf_op jit(solution)/shard_map/ppermute | solution.py:266
  71.8 17.0 %collective-permute-start.9 = (f32[2,2,64,640]{3,2,1,0:T(8,128)S(1)}, f32[2,2,64,640]{3,2,1,0:T(8,128)S(1)}, u32[]{:S(2)}, u32[]{:S(2)}) collective-permute-start(f32[2,2,64,640]{3,2,1,0:T(8,128)S(1)} %get-tuple-element.60), channel_id=1, source_target_pairs={{0,8},{8,0},{16,24},{24,16},{1,9},{9,1},{17,25},{25,17},{2,10},{10... | collective-permute-start | bytes 1966088 | tf_op jit(solution)/shard_map/ppermute | solution.py:274
  73.1 17.5 %collective-permute-start.12 = (f32[256,640]{1,0:T(8,128)S(1)}, f32[256,640]{1,0:T(8,128)S(1)}, u32[]{:S(2)}, u32[]{:S(2)}) collective-permute-start(f32[256,640]{1,0:T(8,128)S(1)} %copy-done.4), channel_id=1, source_target_pairs={{0,2},{2,3},{3,1},{1,0},{4,6},{6,7},{7,5},{5,4},{8,10},{10,11},{11... | collective-permute-start | bytes 1966088 | tf_op jit(solution)/shard_map/ppermute | solution.py:265
  74.3 18.4 %collective-permute-start.19 = (f32[2,1,64,640]{3,2,1,0:T(8,128)S(1)}, f32[2,1,64,640]{3,2,1,0:T(8,128)S(1)}, u32[]{:S(2)}, u32[]{:S(2)}) collective-permute-start(f32[2,1,64,640]{3,2,1,0:T(8,128)S(1)} %get-tuple-element.74), channel_id=1, source_target_pairs={{0,16},{8,24},{16,0},{24,8},{1,17},{9,25},{17,1},{25,9},{2,18},{10... | collective-permute-start | bytes 983048 | tf_op jit(solution)/shard_map/ppermute | solution.py:274
  88.9 9.2 %collective-permute-start.10 = (f32[2,64,640]{2,1,0:T(8,128)S(1)}, f32[2,64,640]{2,1,0:T(8,128)S(1)}, u32[]{:S(2)}, u32[]{:S(2)}) collective-permute-start(f32[2,64,640]{2,1,0:T(8,128)S(1)} %slice_bitcast_fusion), channel_id=1, source_target_pairs={{0,16},{8,24},{16,0},{24,8},{1,17},{9,25},{17,1},{25,9},{2,18},{10... | collective-permute-start | bytes 983048 | tf_op jit(solution)/shard_map/ppermute | solution.py:274
  92.6 8.0 %collective-permute-start.14 = (f32[256,640]{1,0:T(8,128)S(1)}, f32[256,640]{1,0:T(8,128)S(1)}, u32[]{:S(2)}, u32[]{:S(2)}) collective-permute-start(f32[256,640]{1,0:T(8,128)S(1)} %get-tuple-element.68), channel_id=1, source_target_pairs={{0,4},{4,0},{1,5},{5,1},{2,6},{6,2},{3,7},{7,3},{8,12},{12,8},{9,1... | collective-permute-start | bytes 1966088 | tf_op jit(solution)/shard_map/ppermute | solution.py:266
  92.8 11.5 %collective-permute-start.20 = (f32[1,64,640]{2,1,0:T(8,128)S(1)}, f32[1,64,640]{2,1,0:T(8,128)S(1)}, u32[]{:S(2)}, u32[]{:S(2)}) collective-permute-start(f32[1,64,640]{2,1,0:T(8,128)S(1)} %slice_bitcast_fusion.2), channel_id=1, source_target_pairs={{0,8},{8,0},{16,24},{24,16},{1,9},{9,1},{17,25},{25,17},{2,10},{10... | collective-permute-start | bytes 491528 | tf_op jit(solution)/shard_map/ppermute | solution.py:274
  98.2 12.7 %collective-permute-start.11 = (f32[64,640]{1,0:T(8,128)S(1)}, f32[64,640]{1,0:T(8,128)S(1)}, u32[]{:S(2)}, u32[]{:S(2)}) collective-permute-start(f32[64,640]{1,0:T(8,128)S(1)} %get-tuple-element.78), channel_id=1, source_target_pairs={{0,1},{2,0},{3,2},{1,3},{4,5},{6,4},{7,6},{5,7},{8,9},{10,8},{11,1... | collective-permute-start | bytes 491528 | tf_op jit(solution)/shard_map/ppermute | solution.py:265
  100.7 7.3 %collective-permute-start.17 = (f32[1,1,64,640]{3,2,1,0:T(8,128)S(1)}, f32[1,1,64,640]{3,2,1,0:T(8,128)S(1)}, u32[]{:S(2)}, u32[]{:S(2)}) collective-permute-start(f32[1,1,64,640]{3,2,1,0:T(8,128)S(1)} %get-tuple-element.73), channel_id=1, source_target_pairs={{0,24},{8,16},{16,8},{24,0},{1,25},{9,17},{17,9},{25,1},{2,26},{10... | collective-permute-start | bytes 491528 | tf_op jit(solution)/shard_map/ppermute | solution.py:274
  102.3 7.4 %collective-permute-start.16 = (f32[1,1,64,640]{3,2,1,0:T(8,128)S(1)}, f32[1,1,64,640]{3,2,1,0:T(8,128)S(1)}, u32[]{:S(2)}, u32[]{:S(2)}) collective-permute-start(f32[1,1,64,640]{3,2,1,0:T(8,128)S(1)} %get-tuple-element.72), channel_id=1, source_target_pairs={{0,16},{8,24},{16,0},{24,8},{1,17},{9,25},{17,1},{25,9},{2,18},{10... | collective-permute-start | bytes 491528 | tf_op jit(solution)/shard_map/ppermute | solution.py:274
  103.5 6.3 %collective-permute-start.15 = (f32[1,1,64,640]{3,2,1,0:T(8,128)S(1)}, f32[1,1,64,640]{3,2,1,0:T(8,128)S(1)}, u32[]{:S(2)}, u32[]{:S(2)}) collective-permute-start(f32[1,1,64,640]{3,2,1,0:T(8,128)S(1)} %get-tuple-element.71), channel_id=1, source_target_pairs={{0,8},{8,0},{16,24},{24,16},{1,9},{9,1},{17,25},{25,17},{2,10},{10... | collective-permute-start | bytes 491528 | tf_op jit(solution)/shard_map/ppermute | solution.py:274
  104.9 6.0 %collective-permute-start.21 = (f32[64,640]{1,0:T(8,128)}, f32[64,640]{1,0:T(8,128)S(1)}, u32[]{:S(2)}, u32[]{:S(2)}) collective-permute-start(f32[64,640]{1,0:T(8,128)} %fusion.2), channel_id=1, source_target_pairs={{0,2},{2,3},{3,1},{1,0},{4,6},{6,7},{7,5},{5,4},{8,10},{10,11},{11... | collective-permute-start | bytes 491528 | tf_op jit(solution)/shard_map/ppermute | solution.py:265
  110.5 7.4 %collective-permute-start.18 = (f32[64,640]{1,0:T(8,128)}, f32[64,640]{1,0:T(8,128)S(1)}, u32[]{:S(2)}, u32[]{:S(2)}) collective-permute-start(f32[64,640]{1,0:T(8,128)} %add_bitcast_fusion), channel_id=1, source_target_pairs={{0,3},{2,1},{3,0},{1,2},{4,7},{6,5},{7,4},{5,6},{8,11},{10,9},{11,... | collective-permute-start | bytes 491528 | tf_op jit(solution)/shard_map/ppermute | solution.py:265
  (1 other events, 0.7 us)

commit v3 on v2

--- a/solution.py
+++ b/solution.py
@@ -10,6 +10,7 @@
 F32 = jnp.float32
 BF16 = jnp.bfloat16
 VMEM_LIMIT = 20 * 1024 * 1024
+WHOLE = 60 * 1024 * 1024
 NT = (((1,), (1,)), ((), ()))
 
 
@@ -30,8 +31,8 @@
     return pl.CostEstimate(flops=1 + micros * 10**9, bytes_accessed=1, transcendentals=0)
 
 
-def params():
-    return pltpu.CompilerParams(vmem_limit_bytes=VMEM_LIMIT)
+def params(limit=VMEM_LIMIT):
+    return pltpu.CompilerParams(vmem_limit_bytes=limit)
 
 
 def smem():
@@ -88,16 +89,17 @@
         in_specs=[pl.BlockSpec(memory_space=pltpu.MemorySpace.HBM)] * n,
         out_specs=tuple(vmem(2)),
         scratch_shapes=[pltpu.VMEM((n, 2, rows, d), F32), pltpu.SemaphoreType.DMA((n,))],
-        compiler_params=params(),
+        compiler_params=params(WHOLE),
         cost_estimate=brief(0),
         name="prepare_keys",
     )(*pairs)
 
 
-def attend(meta, blocks, slots, kt, vv):
-    group, rows, d = blocks[0].shape
+def attend(meta, heads, slot, kt, vv):
+    _, rows, d = heads[0].shape
+    group = sum(part.shape[0] for part in heads)
     count = kt.shape[1] // rows
-    n = len(blocks)
+    n = len(heads)
     scale = d ** (-0.5)
 
     def kernel(meta_ref, *refs):
@@ -121,23 +123,27 @@
                     acc[at] += both
                     den[at] += total
 
-        for i, slot in enumerate(slots):
-            high, low = split(refs[i][...].reshape(group * rows, d) * scale)
-            parts[:, 0:d] = high
-            parts[:, d : 2 * d] = low
-            parts[:, 2 * d : 3 * d] = high
-            chunk(slot, True)
-            for j in range(count):
-                if j != slot:
-                    pl.when(meta_ref[j] < meta_ref[slot])(functools.partial(chunk, j, False))
-            for h in range(group):
-                at = pl.ds(h * rows, rows)
-                numerator = acc[at, 0:d] + acc[at, d : 2 * d]
-                out[pl.ds(i * rows, rows), h * d : (h + 1) * d] = numerator / (den[at] + 1.0)
-
-    return pl.pallas_call(
-        kernel,
-        out_shape=jax.ShapeDtypeStruct((n * rows, group * d), F32),
+        start = 0
+        for ref in refs[:n]:
+            m = ref.shape[0] * rows
+            at = pl.ds(start, m)
+            high, low = split(ref[...].reshape(m, d) * scale)
+            parts[at, 0:d] = high
+            parts[at, d : 2 * d] = low
+            parts[at, 2 * d : 3 * d] = high
+            start += m
+        chunk(slot, True)
+        for j in range(count):
+            if j != slot:
+                pl.when(meta_ref[j] < meta_ref[slot])(functools.partial(chunk, j, False))
+        for h in range(group):
+            at = pl.ds(h * rows, rows)
+            numerator = acc[at, 0:d] + acc[at, d : 2 * d]
+            out[:, h * d : (h + 1) * d] = numerator / (den[at] + 1.0)
+
+    return pl.pallas_call(
+        kernel,
+        out_shape=jax.ShapeDtypeStruct((rows, group * d), F32),
         in_specs=[smem()] + vmem(n + 2),
         out_specs=vmem(1)[0],
         scratch_shapes=[
@@ -145,10 +151,10 @@
             pltpu.VMEM((group * rows, 2 * d), F32),
             pltpu.VMEM((group * rows, d), F32),
         ],
-        compiler_params=params(),
+        compiler_params=params(WHOLE),
         cost_estimate=brief(),
         name="attend",
-    )(meta, *blocks, kt, vv)
+    )(meta, *heads, kt, vv)
 
 
 def prepare_weights(meta, pieces):
@@ -175,25 +181,28 @@
     )(meta, *pieces)
 
 
-def project(blocks, high, low):
+def project(blocks, high, low, half, chunks):
     n = len(blocks)
-    rows = blocks[0].shape[0]
+    rows = n * blocks[0].shape[0]
     columns = high.shape[1]
+    ends = [-(-rows * i // (16 * chunks)) * 16 for i in range(chunks + 1)]
 
     def kernel(*refs):
         high_ref, low_ref = refs[n : n + 2]
         a_high, a_low = split(jnp.concatenate([ref[...] for ref in refs[:n]], axis=0))
         dot = functools.partial(lax.dot_general, dimension_numbers=NT, preferred_element_type=F32)
-        for half, out in ((1, refs[-1]), (0, refs[-2])):
-            w_high, w_low = high_ref[half], low_ref[half]
-            out[...] = dot(a_high, w_high) + dot(a_low, w_high) + dot(a_high, w_low)
-
-    shape = jax.ShapeDtypeStruct((n * rows, columns), F32)
-    return pl.pallas_call(
-        kernel,
-        out_shape=(shape, shape),
+        w_high = high_ref[half]
+        total = dot(a_high, w_high) + dot(a_low, w_high) + dot(a_high, low_ref[half])
+        for i, ref in enumerate(refs[n + 2 :]):
+            ref[...] = total[ends[i] : ends[i + 1]]
+
+    return pl.pallas_call(
+        kernel,
+        out_shape=tuple(
+            jax.ShapeDtypeStruct((b - a, columns), F32) for a, b in zip(ends, ends[1:])
+        ),
         in_specs=vmem(n + 2),
-        out_specs=tuple(vmem(2)),
+        out_specs=tuple(vmem(chunks)),
         compiler_params=params(),
         cost_estimate=brief(),
         name="project",
@@ -204,25 +213,32 @@
     rows = kept.shape[0] // blocks
     cut = rows // sum(len(group) for group in order)
     columns = kept.shape[1]
-
-    def kernel(meta_ref, kept_ref, got_ref, *outs):
+    n = len(got)
+
+    def kernel(meta_ref, kept_ref, *refs):
+        outs, total = refs[n:-1], refs[-1]
+        start = 0
+        for ref in refs[:n]:
+            at = pl.ds(start, ref.shape[0])
+            total[at] = kept_ref[at] + ref[...]
+            start += ref.shape[0]
         for out, group in zip(outs, order):
             for i, e in enumerate(group):
                 for b in range(blocks):
-                    at = pl.ds(pl.multiple_of(b * rows + (meta_ref[0] ^ e) * cut, 8), cut)
-                    out[i, b] = kept_ref[at] + got_ref[at]
+                    out[i, b] = total[pl.ds(pl.multiple_of(b * rows + (meta_ref[0] ^ e) * cut, 8), cut)]
 
     return pl.pallas_call(
         kernel,
         out_shape=tuple(
             jax.ShapeDtypeStruct((len(group), blocks, cut, columns), F32) for group in order
         ),
-        in_specs=[smem()] + vmem(2),
+        in_specs=[smem()] + vmem(1 + n),
         out_specs=tuple(vmem(len(order))),
+        scratch_shapes=[pltpu.VMEM((blocks * rows, columns), F32)],
         compiler_params=params(),
         cost_estimate=brief(),
         name="fold",
-    )(meta, kept, got)
+    )(meta, kept, *got)
 
 
 def assemble(meta, parts, halves):
@@ -278,44 +294,43 @@
         places += [jnp.where((f ^ e) // half == c, 0, 1), (f ^ e) % half]
 
     q = lax.dynamic_slice_in_dim(queries, f * group, group, 1).transpose(1, 0, 2)
-    *pairs, sent = after(*pairs, q)
-    sent = ring(sent, 1)
+    *pairs, mine, meta, place, upper, lower = after(
+        *pairs, turn(f), ints(*held), ints(f), q[: group // 2], q[group // 2 :]
+    )
+    sent = [ring(upper, 1), ring(lower, 1)]
     kt, vv = prepare_keys(pairs)
-    meta = ints(*held)
-    owns = {0: attend(meta, [q], (0,), kt, vv)}
-    sent, back, *pieces = after(sent, owns[0], *pieces)
+    owns = {0: attend(meta, [upper, lower], 0, kt, vv)}
+    back, *sent = after(owns[0], *sent)
     owns[planes - 1] = ring(back, -1)
-    owns[1] = attend(meta, [sent], (1,), kt, vv)
-    owns[1], mine = after(owns[1], f)
+    sent[0], sent[1], *pieces = after(*sent, *pieces)
+    owns[1] = attend(meta, sent, 1, kt, vv)
     owns[2] = ring(owns[1], 1)
-    high, low = prepare_weights(ints(*places), [turn(mine)] + pieces)
-
-    results = [None] * planes
-    place = ints(f)
-    last, crossed = None, None
-    for slots, way in (((0, 1), 1), ((3,), 2), ((2,), 0)):
-        blocks = [owns[j] for j in slots]
-        if last is not None:
-            *blocks, _ = after(*blocks, last)
-        kept, given = project(blocks, high, low)
-        if slots[0] == 0:
-            given, owns[planes - 1] = after(given, owns[planes - 1])
-        got = swap(given)
-        if way:
-            keep, send = fold(place, kept, got, len(slots), ((0, 3 - way), (way, 3)))
-            last, send = after(keep, send)
-            both = last + cross(send, way)
-            crossed = both if crossed is None else crossed
-            total = both[0] + cross(both[1], 3 - way)
-        else:
-            got, _ = after(got, crossed)
-            outs = fold(place, kept, got, len(slots), tuple((e,) for e in range(parts)))
-            total = outs[0]
-            for e in range(1, parts):
-                total = total + cross(outs[e], e)
-            total = total[0]
-        for i, j in enumerate(slots):
-            results[j] = ring(total[i], -j) if j else total[i]
+    high, low = prepare_weights(ints(*places), [mine] + pieces)
+
+    exchange = lambda xs: [swap(x) for x in xs]
+    single = tuple((e,) for e in range(parts))
+    both = [owns[0], owns[1]]
+    given = exchange(project(both, high, low, 1, 4))
+    (kept,) = project(both, high, low, 0, 1)
+    owns[3], *given = after(owns[3], *given)
+    keep_a, send_a = fold(place, kept, given, 2, ((0, 2), (1, 3)))
+    owns[3], keep_a, send_a = after(owns[3], keep_a, send_a)
+    got_a = cross(send_a, 1)
+    given = exchange(project([owns[3]], high, low, 1, 3))
+    (kept,) = project([owns[3]], high, low, 0, 1)
+    keep_b, send_b = fold(place, kept, given, 1, ((0, 1), (2, 3)))
+    got_b = cross(send_b, 2)
+    owns[2], got_a, got_b = after(owns[2], got_a, got_b)
+    given = exchange(project([owns[2]], high, low, 1, 2))
+    (kept,) = project([owns[2]], high, low, 0, 1)
+    keep_a, keep_b = keep_a + got_a, keep_b + got_b
+    keep_c, *send_c = fold(place, kept, given, 1, single)
+    got_a, got_b = cross(keep_a[1], 2), cross(keep_b[1], 1)
+    total_a, total_b = keep_a[0] + got_a, keep_b[0] + got_b
+    total = keep_c
+    for e, x in enumerate(send_c):
+        total = total + cross(x, e + 1)
+    results = [total_a[0], ring(total_a[1], -1), ring(total[0, 0], -2), ring(total_b[0], -3)]
     return assemble(ints(*sender), [results[j] for j in range(planes)], half)
 
 

time: 120 us -> 113 us (0.942)
  waiting for transfers between devices: 56.8 us -> 39.3 us
  starting transfers between devices: 25.5 us -> 36.9 us
  local copies, waits for them, and re-layouts: 13.6 us -> 8.13 us
  Pallas kernels: 21.6 us -> 25.9 us
    ppermute x10, waiting for transfers between devices: 33.3 us -> 3.87 us  [by_heads(): lax.ppermute(x, 'feature', [(i, i ^ e) for i in range(parts)])]
    ppermute x9 -> x10, waiting for transfers between devices: 20.5 us -> 35.5 us  [by_heads(): ring = lambda x, step: lax.ppermute(x, 'seq', ring_perm(planes, step))]
    ppermute x9 -> x10, starting transfers between devices: 13 us -> 21.9 us  [by_heads(): ring = lambda x, step: lax.ppermute(x, 'seq', ring_perm(planes, step))]
    unnamed x22 -> x18, local copies, waits for them, and re-layouts: 6.61 us -> 2.67 us
    ppermute x3 -> x9, waiting for transfers between devices: 3.03 us -> 0.02 us  [by_heads(): swap = lambda x: lax.ppermute(x, 'kvhead', [(0, 1), (1, 0)])]
    pallas_call x5 -> x8, Pallas kernels: 16.5 us -> 19 us  [the longest x6 10.4 us: project(): pl.pallas_call(kernel, out_shape=tuple((jax.ShapeDtypeStruct((b - a, colu...]
    ppermute x3 -> x9, starting transfers between devices: 0.35 us -> 2.29 us  [by_heads(): swap = lambda x: lax.ppermute(x, 'kvhead', [(0, 1), (1, 0)])]
    pallas_call x1, Pallas kernels: 1.16 us -> 2.67 us  [prepare_keys(): pl.pallas_call(kernel, out_shape=(jax.ShapeDtypeStruct((3 * d, n * rows),...]
  transfers between devices with their start and end apart: 22 -> 29, of which waited for: 10 -> 10; matrix products, arithmetic and copies ran while one was open for 6% -> 5% of each run, Pallas kernels for 14% -> 21%
where the time goes in v3:
time: 113 us
  waiting for transfers between devices  39.3 us (35%)
  starting transfers between devices  36.9 us (33%)
  Pallas kernels  25.9 us (23%)
  local copies, waits for them, and re-layouts  8.13 us (7%)
  other arithmetic  2.23 us (2%)
    ppermute x10, waiting for transfers between devices, by_heads(): ring = lambda x, step: lax.ppermute(x, 'seq', ring_perm(planes, step))  35.5 us
    ppermute x10, starting transfers between devices, by_heads(): ring = lambda x, step: lax.ppermute(x, 'seq', ring_perm(planes, step))  21.9 us
    ppermute x10, starting transfers between devices, by_heads(): lax.ppermute(x, 'feature', [(i, i ^ e) for i in range(parts)])  12.7 us
    pallas_call x6, Pallas kernels, project(): pl.pallas_call(kernel, out_shape=tuple((jax.ShapeDtypeStruct((b - a, colu...  10.4 us
    pallas_call x2, Pallas kernels, attend(): pl.pallas_call(kernel, out_shape=jax.ShapeDtypeStruct((rows, group * d),...  8.57 us
    ppermute x10, waiting for transfers between devices, by_heads(): lax.ppermute(x, 'feature', [(i, i ^ e) for i in range(parts)])  3.87 us
    transpose x1, local copies, waits for them, and re-layouts, by_heads(): turn = lambda x: lax.dynamic_slice_in_dim(w_out, x * k_rows, k_rows, 0).T  3.6 us
    unnamed x18, local copies, waits for them, and re-layouts  2.67 us
  transfers between devices with their start and end apart: 29, of which 10 were waited for; matrix products, arithmetic and copies ran while one was open for 5% of the time, Pallas kernels for 21%

profile of v3, /device:TPU:0, one launch (start us, length us, event | category | flops | bytes accessed | tf_op | source)
XLA Modules:
  0.0 112.8 jit_solution(4006151076225957659)
XLA Ops:
  0.0 1.6 %constant_dynamic-slice_fusion = (f32[256,1,128]{2,1,0:T(1,128)S(1)}, f32[256,1,128]{2,1,0:T(1,128)S(1)}) fusion(f32[256,4,128]{2,1,0:T(4,128)} %param.6, s32[]{:T(128)S(6)} %select_n.139, f32[256,4,128]{2,1,0:T(4,128)} %param.5), kind=kLoop, calls=%fused_computation.16 | loop fusion | bytes 524292 | tf_op jit(solution)/shard_map/jit(dynamic_index_in_dim)/dynamic_slice | solution.py:284
  1.7 4.1 %collective-permute-start = (f32[2,256,128]{2,1,0:T(8,128)S(1)}, f32[2,256,128]{2,1,0:T(8,128)}, u32[]{:S(2)}, u32[]{:S(2)}) collective-permute-start(f32[2,256,128]{2,1,0:T(8,128)S(1)} %pad_maximum_fusion.refs_0_), channel_id=1, source_target_pairs={{0,2},{2,3},{3,1},{1,0},{4,6},{6,7},{7,5},{5,4},{8,10},{10,11},{11... | collective-permute-start | bytes 786440 | tf_op jit(solution)/shard_map/ppermute | solution.py:281
  5.8 1.3 %collective-permute-start.1 = (f32[2,256,128]{2,1,0:T(8,128)S(1)}, f32[2,256,128]{2,1,0:T(8,128)}, u32[]{:S(2)}, u32[]{:S(2)}) collective-permute-start(f32[2,256,128]{2,1,0:T(8,128)S(1)} %pad_maximum_fusion.refs_0_), channel_id=1, source_target_pairs={{0,3},{2,1},{3,0},{1,2},{4,7},{6,5},{7,4},{5,6},{8,11},{10,9},{11,... | collective-permute-start | bytes 786440 | tf_op jit(solution)/shard_map/ppermute | solution.py:281
  7.9 3.6 %dynamic-slice_bitcast_fusion = (f32[320,640]{1,0:T(8,128)}, f32[320,640]{1,0:T(8,128)}, f32[320,640]{1,0:T(8,128)}, f32[320,640]{1,0:T(8,128)}) fusion(f32[2560,320]{0,1:T(8,128)} %param.7, s32[]{:T(128)S(6)} %select_n.150, s32[]{:T(128)S(6)} %select_n.148, s32[]{:T(128)S(6)} %select_n.140, s32[]{:T(128)S(6)} %select_n.149), kind=kLoop, calls=%fused_computation | loop fusion | bytes 6553616 | tf_op jit(solution)/shard_map/transpose | solution.py:289
  11.5 1.5 %collective-permute-start.6 = (f32[320,640]{1,0:T(8,128)}, f32[320,640]{1,0:T(8,128)}, u32[]{:S(2)}, u32[]{:S(2)}) collective-permute-start(f32[320,640]{1,0:T(8,128)} %get-tuple-element.104), channel_id=1, source_target_pairs={{0,8},{8,0},{16,24},{24,16},{1,9},{9,1},{17,25},{25,17},{2,10},{10... | collective-permute-start | bytes 2457608 | tf_op jit(solution)/shard_map/ppermute | solution.py:290
  13.0 1.5 %collective-permute-start.7 = (f32[320,640]{1,0:T(8,128)}, f32[320,640]{1,0:T(8,128)}, u32[]{:S(2)}, u32[]{:S(2)}) collective-permute-start(f32[320,640]{1,0:T(8,128)} %get-tuple-element.106), channel_id=1, source_target_pairs={{0,16},{8,24},{16,0},{24,8},{1,17},{9,25},{17,1},{25,9},{2,18},{10... | collective-permute-start | bytes 2457608 | tf_op jit(solution)/shard_map/ppermute | solution.py:290
  15.9 4.2 %collective-permute-done.1.refs_2_ = f32[2,256,128]{2,1,0:T(8,128)} collective-permute-done((f32[2,256,128]{2,1,0:T(8,128)S(1)}, f32[2,256,128]{2,1,0:T(8,128)}, u32[]{:S(2)}, u32[]{:S(2)}) %collective-permute-start.1) | collective-permute-done | bytes 262176 | tf_op jit(solution)/shard_map/ppermute | solution.py:281
  20.0 10.0 %collective-permute-done.2.refs_3_ = f32[2,256,128]{2,1,0:T(8,128)} collective-permute-done((f32[2,256,128]{2,1,0:T(8,128)S(1)}, f32[2,256,128]{2,1,0:T(8,128)}, u32[]{:S(2)}, u32[]{:S(2)}) %collective-permute-start.2) | collective-permute-done | bytes 262176 | tf_op jit(solution)/shard_map/ppermute | solution.py:281
  30.1 3.0 %collective-permute-start.3 = (f32[2,256,128]{2,1,0:T(8,128)S(1)}, f32[2,256,128]{2,1,0:T(8,128)S(1)}, u32[]{:S(2)}, u32[]{:S(2)}) collective-permute-start(f32[2,256,128]{2,1,0:T(8,128)S(1)} %slice.32.refs_0_), channel_id=1, source_target_pairs={{0,2},{2,3},{3,1},{1,0},{4,6},{6,7},{7,5},{5,4},{8,10},{10,11},{11... | collective-permute-start | bytes 786440 | tf_op jit(solution)/shard_map/ppermute | solution.py:281
  33.1 2.7 %prepare_keys.1 = (bf16[384,1024]{1,0:T(8,128)(2,1)}, bf16[2048,256]{1,0:T(8,128)(2,1)}) custom-call(f32[2,256,128]{2,1,0:T(8,128)} %copy-done.5, f32[2,256,128]{2,1,0:T(8,128)} %collective-permute-done.refs_1_, f32[2,256,128]{2,1,0:T(8,128)} %collective-permute-done.1.refs_2_, f32[2,256,128]{2,1,0:T(8,128)} %collective-permute-done.2.refs_3_), custom_call_target="tpu_custom_call" | custom-call | flops 1 | bytes 1 | tf_op jit(solution)/shard_map/prepare_keys/pallas_call | solution.py:83
  35.8 3.7 %attend.2.refs_0_ = f32[256,640]{1,0:T(8,128)} custom-call(s32[4]{0:T(128)} %pad_add_fusion.1.meta_ref, f32[2,256,128]{2,1,0:T(8,128)} %copy-done.6, f32[3,256,128]{2,1,0:T(8,128)} %copy-done.4, bf16[384,1024]{1,0:T(8,128)(2,1)} %get-tuple-element.61.refs_2_, bf16[2048,256]{1,0:T(8,128)(2,1)} %get-tuple-element.62.refs_3_), custom_call_target="tpu_custom_call" | custom-call | flops 1 | bytes 1 | tf_op jit(solution)/shard_map/attend/pallas_call | solution.py:144
  39.5 7.3 %collective-permute-done.3.refs_0_ = f32[2,256,128]{2,1,0:T(8,128)S(1)} collective-permute-done((f32[2,256,128]{2,1,0:T(8,128)S(1)}, f32[2,256,128]{2,1,0:T(8,128)S(1)}, u32[]{:S(2)}, u32[]{:S(2)}) %collective-permute-start.3) | collective-permute-done | bytes 262176 | tf_op jit(solution)/shard_map/ppermute | solution.py:281
  48.2 1.3 %collective-permute-start.5 = (f32[256,640]{1,0:T(8,128)}, f32[256,640]{1,0:T(8,128)}, u32[]{:S(2)}, u32[]{:S(2)}) collective-permute-start(f32[256,640]{1,0:T(8,128)} %attend.2.refs_0_), channel_id=1, source_target_pairs={{0,1},{2,0},{3,2},{1,3},{4,5},{6,4},{7,6},{5,7},{8,9},{10,8},{11,1... | collective-permute-start | bytes 1966088 | tf_op jit(solution)/shard_map/ppermute | solution.py:281
  49.7 4.9 %attend.3.refs_1_ = f32[256,640]{1,0:T(8,128)} custom-call(s32[4]{0:T(128)} %pad_add_fusion.1.meta_ref, f32[2,256,128]{2,1,0:T(8,128)} %copy-done.8, f32[3,256,128]{2,1,0:T(8,128)} %copy-done.7, bf16[384,1024]{1,0:T(8,128)(2,1)} %get-tuple-element.61.refs_2_, bf16[2048,256]{1,0:T(8,128)(2,1)} %get-tuple-element.62.refs_3_), custom_call_target="tpu_custom_call" | custom-call | flops 1 | bytes 1 | tf_op jit(solution)/shard_map/attend/pallas_call | solution.py:144
  54.6 1.1 %copy-done.3 = f32[320,640]{1,0:T(8,128)S(1)} copy-done((f32[320,640]{1,0:T(8,128)S(1)}, f32[320,640]{1,0:T(8,128)}, u32[]{:S(2)}) %copy-start.3) | copy-done | bytes 819224
  55.8 2.2 %prepare_weights.1 = (bf16[2,640,640]{2,1,0:T(8,128)(2,1)S(1)}, bf16[2,640,640]{2,1,0:T(8,128)(2,1)S(1)}) custom-call(s32[8]{0:T(128)S(1)} %stack.88.meta_ref, f32[320,640]{1,0:T(8,128)S(1)} %copy-done.3, f32[320,640]{1,0:T(8,128)} %collective-permute-done.6.refs_1_, f32[320,640]{1,0:T(8,128)} %collective-permute-done.7.refs_2_, ...), custom_call_target="tpu_custom_call" | custom-call | flops 1 | bytes 1 | tf_op jit(solution)/shard_map/prepare_weights/pallas_call | solution.py:173
  58.0 2.0 %project.6 = (f32[128,640]{1,0:T(8,128)S(1)}, f32[128,640]{1,0:T(8,128)S(1)}, f32[128,640]{1,0:T(8,128)S(1)}, f32[128,640]{1,0:T(8,128)S(1)}) custom-call(f32[256,640]{1,0:T(8,128)S(1)} %copy-done.1, f32[256,640]{1,0:T(8,128)S(1)} %copy-done.2, bf16[2,640,640]{2,1,0:T(8,128)(2,1)S(1)} %get-tuple-element.72.refs_2_.refs_1_, ...), custom_call_target="tpu_custom_call" | custom-call | flops 1 | bytes 1 | tf_op jit(solution)/shard_map/project/pallas_call | solution.py:199
  61.0 1.9 %project.7.kept_ref = f32[512,640]{1,0:T(8,128)S(1)} custom-call(f32[256,640]{1,0:T(8,128)S(1)} %copy-done.1, f32[256,640]{1,0:T(8,128)S(1)} %copy-done.2, bf16[2,640,640]{2,1,0:T(8,128)(2,1)S(1)} %get-tuple-element.72.refs_2_.refs_1_, bf16[2,640,640]{2,1,0:T(8,128)(2,1)S(1)} %get-tuple-element.73.refs_3_.refs_2_), custom_call_target="tpu_custom_call" | custom-call | flops 1 | bytes 1 | tf_op jit(solution)/shard_map/project/pallas_call | solution.py:199
  63.0 1.1 %collective-permute-start.13 = (f32[256,640]{1,0:T(8,128)S(1)}, f32[256,640]{1,0:T(8,128)S(1)}, u32[]{:S(2)}, u32[]{:S(2)}) collective-permute-start(f32[256,640]{1,0:T(8,128)S(1)} %copy-done.2), channel_id=1, source_target_pairs={{0,2},{2,3},{3,1},{1,0},{4,6},{6,7},{7,5},{5,4},{8,10},{10,11},{11... | collective-permute-start | bytes 1966088 | tf_op jit(solution)/shard_map/ppermute | solution.py:281
  64.2 1.2 %collective-permute-done.5.refs_0_ = f32[256,640]{1,0:T(8,128)} collective-permute-done((f32[256,640]{1,0:T(8,128)}, f32[256,640]{1,0:T(8,128)}, u32[]{:S(2)}, u32[]{:S(2)}) %collective-permute-start.5) | collective-permute-done | bytes 655392 | tf_op jit(solution)/shard_map/ppermute | solution.py:281
  65.6 1.6 %collective-permute-start.14 = (f32[2,2,64,640]{3,2,1,0:T(8,128)S(1)}, f32[2,2,64,640]{3,2,1,0:T(8,128)S(1)}, u32[]{:S(2)}, u32[]{:S(2)}) collective-permute-start(f32[2,2,64,640]{3,2,1,0:T(8,128)S(1)} %get-tuple-element.87), channel_id=1, source_target_pairs={{0,8},{8,0},{16,24},{24,16},{1,9},{9,1},{17,25},{25,17},{2,10},{10... | collective-permute-start | bytes 1966088 | tf_op jit(solution)/shard_map/ppermute | solution.py:290
  67.1 2.2 %project.9 = (f32[96,640]{1,0:T(8,128)S(1)}, f32[80,640]{1,0:T(8,128)S(1)}, f32[80,640]{1,0:T(8,128)S(1)}) custom-call(f32[256,640]{1,0:T(8,128)} %collective-permute-done.5.refs_0_, bf16[2,640,640]{2,1,0:T(8,128)(2,1)S(1)} %get-tuple-element.72.refs_2_.refs_1_, bf16[2,640,640]{2,1,0:T(8,128)(2,1)S(1)} %get-tuple-element.73.refs_3_.refs_2_), custom_call_target="tpu_custom_call" | custom-call | flops 1 | bytes 1 | tf_op jit(solution)/shard_map/project/pallas_call | solution.py:199
  70.0 2.2 %project.8.kept_ref = f32[256,640]{1,0:T(8,128)S(1)} custom-call(f32[256,640]{1,0:T(8,128)} %collective-permute-done.5.refs_0_, bf16[2,640,640]{2,1,0:T(8,128)(2,1)S(1)} %get-tuple-element.72.refs_2_.refs_1_, bf16[2,640,640]{2,1,0:T(8,128)(2,1)S(1)} %get-tuple-element.73.refs_3_.refs_2_), custom_call_target="tpu_custom_call" | custom-call | flops 1 | bytes 1 | tf_op jit(solution)/shard_map/project/pallas_call | solution.py:199
  72.3 1.6 %collective-permute-start.18 = (f32[2,1,64,640]{3,2,1,0:T(8,128)S(1)}, f32[2,1,64,640]{3,2,1,0:T(8,128)S(1)}, u32[]{:S(2)}, u32[]{:S(2)}) collective-permute-start(f32[2,1,64,640]{3,2,1,0:T(8,128)S(1)} %get-tuple-element.92), channel_id=1, source_target_pairs={{0,16},{8,24},{16,0},{24,8},{1,17},{9,25},{17,1},{25,9},{2,18},{10... | collective-permute-start | bytes 983048 | tf_op jit(solution)/shard_map/ppermute | solution.py:290
  73.9 8.4 %collective-permute-done.13.refs_0_ = f32[256,640]{1,0:T(8,128)S(1)} collective-permute-done((f32[256,640]{1,0:T(8,128)S(1)}, f32[256,640]{1,0:T(8,128)S(1)}, u32[]{:S(2)}, u32[]{:S(2)}) %collective-permute-start.13) | collective-permute-done | bytes 655392 | tf_op jit(solution)/shard_map/ppermute | solution.py:281
  85.4 1.3 %collective-permute-start.19 = (f32[2,64,640]{2,1,0:T(8,128)S(1)}, f32[2,64,640]{2,1,0:T(8,128)S(1)}, u32[]{:S(2)}, u32[]{:S(2)}) collective-permute-start(f32[2,64,640]{2,1,0:T(8,128)S(1)} %slice_bitcast_fusion), channel_id=1, source_target_pairs={{0,16},{8,24},{16,0},{24,8},{1,17},{9,25},{17,1},{25,9},{2,18},{10... | collective-permute-start | bytes 983048 | tf_op jit(solution)/shard_map/ppermute | solution.py:290
  87.8 2.6 %collective-permute-done.27 = f32[1,64,640]{2,1,0:T(8,128)S(1)} collective-permute-done((f32[1,64,640]{2,1,0:T(8,128)S(1)}, f32[1,64,640]{2,1,0:T(8,128)S(1)}, u32[]{:S(2)}, u32[]{:S(2)}) %collective-permute-start.27) | collective-permute-done | bytes 163872 | tf_op jit(solution)/shard_map/ppermute | solution.py:290
  92.2 1.8 %collective-permute-start.25 = (f32[1,1,64,640]{3,2,1,0:T(8,128)S(1)}, f32[1,1,64,640]{3,2,1,0:T(8,128)S(1)}, u32[]{:S(2)}, u32[]{:S(2)}) collective-permute-start(f32[1,1,64,640]{3,2,1,0:T(8,128)S(1)} %get-tuple-element.100), channel_id=1, source_target_pairs={{0,24},{8,16},{16,8},{24,0},{1,25},{9,17},{17,9},{25,1},{2,26},{10... | collective-permute-start | bytes 491528 | tf_op jit(solution)/shard_map/ppermute | solution.py:290
  96.7 5.3 %collective-permute-start.20 = (f32[64,640]{1,0:T(8,128)S(1)}, f32[64,640]{1,0:T(8,128)S(1)}, u32[]{:S(2)}, u32[]{:S(2)}) collective-permute-start(f32[64,640]{1,0:T(8,128)S(1)} %get-tuple-element.107), channel_id=1, source_target_pairs={{0,1},{2,0},{3,2},{1,3},{4,5},{6,4},{7,6},{5,7},{8,9},{10,8},{11,1... | collective-permute-start | bytes 491528 | tf_op jit(solution)/shard_map/ppermute | solution.py:281
  102.7 4.0 %collective-permute-start.26 = (f32[64,640]{1,0:T(8,128)}, f32[64,640]{1,0:T(8,128)S(1)}, u32[]{:S(2)}, u32[]{:S(2)}) collective-permute-start(f32[64,640]{1,0:T(8,128)} %add_bitcast_fusion), channel_id=1, source_target_pairs={{0,3},{2,1},{3,0},{1,2},{4,7},{6,5},{7,4},{5,6},{8,11},{10,9},{11,... | collective-permute-start | bytes 491528 | tf_op jit(solution)/shard_map/ppermute | solution.py:281
  106.8 4.4 %collective-permute-done.26.refs_2_ = f32[64,640]{1,0:T(8,128)S(1)} collective-permute-done((f32[64,640]{1,0:T(8,128)}, f32[64,640]{1,0:T(8,128)S(1)}, u32[]{:S(2)}, u32[]{:S(2)}) %collective-permute-start.26) | collective-permute-done | bytes 163872 | tf_op jit(solution)/shard_map/ppermute | solution.py:281
  111.2 1.6 %assemble.1 = f32[64,2560]{1,0:T(8,128)} custom-call(s32[4]{0:T(128)S(1)} %pad_add_fusion.meta_ref, f32[64,640]{1,0:T(8,128)S(1)} %get-tuple-element.108.refs_0_, f32[64,640]{1,0:T(8,128)S(1)} %collective-permute-done.20.refs_1_, f32[64,640]{1,0:T(8,128)S(1)} %collective-permute-done.26.refs_2_, f32[64,640]{1,0:T(8,128)S(1)} %collective-permute-done.28.refs_3_), custom_call_target="tpu_custom_call" | custom-call | flops 1 | bytes 1 | tf_op jit(solution)/shard_map/assemble/pallas_call | solution.py:258
  (75 shorter events, 15.3 us)
Async XLA Ops:
  0.0 14.5 %copy-start = (f32[256,20,128]{2,0,1:T(8,128)S(1)}, f32[256,20,128]{2,0,1:T(8,128)}, u32[]{:S(2)}) copy-start(f32[256,20,128]{2,0,1:T(8,128)} %param.4) | copy-start | bytes 7864324
  1.7 13.0 %collective-permute-start = (f32[2,256,128]{2,1,0:T(8,128)S(1)}, f32[2,256,128]{2,1,0:T(8,128)}, u32[]{:S(2)}, u32[]{:S(2)}) collective-permute-start(f32[2,256,128]{2,1,0:T(8,128)S(1)} %pad_maximum_fusion.refs_0_), channel_id=1, source_target_pairs={{0,2},{2,3},{3,1},{1,0},{4,6},{6,7},{7,5},{5,4},{8,10},{10,11},{11... | collective-permute-start | bytes 786440 | tf_op jit(solution)/shard_map/ppermute | solution.py:281
  5.8 14.3 %collective-permute-start.1 = (f32[2,256,128]{2,1,0:T(8,128)S(1)}, f32[2,256,128]{2,1,0:T(8,128)}, u32[]{:S(2)}, u32[]{:S(2)}) collective-permute-start(f32[2,256,128]{2,1,0:T(8,128)S(1)} %pad_maximum_fusion.refs_0_), channel_id=1, source_target_pairs={{0,3},{2,1},{3,0},{1,2},{4,7},{6,5},{7,4},{5,6},{8,11},{10,9},{11,... | collective-permute-start | bytes 786440 | tf_op jit(solution)/shard_map/ppermute | solution.py:281
  7.1 23.0 %collective-permute-start.2 = (f32[2,256,128]{2,1,0:T(8,128)S(1)}, f32[2,256,128]{2,1,0:T(8,128)}, u32[]{:S(2)}, u32[]{:S(2)}) collective-permute-start(f32[2,256,128]{2,1,0:T(8,128)S(1)} %pad_maximum_fusion.refs_0_), channel_id=1, source_target_pairs={{0,1},{2,0},{3,2},{1,3},{4,5},{6,4},{7,6},{5,7},{8,9},{10,8},{11,1... | collective-permute-start | bytes 786440 | tf_op jit(solution)/shard_map/ppermute | solution.py:281
  11.5 38.1 %collective-permute-start.6 = (f32[320,640]{1,0:T(8,128)}, f32[320,640]{1,0:T(8,128)}, u32[]{:S(2)}, u32[]{:S(2)}) collective-permute-start(f32[320,640]{1,0:T(8,128)} %get-tuple-element.104), channel_id=1, source_target_pairs={{0,8},{8,0},{16,24},{24,16},{1,9},{9,1},{17,25},{25,17},{2,10},{10... | collective-permute-start | bytes 2457608 | tf_op jit(solution)/shard_map/ppermute | solution.py:290
  13.0 36.7 %collective-permute-start.7 = (f32[320,640]{1,0:T(8,128)}, f32[320,640]{1,0:T(8,128)}, u32[]{:S(2)}, u32[]{:S(2)}) collective-permute-start(f32[320,640]{1,0:T(8,128)} %get-tuple-element.106), channel_id=1, source_target_pairs={{0,16},{8,24},{16,0},{24,8},{1,17},{9,25},{17,1},{25,9},{2,18},{10... | collective-permute-start | bytes 2457608 | tf_op jit(solution)/shard_map/ppermute | solution.py:290
  14.6 21.2 %copy-start.6 = (f32[2,256,128]{2,1,0:T(8,128)}, f32[2,256,128]{2,1,0:T(8,128)S(1)}, u32[]{:S(2)}) copy-start(f32[2,256,128]{2,1,0:T(8,128)S(1)} %slice.32.refs_0_) | copy-start | bytes 786436
  14.6 21.2 %copy-start.4 = (f32[3,256,128]{2,1,0:T(8,128)}, f32[3,256,128]{2,1,0:T(8,128)S(1)}, u32[]{:S(2)}) copy-start(f32[3,256,128]{2,1,0:T(8,128)S(1)} %slice.33.refs_1_) | copy-start | bytes 1179652
  14.7 35.0 %collective-permute-start.8 = (f32[320,640]{1,0:T(8,128)}, f32[320,640]{1,0:T(8,128)}, u32[]{:S(2)}, u32[]{:S(2)}) collective-permute-start(f32[320,640]{1,0:T(8,128)} %get-tuple-element.103), channel_id=1, source_target_pairs={{0,24},{8,16},{16,8},{24,0},{1,25},{9,17},{17,9},{25,1},{2,26},{10... | collective-permute-start | bytes 2457608 | tf_op jit(solution)/shard_map/ppermute | solution.py:290
  30.1 16.7 %collective-permute-start.4 = (f32[3,256,128]{2,1,0:T(8,128)S(1)}, f32[3,256,128]{2,1,0:T(8,128)S(1)}, u32[]{:S(2)}, u32[]{:S(2)}) collective-permute-start(f32[3,256,128]{2,1,0:T(8,128)S(1)} %slice.33.refs_1_), channel_id=1, source_target_pairs={{0,2},{2,3},{3,1},{1,0},{4,6},{6,7},{7,5},{5,4},{8,10},{10,11},{11... | collective-permute-start | bytes 1179656 | tf_op jit(solution)/shard_map/ppermute | solution.py:281
  30.1 16.7 %collective-permute-start.3 = (f32[2,256,128]{2,1,0:T(8,128)S(1)}, f32[2,256,128]{2,1,0:T(8,128)S(1)}, u32[]{:S(2)}, u32[]{:S(2)}) collective-permute-start(f32[2,256,128]{2,1,0:T(8,128)S(1)} %slice.32.refs_0_), channel_id=1, source_target_pairs={{0,2},{2,3},{3,1},{1,0},{4,6},{6,7},{7,5},{5,4},{8,10},{10,11},{11... | collective-permute-start | bytes 786440 | tf_op jit(solution)/shard_map/ppermute | solution.py:281
  48.2 17.1 %collective-permute-start.5 = (f32[256,640]{1,0:T(8,128)}, f32[256,640]{1,0:T(8,128)}, u32[]{:S(2)}, u32[]{:S(2)}) collective-permute-start(f32[256,640]{1,0:T(8,128)} %attend.2.refs_0_), channel_id=1, source_target_pairs={{0,1},{2,0},{3,2},{1,3},{4,5},{6,4},{7,6},{5,7},{8,9},{10,8},{11,1... | collective-permute-start | bytes 1966088 | tf_op jit(solution)/shard_map/ppermute | solution.py:281
  60.0 3.0 %collective-permute-start.9 = (f32[128,640]{1,0:T(8,128)S(1)}, f32[128,640]{1,0:T(8,128)S(1)}, u32[]{:S(2)}, u32[]{:S(2)}) collective-permute-start(f32[128,640]{1,0:T(8,128)S(1)} %get-tuple-element.74), channel_id=1, source_target_pairs={{0,4},{4,0},{1,5},{5,1},{2,6},{6,2},{3,7},{7,3},{8,12},{12,8},{9,1... | collective-permute-start | bytes 983048 | tf_op jit(solution)/shard_map/ppermute | solution.py:282
  60.0 4.1 %collective-permute-start.10 = (f32[128,640]{1,0:T(8,128)S(1)}, f32[128,640]{1,0:T(8,128)S(1)}, u32[]{:S(2)}, u32[]{:S(2)}) collective-permute-start(f32[128,640]{1,0:T(8,128)S(1)} %get-tuple-element.75), channel_id=1, source_target_pairs={{0,4},{4,0},{1,5},{5,1},{2,6},{6,2},{3,7},{7,3},{8,12},{12,8},{9,1... | collective-permute-start | bytes 983048 | tf_op jit(solution)/shard_map/ppermute | solution.py:282
  60.5 3.6 %collective-permute-start.11 = (f32[128,640]{1,0:T(8,128)S(1)}, f32[128,640]{1,0:T(8,128)S(1)}, u32[]{:S(2)}, u32[]{:S(2)}) collective-permute-start(f32[128,640]{1,0:T(8,128)S(1)} %get-tuple-element.76), channel_id=1, source_target_pairs={{0,4},{4,0},{1,5},{5,1},{2,6},{6,2},{3,7},{7,3},{8,12},{12,8},{9,1... | collective-permute-start | bytes 983048 | tf_op jit(solution)/shard_map/ppermute | solution.py:282
  60.6 3.5 %collective-permute-start.12 = (f32[128,640]{1,0:T(8,128)S(1)}, f32[128,640]{1,0:T(8,128)S(1)}, u32[]{:S(2)}, u32[]{:S(2)}) collective-permute-start(f32[128,640]{1,0:T(8,128)S(1)} %get-tuple-element.77), channel_id=1, source_target_pairs={{0,4},{4,0},{1,5},{5,1},{2,6},{6,2},{3,7},{7,3},{8,12},{12,8},{9,1... | collective-permute-start | bytes 983048 | tf_op jit(solution)/shard_map/ppermute | solution.py:282
  63.0 19.3 %collective-permute-start.13 = (f32[256,640]{1,0:T(8,128)S(1)}, f32[256,640]{1,0:T(8,128)S(1)}, u32[]{:S(2)}, u32[]{:S(2)}) collective-permute-start(f32[256,640]{1,0:T(8,128)S(1)} %copy-done.2), channel_id=1, source_target_pairs={{0,2},{2,3},{3,1},{1,0},{4,6},{6,7},{7,5},{5,4},{8,10},{10,11},{11... | collective-permute-start | bytes 1966088 | tf_op jit(solution)/shard_map/ppermute | solution.py:281
  65.6 16.9 %collective-permute-start.14 = (f32[2,2,64,640]{3,2,1,0:T(8,128)S(1)}, f32[2,2,64,640]{3,2,1,0:T(8,128)S(1)}, u32[]{:S(2)}, u32[]{:S(2)}) collective-permute-start(f32[2,2,64,640]{3,2,1,0:T(8,128)S(1)} %get-tuple-element.87), channel_id=1, source_target_pairs={{0,8},{8,0},{16,24},{24,16},{1,9},{9,1},{17,25},{25,17},{2,10},{10... | collective-permute-start | bytes 1966088 | tf_op jit(solution)/shard_map/ppermute | solution.py:290
  69.3 2.9 %collective-permute-start.15 = (f32[96,640]{1,0:T(8,128)S(1)}, f32[96,640]{1,0:T(8,128)S(1)}, u32[]{:S(2)}, u32[]{:S(2)}) collective-permute-start(f32[96,640]{1,0:T(8,128)S(1)} %get-tuple-element.89), channel_id=1, source_target_pairs={{0,4},{4,0},{1,5},{5,1},{2,6},{6,2},{3,7},{7,3},{8,12},{12,8},{9,1... | collective-permute-start | bytes 737288 | tf_op jit(solution)/shard_map/ppermute | solution.py:282
  69.4 2.8 %collective-permute-start.16 = (f32[80,640]{1,0:T(8,128)S(1)}, f32[80,640]{1,0:T(8,128)S(1)}, u32[]{:S(2)}, u32[]{:S(2)}) collective-permute-start(f32[80,640]{1,0:T(8,128)S(1)} %get-tuple-element.90), channel_id=1, source_target_pairs={{0,4},{4,0},{1,5},{5,1},{2,6},{6,2},{3,7},{7,3},{8,12},{12,8},{9,1... | collective-permute-start | bytes 614408 | tf_op jit(solution)/shard_map/ppermute | solution.py:282
  69.9 2.3 %collective-permute-start.17 = (f32[80,640]{1,0:T(8,128)S(1)}, f32[80,640]{1,0:T(8,128)S(1)}, u32[]{:S(2)}, u32[]{:S(2)}) collective-permute-start(f32[80,640]{1,0:T(8,128)S(1)} %get-tuple-element.91), channel_id=1, source_target_pairs={{0,4},{4,0},{1,5},{5,1},{2,6},{6,2},{3,7},{7,3},{8,12},{12,8},{9,1... | collective-permute-start | bytes 614408 | tf_op jit(solution)/shard_map/ppermute | solution.py:282
  72.3 10.1 %collective-permute-start.18 = (f32[2,1,64,640]{3,2,1,0:T(8,128)S(1)}, f32[2,1,64,640]{3,2,1,0:T(8,128)S(1)}, u32[]{:S(2)}, u32[]{:S(2)}) collective-permute-start(f32[2,1,64,640]{3,2,1,0:T(8,128)S(1)} %get-tuple-element.92), channel_id=1, source_target_pairs={{0,16},{8,24},{16,0},{24,8},{1,17},{9,25},{17,1},{25,9},{2,18},{10... | collective-permute-start | bytes 983048 | tf_op jit(solution)/shard_map/ppermute | solution.py:290
  83.5 8.5 %collective-permute-start.21 = (f32[128,640]{1,0:T(8,128)S(1)}, f32[128,640]{1,0:T(8,128)S(1)}, u32[]{:S(2)}, u32[]{:S(2)}) collective-permute-start(f32[128,640]{1,0:T(8,128)S(1)} %get-tuple-element.95), channel_id=1, source_target_pairs={{0,4},{4,0},{1,5},{5,1},{2,6},{6,2},{3,7},{7,3},{8,12},{12,8},{9,1... | collective-permute-start | bytes 983048 | tf_op jit(solution)/shard_map/ppermute | solution.py:282
  83.6 8.4 %collective-permute-start.22 = (f32[128,640]{1,0:T(8,128)S(1)}, f32[128,640]{1,0:T(8,128)S(1)}, u32[]{:S(2)}, u32[]{:S(2)}) collective-permute-start(f32[128,640]{1,0:T(8,128)S(1)} %get-tuple-element.96), channel_id=1, source_target_pairs={{0,4},{4,0},{1,5},{5,1},{2,6},{6,2},{3,7},{7,3},{8,12},{12,8},{9,1... | collective-permute-start | bytes 983048 | tf_op jit(solution)/shard_map/ppermute | solution.py:282
  84.2 6.2 %collective-permute-start.27 = (f32[1,64,640]{2,1,0:T(8,128)S(1)}, f32[1,64,640]{2,1,0:T(8,128)S(1)}, u32[]{:S(2)}, u32[]{:S(2)}) collective-permute-start(f32[1,64,640]{2,1,0:T(8,128)S(1)} %slice_bitcast_fusion.2), channel_id=1, source_target_pairs={{0,8},{8,0},{16,24},{24,16},{1,9},{9,1},{17,25},{25,17},{2,10},{10... | collective-permute-start | bytes 491528 | tf_op jit(solution)/shard_map/ppermute | solution.py:290
  85.4 11.3 %collective-permute-start.19 = (f32[2,64,640]{2,1,0:T(8,128)S(1)}, f32[2,64,640]{2,1,0:T(8,128)S(1)}, u32[]{:S(2)}, u32[]{:S(2)}) collective-permute-start(f32[2,64,640]{2,1,0:T(8,128)S(1)} %slice_bitcast_fusion), channel_id=1, source_target_pairs={{0,16},{8,24},{16,0},{24,8},{1,17},{9,25},{17,1},{25,9},{2,18},{10... | collective-permute-start | bytes 983048 | tf_op jit(solution)/shard_map/ppermute | solution.py:290
  91.1 15.7 %collective-permute-start.28 = (f32[64,640]{1,0:T(8,128)}, f32[64,640]{1,0:T(8,128)S(1)}, u32[]{:S(2)}, u32[]{:S(2)}) collective-permute-start(f32[64,640]{1,0:T(8,128)} %fusion.2), channel_id=1, source_target_pairs={{0,2},{2,3},{3,1},{1,0},{4,6},{6,7},{7,5},{5,4},{8,10},{10,11},{11... | collective-permute-start | bytes 491528 | tf_op jit(solution)/shard_map/ppermute | solution.py:281
  92.2 9.8 %collective-permute-start.25 = (f32[1,1,64,640]{3,2,1,0:T(8,128)S(1)}, f32[1,1,64,640]{3,2,1,0:T(8,128)S(1)}, u32[]{:S(2)}, u32[]{:S(2)}) collective-permute-start(f32[1,1,64,640]{3,2,1,0:T(8,128)S(1)} %get-tuple-element.100), channel_id=1, source_target_pairs={{0,24},{8,16},{16,8},{24,0},{1,25},{9,17},{17,9},{25,1},{2,26},{10... | collective-permute-start | bytes 491528 | tf_op jit(solution)/shard_map/ppermute | solution.py:290
  94.0 8.0 %collective-permute-start.24 = (f32[1,1,64,640]{3,2,1,0:T(8,128)S(1)}, f32[1,1,64,640]{3,2,1,0:T(8,128)S(1)}, u32[]{:S(2)}, u32[]{:S(2)}) collective-permute-start(f32[1,1,64,640]{3,2,1,0:T(8,128)S(1)} %get-tuple-element.99), channel_id=1, source_target_pairs={{0,16},{8,24},{16,0},{24,8},{1,17},{9,25},{17,1},{25,9},{2,18},{10... | collective-permute-start | bytes 491528 | tf_op jit(solution)/shard_map/ppermute | solution.py:290
  94.8 7.2 %collective-permute-start.23 = (f32[1,1,64,640]{3,2,1,0:T(8,128)S(1)}, f32[1,1,64,640]{3,2,1,0:T(8,128)S(1)}, u32[]{:S(2)}, u32[]{:S(2)}) collective-permute-start(f32[1,1,64,640]{3,2,1,0:T(8,128)S(1)} %get-tuple-element.98), channel_id=1, source_target_pairs={{0,8},{8,0},{16,24},{24,16},{1,9},{9,1},{17,25},{25,17},{2,10},{10... | collective-permute-start | bytes 491528 | tf_op jit(solution)/shard_map/ppermute | solution.py:290
  96.7 10.1 %collective-permute-start.20 = (f32[64,640]{1,0:T(8,128)S(1)}, f32[64,640]{1,0:T(8,128)S(1)}, u32[]{:S(2)}, u32[]{:S(2)}) collective-permute-start(f32[64,640]{1,0:T(8,128)S(1)} %get-tuple-element.107), channel_id=1, source_target_pairs={{0,1},{2,0},{3,2},{1,3},{4,5},{6,4},{7,6},{5,7},{8,9},{10,8},{11,1... | collective-permute-start | bytes 491528 | tf_op jit(solution)/shard_map/ppermute | solution.py:281
  102.7 8.5 %collective-permute-start.26 = (f32[64,640]{1,0:T(8,128)}, f32[64,640]{1,0:T(8,128)S(1)}, u32[]{:S(2)}, u32[]{:S(2)}) collective-permute-start(f32[64,640]{1,0:T(8,128)} %add_bitcast_fusion), channel_id=1, source_target_pairs={{0,3},{2,1},{3,0},{1,2},{4,7},{6,5},{7,4},{5,6},{8,11},{10,9},{11,... | collective-permute-start | bytes 491528 | tf_op jit(solution)/shard_map/ppermute | solution.py:281
  (6 other events, 23.0 us)

commit v4 on v3

--- a/solution.py
+++ b/solution.py
@@ -10,7 +10,7 @@
 F32 = jnp.float32
 BF16 = jnp.bfloat16
 VMEM_LIMIT = 20 * 1024 * 1024
-WHOLE = 60 * 1024 * 1024
+WHOLE = 63 * 1024 * 1024
 NT = (((1,), (1,)), ((), ()))
 
 
@@ -162,10 +162,14 @@
     columns, k = pieces[0].shape
 
     def kernel(meta_ref, *refs):
-        high, low = refs[n:]
-        for i in range(n):
+        high, low, held, sem = refs[n:]
+        copy = pltpu.make_async_copy(refs[0], held, sem)
+        copy.start()
+        for i in list(range(1, n)) + [0]:
+            if i == 0:
+                copy.wait()
             at = pl.ds(pl.multiple_of(meta_ref[2 * i + 1] * columns, 16), columns)
-            w_high, w_low = split(refs[i][...])
+            w_high, w_low = split(refs[i][...] if i else held[...])
             high[meta_ref[2 * i], at] = w_high
             low[meta_ref[2 * i], at] = w_low
 
@@ -173,8 +177,9 @@
     return pl.pallas_call(
         kernel,
         out_shape=(shape, shape),
-        in_specs=[smem()] + vmem(n),
+        in_specs=[smem(), pl.BlockSpec(memory_space=pltpu.MemorySpace.HBM)] + vmem(n - 1),
         out_specs=tuple(vmem(2)),
+        scratch_shapes=[pltpu.VMEM((columns, k), F32), pltpu.SemaphoreType.DMA],
         compiler_params=params(),
         cost_estimate=brief(),
         name="prepare_weights",
@@ -209,9 +214,10 @@
     )(*blocks, high, low)
 
 
-def fold(meta, kept, got, blocks, order):
+def fold(meta, kept, got, blocks, parts, orders):
     rows = kept.shape[0] // blocks
-    cut = rows // sum(len(group) for group in order)
+    cut = rows // parts
+    half = cut // 2
     columns = kept.shape[1]
     n = len(got)
 
@@ -222,18 +228,20 @@
             at = pl.ds(start, ref.shape[0])
             total[at] = kept_ref[at] + ref[...]
             start += ref.shape[0]
-        for out, group in zip(outs, order):
+        for out, (side, group) in zip(outs, orders):
             for i, e in enumerate(group):
                 for b in range(blocks):
-                    out[i, b] = total[pl.ds(pl.multiple_of(b * rows + (meta_ref[0] ^ e) * cut, 8), cut)]
+                    start = b * rows + (meta_ref[0] ^ e) * cut + (side or 0) * half
+                    out[i, b] = total[pl.ds(pl.multiple_of(start, 8), out.shape[2])]
 
     return pl.pallas_call(
         kernel,
         out_shape=tuple(
-            jax.ShapeDtypeStruct((len(group), blocks, cut, columns), F32) for group in order
+            jax.ShapeDtypeStruct((len(group), blocks, cut if side is None else half, columns), F32)
+            for side, group in orders
         ),
         in_specs=[smem()] + vmem(1 + n),
-        out_specs=tuple(vmem(len(order))),
+        out_specs=tuple(vmem(len(orders))),
         scratch_shapes=[pltpu.VMEM((blocks * rows, columns), F32)],
         compiler_params=params(),
         cost_estimate=brief(),
@@ -308,29 +316,38 @@
     high, low = prepare_weights(ints(*places), [mine] + pieces)
 
     exchange = lambda xs: [swap(x) for x in xs]
-    single = tuple((e,) for e in range(parts))
     both = [owns[0], owns[1]]
     given = exchange(project(both, high, low, 1, 4))
     (kept,) = project(both, high, low, 0, 1)
     owns[3], *given = after(owns[3], *given)
-    keep_a, send_a = fold(place, kept, given, 2, ((0, 2), (1, 3)))
-    owns[3], keep_a, send_a = after(owns[3], keep_a, send_a)
-    got_a = cross(send_a, 1)
+    orders = ((0, (0, 2)), (1, (0, 1)), (0, (1, 3)), (1, (2, 3)))
+    add = lambda xs, ys: [x + y for x, y in zip(xs, ys)]
+    first = lambda sends: [cross(sends[0], 1), cross(sends[1], 2)]
+    second = lambda xs: [cross(xs[0][1], 2), cross(xs[1][1], 1)]
+    join = lambda xs, ys: jnp.concatenate([x[0] + y for x, y in zip(xs, ys)], axis=1)
+    *keep_a, up, down = fold(place, kept, given, 2, parts, orders)
+    owns[3], up, down, *keep_a = after(owns[3], up, down, *keep_a)
+    got_a = first([up, down])
     given = exchange(project([owns[3]], high, low, 1, 3))
     (kept,) = project([owns[3]], high, low, 0, 1)
-    keep_b, send_b = fold(place, kept, given, 1, ((0, 1), (2, 3)))
-    got_b = cross(send_b, 2)
-    owns[2], got_a, got_b = after(owns[2], got_a, got_b)
+    kept, *got_a = after(kept, *got_a)
+    keep_a = add(keep_a, got_a)
+    *keep_b, up, down = fold(place, kept, given, 1, parts, orders)
+    got_b = first([up, down])
+    owns[2], *got_b = after(owns[2], *got_b)
+    keep_b = add(keep_b, got_b)
     given = exchange(project([owns[2]], high, low, 1, 2))
     (kept,) = project([owns[2]], high, low, 0, 1)
-    keep_a, keep_b = keep_a + got_a, keep_b + got_b
-    keep_c, *send_c = fold(place, kept, given, 1, single)
-    got_a, got_b = cross(keep_a[1], 2), cross(keep_b[1], 1)
-    total_a, total_b = keep_a[0] + got_a, keep_b[0] + got_b
-    total = keep_c
-    for e, x in enumerate(send_c):
-        total = total + cross(x, e + 1)
-    results = [total_a[0], ring(total_a[1], -1), ring(total[0, 0], -2), ring(total_b[0], -3)]
+    *keep_c, up, down = fold(place, kept, given, 1, parts, orders)
+    got_a = second(keep_a)
+    got_b = second(keep_b)
+    *got, _, _ = after(*got_a, *got_b, up, down)
+    got_a, got_b = got[: len(got_a)], got[len(got_a) :]
+    total_a = join(keep_a, got_a)
+    total_b = join(keep_b, got_b)
+    keep_c = add(keep_c, first([up, down]))
+    total = join(keep_c, second(keep_c))
+    results = [total_a[0], ring(total_a[1], -1), ring(total[0], -2), ring(total_b[0], -3)]
     return assemble(ints(*sender), [results[j] for j in range(planes)], half)
 
 

time: 113 us -> 110 us (0.973)
  waiting for transfers between devices: 39.3 us -> 37.5 us
  other arithmetic: 2.23 us -> 1.01 us
    ppermute x10, waiting for transfers between devices: 35.5 us -> 30.7 us  [by_heads(): ring = lambda x, step: lax.ppermute(x, 'seq', ring_perm(planes, step))]
    ppermute x10, starting transfers between devices: 21.9 us -> 17.4 us  [by_heads(): ring = lambda x, step: lax.ppermute(x, 'seq', ring_perm(planes, step))]
    ppermute x10 -> x15, starting transfers between devices: 12.7 us -> 17.1 us  [by_heads(): lax.ppermute(x, 'feature', [(i, i ^ e) for i in range(parts)])]
    ppermute x10 -> x15, waiting for transfers between devices: 3.87 us -> 6.69 us  [by_heads(): lax.ppermute(x, 'feature', [(i, i ^ e) for i in range(parts)])]
    unnamed x18 -> x20, local copies, waits for them, and re-layouts: 2.67 us -> 1.86 us
  transfers between devices with their start and end apart: 29 -> 34, of which waited for: 10 -> 12; matrix products, arithmetic and copies ran while one was open for 5% -> 5% of each run, Pallas kernels for 21% -> 22%
where the time goes in v4:
time: 110 us
  waiting for transfers between devices  37.5 us (34%)
  starting transfers between devices  36.8 us (33%)
  Pallas kernels  25.9 us (24%)
  local copies, waits for them, and re-layouts  8.24 us (7%)
    ppermute x10, waiting for transfers between devices, by_heads(): ring = lambda x, step: lax.ppermute(x, 'seq', ring_perm(planes, step))  30.7 us
    ppermute x10, starting transfers between devices, by_heads(): ring = lambda x, step: lax.ppermute(x, 'seq', ring_perm(planes, step))  17.4 us
    ppermute x15, starting transfers between devices, by_heads(): lax.ppermute(x, 'feature', [(i, i ^ e) for i in range(parts)])  17.1 us
    pallas_call x6, Pallas kernels, project(): pl.pallas_call(kernel, out_shape=tuple((jax.ShapeDtypeStruct((b - a, colu...  10.4 us
    pallas_call x2, Pallas kernels, attend(): pl.pallas_call(kernel, out_shape=jax.ShapeDtypeStruct((rows, group * d),...  8.53 us
    ppermute x15, waiting for transfers between devices, by_heads(): lax.ppermute(x, 'feature', [(i, i ^ e) for i in range(parts)])  6.69 us
    transpose x1, local copies, waits for them, and re-layouts, by_heads(): turn = lambda x: lax.dynamic_slice_in_dim(w_out, x * k_rows, k_rows, 0).T  3.59 us
    pallas_call x1, Pallas kernels, prepare_keys(): pl.pallas_call(kernel, out_shape=(jax.ShapeDtypeStruct((3 * d, n * rows),...  2.66 us
  transfers between devices with their start and end apart: 34, of which 12 were waited for; matrix products, arithmetic and copies ran while one was open for 5% of the time, Pallas kernels for 22%

profile of v4, /device:TPU:0, one launch (start us, length us, event | category | flops | bytes accessed | tf_op | source)
XLA Modules:
  0.0 109.9 jit_solution(16010372955954679371)
XLA Ops:
  0.0 1.5 %constant_dynamic-slice_fusion = (f32[256,1,128]{2,1,0:T(1,128)S(1)}, f32[256,1,128]{2,1,0:T(1,128)S(1)}) fusion(f32[256,4,128]{2,1,0:T(4,128)} %param.6, s32[]{:T(128)S(6)} %select_n.139, f32[256,4,128]{2,1,0:T(4,128)} %param.5), kind=kLoop, calls=%fused_computation.32 | loop fusion | bytes 524292 | tf_op jit(solution)/shard_map/jit(dynamic_index_in_dim)/dynamic_slice | solution.py:292
  1.5 4.1 %collective-permute-start = (f32[2,256,128]{2,1,0:T(8,128)S(1)}, f32[2,256,128]{2,1,0:T(8,128)S(1)}, u32[]{:S(2)}, u32[]{:S(2)}) collective-permute-start(f32[2,256,128]{2,1,0:T(8,128)S(1)} %pad_maximum_fusion.refs_0_), channel_id=1, source_target_pairs={{0,2},{2,3},{3,1},{1,0},{4,6},{6,7},{7,5},{5,4},{8,10},{10,11},{11... | collective-permute-start | bytes 786440 | tf_op jit(solution)/shard_map/ppermute | solution.py:289
  5.6 1.3 %collective-permute-start.1 = (f32[2,256,128]{2,1,0:T(8,128)S(1)}, f32[2,256,128]{2,1,0:T(8,128)S(1)}, u32[]{:S(2)}, u32[]{:S(2)}) collective-permute-start(f32[2,256,128]{2,1,0:T(8,128)S(1)} %pad_maximum_fusion.refs_0_), channel_id=1, source_target_pairs={{0,3},{2,1},{3,0},{1,2},{4,7},{6,5},{7,4},{5,6},{8,11},{10,9},{11,... | collective-permute-start | bytes 786440 | tf_op jit(solution)/shard_map/ppermute | solution.py:289
  7.7 3.6 %dynamic-slice_bitcast_fusion = (f32[320,640]{1,0:T(8,128)}, f32[320,640]{1,0:T(8,128)}, f32[320,640]{1,0:T(8,128)}, f32[320,640]{1,0:T(8,128)}) fusion(f32[2560,320]{0,1:T(8,128)} %param.7, s32[]{:T(128)S(6)} %select_n.150, s32[]{:T(128)S(6)} %select_n.148, s32[]{:T(128)S(6)} %select_n.140, s32[]{:T(128)S(6)} %select_n.149), kind=kLoop, calls=%fused_computation | loop fusion | bytes 6553616 | tf_op jit(solution)/shard_map/transpose | solution.py:297
  11.3 1.5 %collective-permute-start.6 = (f32[320,640]{1,0:T(8,128)}, f32[320,640]{1,0:T(8,128)}, u32[]{:S(2)}, u32[]{:S(2)}) collective-permute-start(f32[320,640]{1,0:T(8,128)} %get-tuple-element.130), channel_id=1, source_target_pairs={{0,8},{8,0},{16,24},{24,16},{1,9},{9,1},{17,25},{25,17},{2,10},{10... | collective-permute-start | bytes 2457608 | tf_op jit(solution)/shard_map/ppermute | solution.py:298
  12.8 1.5 %collective-permute-start.7 = (f32[320,640]{1,0:T(8,128)}, f32[320,640]{1,0:T(8,128)}, u32[]{:S(2)}, u32[]{:S(2)}) collective-permute-start(f32[320,640]{1,0:T(8,128)} %get-tuple-element.132), channel_id=1, source_target_pairs={{0,16},{8,24},{16,0},{24,8},{1,17},{9,25},{17,1},{25,9},{2,18},{10... | collective-permute-start | bytes 2457608 | tf_op jit(solution)/shard_map/ppermute | solution.py:298
  16.8 3.0 %collective-permute-done.1.refs_2_ = f32[2,256,128]{2,1,0:T(8,128)S(1)} collective-permute-done((f32[2,256,128]{2,1,0:T(8,128)S(1)}, f32[2,256,128]{2,1,0:T(8,128)S(1)}, u32[]{:S(2)}, u32[]{:S(2)}) %collective-permute-start.1) | collective-permute-done | bytes 262176 | tf_op jit(solution)/shard_map/ppermute | solution.py:289
  19.8 10.0 %collective-permute-done.2.refs_3_ = f32[2,256,128]{2,1,0:T(8,128)S(1)} collective-permute-done((f32[2,256,128]{2,1,0:T(8,128)S(1)}, f32[2,256,128]{2,1,0:T(8,128)S(1)}, u32[]{:S(2)}, u32[]{:S(2)}) %collective-permute-start.2) | collective-permute-done | bytes 262176 | tf_op jit(solution)/shard_map/ppermute | solution.py:289
  30.5 2.3 %collective-permute-start.3 = (f32[2,256,128]{2,1,0:T(8,128)S(1)}, f32[2,256,128]{2,1,0:T(8,128)S(1)}, u32[]{:S(2)}, u32[]{:S(2)}) collective-permute-start(f32[2,256,128]{2,1,0:T(8,128)S(1)} %slice.64.refs_0_), channel_id=1, source_target_pairs={{0,2},{2,3},{3,1},{1,0},{4,6},{6,7},{7,5},{5,4},{8,10},{10,11},{11... | collective-permute-start | bytes 786440 | tf_op jit(solution)/shard_map/ppermute | solution.py:289
  32.9 2.7 %prepare_keys.1 = (bf16[384,1024]{1,0:T(8,128)(2,1)}, bf16[2048,256]{1,0:T(8,128)(2,1)}) custom-call(f32[2,256,128]{2,1,0:T(8,128)} %copy-done.4, f32[2,256,128]{2,1,0:T(8,128)} %copy-done.6, f32[2,256,128]{2,1,0:T(8,128)} %copy-done.7, f32[2,256,128]{2,1,0:T(8,128)} %copy-done.8), custom_call_target="tpu_custom_call" | custom-call | flops 1 | bytes 1 | tf_op jit(solution)/shard_map/prepare_keys/pallas_call | solution.py:83
  35.6 3.7 %attend.2.refs_0_ = f32[256,640]{1,0:T(8,128)} custom-call(s32[4]{0:T(128)} %pad_add_fusion.1.meta_ref, f32[2,256,128]{2,1,0:T(8,128)} %copy-done.5, f32[3,256,128]{2,1,0:T(8,128)} %copy-done.3, bf16[384,1024]{1,0:T(8,128)(2,1)} %get-tuple-element.74.refs_2_, bf16[2048,256]{1,0:T(8,128)(2,1)} %get-tuple-element.75.refs_3_), custom_call_target="tpu_custom_call" | custom-call | flops 1 | bytes 1 | tf_op jit(solution)/shard_map/attend/pallas_call | solution.py:144
  39.2 7.3 %collective-permute-done.3.refs_0_ = f32[2,256,128]{2,1,0:T(8,128)S(1)} collective-permute-done((f32[2,256,128]{2,1,0:T(8,128)S(1)}, f32[2,256,128]{2,1,0:T(8,128)S(1)}, u32[]{:S(2)}, u32[]{:S(2)}) %collective-permute-start.3) | collective-permute-done | bytes 262176 | tf_op jit(solution)/shard_map/ppermute | solution.py:289
  46.5 1.3 %collective-permute-start.5 = (f32[256,640]{1,0:T(8,128)}, f32[256,640]{1,0:T(8,128)}, u32[]{:S(2)}, u32[]{:S(2)}) collective-permute-start(f32[256,640]{1,0:T(8,128)} %attend.2.refs_0_), channel_id=1, source_target_pairs={{0,1},{2,0},{3,2},{1,3},{4,5},{6,4},{7,6},{5,7},{8,9},{10,8},{11,1... | collective-permute-start | bytes 1966088 | tf_op jit(solution)/shard_map/ppermute | solution.py:289
  47.9 1.7 %collective-permute-done.7.refs_2_ = f32[320,640]{1,0:T(8,128)} collective-permute-done((f32[320,640]{1,0:T(8,128)}, f32[320,640]{1,0:T(8,128)}, u32[]{:S(2)}, u32[]{:S(2)}) %collective-permute-start.7) | collective-permute-done | bytes 819232 | tf_op jit(solution)/shard_map/ppermute | solution.py:298
  49.6 4.9 %attend.3.refs_1_ = f32[256,640]{1,0:T(8,128)} custom-call(s32[4]{0:T(128)} %pad_add_fusion.1.meta_ref, f32[2,256,128]{2,1,0:T(8,128)} %copy-done.9, f32[3,256,128]{2,1,0:T(8,128)} %collective-permute-done.4.refs_1_, bf16[384,1024]{1,0:T(8,128)(2,1)} %get-tuple-element.74.refs_2_, bf16[2048,256]{1,0:T(8,128)(2,1)} %get-tuple-element.75.refs_3_), custom_call_target="tpu_custom_call" | custom-call | flops 1 | bytes 1 | tf_op jit(solution)/shard_map/attend/pallas_call | solution.py:144
  55.6 2.3 %prepare_weights.1 = (bf16[2,640,640]{2,1,0:T(8,128)(2,1)S(1)}, bf16[2,640,640]{2,1,0:T(8,128)(2,1)S(1)}) custom-call(s32[8]{0:T(128)S(1)} %stack.88.meta_ref, f32[320,640]{1,0:T(8,128)S(1)} %copy-done.2, f32[320,640]{1,0:T(8,128)} %collective-permute-done.6.refs_1_, f32[320,640]{1,0:T(8,128)} %collective-permute-done.7.refs_2_, ...), custom_call_target="tpu_custom_call" | custom-call | flops 1 | bytes 1 | tf_op jit(solution)/shard_map/prepare_weights/pallas_call | solution.py:177
  57.9 2.0 %project.6 = (f32[128,640]{1,0:T(8,128)S(1)}, f32[128,640]{1,0:T(8,128)S(1)}, f32[128,640]{1,0:T(8,128)S(1)}, f32[128,640]{1,0:T(8,128)S(1)}) custom-call(f32[256,640]{1,0:T(8,128)S(1)} %copy-done, f32[256,640]{1,0:T(8,128)S(1)} %copy-done.1, bf16[2,640,640]{2,1,0:T(8,128)(2,1)S(1)} %get-tuple-element.85.refs_2_.refs_1_, ...), custom_call_target="tpu_custom_call" | custom-call | flops 1 | bytes 1 | tf_op jit(solution)/shard_map/project/pallas_call | solution.py:204
  60.9 1.9 %project.7.kept_ref = f32[512,640]{1,0:T(8,128)S(1)} custom-call(f32[256,640]{1,0:T(8,128)S(1)} %copy-done, f32[256,640]{1,0:T(8,128)S(1)} %copy-done.1, bf16[2,640,640]{2,1,0:T(8,128)(2,1)S(1)} %get-tuple-element.85.refs_2_.refs_1_, bf16[2,640,640]{2,1,0:T(8,128)(2,1)S(1)} %get-tuple-element.86.refs_3_.refs_2_), custom_call_target="tpu_custom_call" | custom-call | flops 1 | bytes 1 | tf_op jit(solution)/shard_map/project/pallas_call | solution.py:204
  63.8 1.6 %collective-permute-start.13 = (f32[2,2,32,640]{3,2,1,0:T(8,128)S(1)}, f32[2,2,32,640]{3,2,1,0:T(8,128)S(1)}, u32[]{:S(2)}, u32[]{:S(2)}) collective-permute-start(f32[2,2,32,640]{3,2,1,0:T(8,128)S(1)} %get-tuple-element.103), channel_id=1, source_target_pairs={{0,8},{8,0},{16,24},{24,16},{1,9},{9,1},{17,25},{25,17},{2,10},{10... | collective-permute-start | bytes 983048 | tf_op jit(solution)/shard_map/ppermute | solution.py:298
  65.4 1.5 %collective-permute-start.14 = (f32[2,2,32,640]{3,2,1,0:T(8,128)S(1)}, f32[2,2,32,640]{3,2,1,0:T(8,128)S(1)}, u32[]{:S(2)}, u32[]{:S(2)}) collective-permute-start(f32[2,2,32,640]{3,2,1,0:T(8,128)S(1)} %get-tuple-element.104), channel_id=1, source_target_pairs={{0,16},{8,24},{16,0},{24,8},{1,17},{9,25},{17,1},{25,9},{2,18},{10... | collective-permute-start | bytes 983048 | tf_op jit(solution)/shard_map/ppermute | solution.py:298
  67.5 2.2 %project.9 = (f32[96,640]{1,0:T(8,128)S(1)}, f32[80,640]{1,0:T(8,128)S(1)}, f32[80,640]{1,0:T(8,128)S(1)}) custom-call(f32[256,640]{1,0:T(8,128)} %collective-permute-done.5.refs_0_, bf16[2,640,640]{2,1,0:T(8,128)(2,1)S(1)} %get-tuple-element.85.refs_2_.refs_1_, bf16[2,640,640]{2,1,0:T(8,128)(2,1)S(1)} %get-tuple-element.86.refs_3_.refs_2_), custom_call_target="tpu_custom_call" | custom-call | flops 1 | bytes 1 | tf_op jit(solution)/shard_map/project/pallas_call | solution.py:204
  69.8 2.2 %project.8.kept_ref = f32[256,640]{1,0:T(8,128)S(1)} custom-call(f32[256,640]{1,0:T(8,128)} %collective-permute-done.5.refs_0_, bf16[2,640,640]{2,1,0:T(8,128)(2,1)S(1)} %get-tuple-element.85.refs_2_.refs_1_, bf16[2,640,640]{2,1,0:T(8,128)(2,1)S(1)} %get-tuple-element.86.refs_3_.refs_2_), custom_call_target="tpu_custom_call" | custom-call | flops 1 | bytes 1 | tf_op jit(solution)/shard_map/project/pallas_call | solution.py:204
  75.0 1.6 %collective-permute-start.21 = (f32[2,1,32,640]{3,2,1,0:T(8,128)S(1)}, f32[2,1,32,640]{3,2,1,0:T(8,128)S(1)}, u32[]{:S(2)}, u32[]{:S(2)}) collective-permute-start(f32[2,1,32,640]{3,2,1,0:T(8,128)S(1)} %get-tuple-element.113), channel_id=1, source_target_pairs={{0,8},{8,0},{16,24},{24,16},{1,9},{9,1},{17,25},{25,17},{2,10},{10... | collective-permute-start | bytes 491528 | tf_op jit(solution)/shard_map/ppermute | solution.py:298
  77.2 1.3 %collective-permute-start.16 = (f32[2,32,640]{2,1,0:T(8,128)S(1)}, f32[2,32,640]{2,1,0:T(8,128)S(1)}, u32[]{:S(2)}, u32[]{:S(2)}) collective-permute-start(f32[2,32,640]{2,1,0:T(8,128)S(1)} %slice_bitcast_fusion.1), channel_id=1, source_target_pairs={{0,8},{8,0},{16,24},{24,16},{1,9},{9,1},{17,25},{25,17},{2,10},{10... | collective-permute-start | bytes 491528 | tf_op jit(solution)/shard_map/ppermute | solution.py:298
  78.5 5.6 %collective-permute-done.20.refs_0_ = f32[256,640]{1,0:T(8,128)S(1)} collective-permute-done((f32[256,640]{1,0:T(8,128)S(1)}, f32[256,640]{1,0:T(8,128)S(1)}, u32[]{:S(2)}, u32[]{:S(2)}) %collective-permute-start.20) | collective-permute-done | bytes 655392 | tf_op jit(solution)/shard_map/ppermute | solution.py:289
  85.8 1.3 %collective-permute-start.23 = (f32[1,32,640]{2,1,0:T(8,128)S(1)}, f32[1,32,640]{2,1,0:T(8,128)S(1)}, u32[]{:S(2)}, u32[]{:S(2)}) collective-permute-start(f32[1,32,640]{2,1,0:T(8,128)S(1)} %slice_bitcast_fusion.11), channel_id=1, source_target_pairs={{0,16},{8,24},{16,0},{24,8},{1,17},{9,25},{17,1},{25,9},{2,18},{10... | collective-permute-start | bytes 245768 | tf_op jit(solution)/shard_map/ppermute | solution.py:298
  87.1 1.3 %collective-permute-start.24 = (f32[1,32,640]{2,1,0:T(8,128)S(1)}, f32[1,32,640]{2,1,0:T(8,128)S(1)}, u32[]{:S(2)}, u32[]{:S(2)}) collective-permute-start(f32[1,32,640]{2,1,0:T(8,128)S(1)} %slice_bitcast_fusion.10), channel_id=1, source_target_pairs={{0,8},{8,0},{16,24},{24,16},{1,9},{9,1},{17,25},{25,17},{2,10},{10... | collective-permute-start | bytes 245768 | tf_op jit(solution)/shard_map/ppermute | solution.py:298
  91.7 3.8 %collective-permute-start.27 = (f32[64,640]{1,0:T(8,128)S(1)}, f32[64,640]{1,0:T(8,128)S(1)}, u32[]{:S(2)}, u32[]{:S(2)}) collective-permute-start(f32[64,640]{1,0:T(8,128)S(1)} %get-tuple-element.133), channel_id=1, source_target_pairs={{0,1},{2,0},{3,2},{1,3},{4,5},{6,4},{7,6},{5,7},{8,9},{10,8},{11,1... | collective-permute-start | bytes 491528 | tf_op jit(solution)/shard_map/ppermute | solution.py:289
  97.6 2.6 %collective-permute-done.31 = f32[1,32,640]{2,1,0:T(8,128)S(1)} collective-permute-done((f32[1,32,640]{2,1,0:T(8,128)S(1)}, f32[1,32,640]{2,1,0:T(8,128)S(1)}, u32[]{:S(2)}, u32[]{:S(2)}) %collective-permute-start.31) | collective-permute-done | bytes 81952 | tf_op jit(solution)/shard_map/ppermute | solution.py:298
  101.0 3.0 %collective-permute-start.32 = (f32[64,640]{1,0:T(8,128)S(1)}, f32[64,640]{1,0:T(8,128)S(1)}, u32[]{:S(2)}, u32[]{:S(2)}) collective-permute-start(f32[64,640]{1,0:T(8,128)S(1)} %maximum_bitcast_fusion), channel_id=1, source_target_pairs={{0,3},{2,1},{3,0},{1,2},{4,7},{6,5},{7,4},{5,6},{8,11},{10,9},{11,... | collective-permute-start | bytes 491528 | tf_op jit(solution)/shard_map/ppermute | solution.py:289
  104.1 4.2 %collective-permute-done.32.refs_2_ = f32[64,640]{1,0:T(8,128)S(1)} collective-permute-done((f32[64,640]{1,0:T(8,128)S(1)}, f32[64,640]{1,0:T(8,128)S(1)}, u32[]{:S(2)}, u32[]{:S(2)}) %collective-permute-start.32) | collective-permute-done | bytes 163872 | tf_op jit(solution)/shard_map/ppermute | solution.py:289
  108.3 1.6 %assemble.1 = f32[64,2560]{1,0:T(8,128)} custom-call(s32[4]{0:T(128)S(1)} %pad_add_fusion.meta_ref, f32[64,640]{1,0:T(8,128)S(1)} %get-tuple-element.134.refs_0_, f32[64,640]{1,0:T(8,128)S(1)} %collective-permute-done.27.refs_1_, f32[64,640]{1,0:T(8,128)S(1)} %collective-permute-done.32.refs_2_, f32[64,640]{1,0:T(8,128)S(1)} %collective-permute-done.33.refs_3_), custom_call_target="tpu_custom_call" | custom-call | flops 1 | bytes 1 | tf_op jit(solution)/shard_map/assemble/pallas_call | solution.py:266
  (100 shorter events, 19.3 us)
Async XLA Ops:
  1.5 14.1 %collective-permute-start = (f32[2,256,128]{2,1,0:T(8,128)S(1)}, f32[2,256,128]{2,1,0:T(8,128)S(1)}, u32[]{:S(2)}, u32[]{:S(2)}) collective-permute-start(f32[2,256,128]{2,1,0:T(8,128)S(1)} %pad_maximum_fusion.refs_0_), channel_id=1, source_target_pairs={{0,2},{2,3},{3,1},{1,0},{4,6},{6,7},{7,5},{5,4},{8,10},{10,11},{11... | collective-permute-start | bytes 786440 | tf_op jit(solution)/shard_map/ppermute | solution.py:289
  5.6 14.2 %collective-permute-start.1 = (f32[2,256,128]{2,1,0:T(8,128)S(1)}, f32[2,256,128]{2,1,0:T(8,128)S(1)}, u32[]{:S(2)}, u32[]{:S(2)}) collective-permute-start(f32[2,256,128]{2,1,0:T(8,128)S(1)} %pad_maximum_fusion.refs_0_), channel_id=1, source_target_pairs={{0,3},{2,1},{3,0},{1,2},{4,7},{6,5},{7,4},{5,6},{8,11},{10,9},{11,... | collective-permute-start | bytes 786440 | tf_op jit(solution)/shard_map/ppermute | solution.py:289
  7.0 22.9 %collective-permute-start.2 = (f32[2,256,128]{2,1,0:T(8,128)S(1)}, f32[2,256,128]{2,1,0:T(8,128)S(1)}, u32[]{:S(2)}, u32[]{:S(2)}) collective-permute-start(f32[2,256,128]{2,1,0:T(8,128)S(1)} %pad_maximum_fusion.refs_0_), channel_id=1, source_target_pairs={{0,1},{2,0},{3,2},{1,3},{4,5},{6,4},{7,6},{5,7},{8,9},{10,8},{11,1... | collective-permute-start | bytes 786440 | tf_op jit(solution)/shard_map/ppermute | solution.py:289
  11.3 36.5 %collective-permute-start.6 = (f32[320,640]{1,0:T(8,128)}, f32[320,640]{1,0:T(8,128)}, u32[]{:S(2)}, u32[]{:S(2)}) collective-permute-start(f32[320,640]{1,0:T(8,128)} %get-tuple-element.130), channel_id=1, source_target_pairs={{0,8},{8,0},{16,24},{24,16},{1,9},{9,1},{17,25},{25,17},{2,10},{10... | collective-permute-start | bytes 2457608 | tf_op jit(solution)/shard_map/ppermute | solution.py:298
  12.8 36.7 %collective-permute-start.7 = (f32[320,640]{1,0:T(8,128)}, f32[320,640]{1,0:T(8,128)}, u32[]{:S(2)}, u32[]{:S(2)}) collective-permute-start(f32[320,640]{1,0:T(8,128)} %get-tuple-element.132), channel_id=1, source_target_pairs={{0,16},{8,24},{16,0},{24,8},{1,17},{9,25},{17,1},{25,9},{2,18},{10... | collective-permute-start | bytes 2457608 | tf_op jit(solution)/shard_map/ppermute | solution.py:298
  15.6 33.9 %collective-permute-start.8 = (f32[320,640]{1,0:T(8,128)}, f32[320,640]{1,0:T(8,128)}, u32[]{:S(2)}, u32[]{:S(2)}) collective-permute-start(f32[320,640]{1,0:T(8,128)} %get-tuple-element.129), channel_id=1, source_target_pairs={{0,24},{8,16},{16,8},{24,0},{1,25},{9,17},{17,9},{25,1},{2,26},{10... | collective-permute-start | bytes 2457608 | tf_op jit(solution)/shard_map/ppermute | solution.py:298
  29.8 16.7 %collective-permute-start.4 = (f32[3,256,128]{2,1,0:T(8,128)S(1)}, f32[3,256,128]{2,1,0:T(8,128)}, u32[]{:S(2)}, u32[]{:S(2)}) collective-permute-start(f32[3,256,128]{2,1,0:T(8,128)S(1)} %slice.65.refs_1_), channel_id=1, source_target_pairs={{0,2},{2,3},{3,1},{1,0},{4,6},{6,7},{7,5},{5,4},{8,10},{10,11},{11... | collective-permute-start | bytes 1179656 | tf_op jit(solution)/shard_map/ppermute | solution.py:289
  30.5 16.0 %collective-permute-start.3 = (f32[2,256,128]{2,1,0:T(8,128)S(1)}, f32[2,256,128]{2,1,0:T(8,128)S(1)}, u32[]{:S(2)}, u32[]{:S(2)}) collective-permute-start(f32[2,256,128]{2,1,0:T(8,128)S(1)} %slice.64.refs_0_), channel_id=1, source_target_pairs={{0,2},{2,3},{3,1},{1,0},{4,6},{6,7},{7,5},{5,4},{8,10},{10,11},{11... | collective-permute-start | bytes 786440 | tf_op jit(solution)/shard_map/ppermute | solution.py:289
  46.5 17.1 %collective-permute-start.5 = (f32[256,640]{1,0:T(8,128)}, f32[256,640]{1,0:T(8,128)}, u32[]{:S(2)}, u32[]{:S(2)}) collective-permute-start(f32[256,640]{1,0:T(8,128)} %attend.2.refs_0_), channel_id=1, source_target_pairs={{0,1},{2,0},{3,2},{1,3},{4,5},{6,4},{7,6},{5,7},{8,9},{10,8},{11,1... | collective-permute-start | bytes 1966088 | tf_op jit(solution)/shard_map/ppermute | solution.py:289
  59.8 3.0 %collective-permute-start.9 = (f32[128,640]{1,0:T(8,128)S(1)}, f32[128,640]{1,0:T(8,128)S(1)}, u32[]{:S(2)}, u32[]{:S(2)}) collective-permute-start(f32[128,640]{1,0:T(8,128)S(1)} %get-tuple-element.87), channel_id=1, source_target_pairs={{0,4},{4,0},{1,5},{5,1},{2,6},{6,2},{3,7},{7,3},{8,12},{12,8},{9,1... | collective-permute-start | bytes 983048 | tf_op jit(solution)/shard_map/ppermute | solution.py:290
  59.9 3.0 %collective-permute-start.10 = (f32[128,640]{1,0:T(8,128)S(1)}, f32[128,640]{1,0:T(8,128)S(1)}, u32[]{:S(2)}, u32[]{:S(2)}) collective-permute-start(f32[128,640]{1,0:T(8,128)S(1)} %get-tuple-element.88), channel_id=1, source_target_pairs={{0,4},{4,0},{1,5},{5,1},{2,6},{6,2},{3,7},{7,3},{8,12},{12,8},{9,1... | collective-permute-start | bytes 983048 | tf_op jit(solution)/shard_map/ppermute | solution.py:290
  60.4 2.5 %collective-permute-start.11 = (f32[128,640]{1,0:T(8,128)S(1)}, f32[128,640]{1,0:T(8,128)S(1)}, u32[]{:S(2)}, u32[]{:S(2)}) collective-permute-start(f32[128,640]{1,0:T(8,128)S(1)} %get-tuple-element.89), channel_id=1, source_target_pairs={{0,4},{4,0},{1,5},{5,1},{2,6},{6,2},{3,7},{7,3},{8,12},{12,8},{9,1... | collective-permute-start | bytes 983048 | tf_op jit(solution)/shard_map/ppermute | solution.py:290
  60.5 2.4 %collective-permute-start.12 = (f32[128,640]{1,0:T(8,128)S(1)}, f32[128,640]{1,0:T(8,128)S(1)}, u32[]{:S(2)}, u32[]{:S(2)}) collective-permute-start(f32[128,640]{1,0:T(8,128)S(1)} %get-tuple-element.90), channel_id=1, source_target_pairs={{0,4},{4,0},{1,5},{5,1},{2,6},{6,2},{3,7},{7,3},{8,12},{12,8},{9,1... | collective-permute-start | bytes 983048 | tf_op jit(solution)/shard_map/ppermute | solution.py:290
  63.8 9.2 %collective-permute-start.13 = (f32[2,2,32,640]{3,2,1,0:T(8,128)S(1)}, f32[2,2,32,640]{3,2,1,0:T(8,128)S(1)}, u32[]{:S(2)}, u32[]{:S(2)}) collective-permute-start(f32[2,2,32,640]{3,2,1,0:T(8,128)S(1)} %get-tuple-element.103), channel_id=1, source_target_pairs={{0,8},{8,0},{16,24},{24,16},{1,9},{9,1},{17,25},{25,17},{2,10},{10... | collective-permute-start | bytes 983048 | tf_op jit(solution)/shard_map/ppermute | solution.py:298
  65.4 8.5 %collective-permute-start.14 = (f32[2,2,32,640]{3,2,1,0:T(8,128)S(1)}, f32[2,2,32,640]{3,2,1,0:T(8,128)S(1)}, u32[]{:S(2)}, u32[]{:S(2)}) collective-permute-start(f32[2,2,32,640]{3,2,1,0:T(8,128)S(1)} %get-tuple-element.104), channel_id=1, source_target_pairs={{0,16},{8,24},{16,0},{24,8},{1,17},{9,25},{17,1},{25,9},{2,18},{10... | collective-permute-start | bytes 983048 | tf_op jit(solution)/shard_map/ppermute | solution.py:298
  66.9 17.1 %collective-permute-start.20 = (f32[256,640]{1,0:T(8,128)S(1)}, f32[256,640]{1,0:T(8,128)S(1)}, u32[]{:S(2)}, u32[]{:S(2)}) collective-permute-start(f32[256,640]{1,0:T(8,128)S(1)} %copy-done.1), channel_id=1, source_target_pairs={{0,2},{2,3},{3,1},{1,0},{4,6},{6,7},{7,5},{5,4},{8,10},{10,11},{11... | collective-permute-start | bytes 1966088 | tf_op jit(solution)/shard_map/ppermute | solution.py:289
  69.7 5.2 %collective-permute-start.17 = (f32[96,640]{1,0:T(8,128)S(1)}, f32[96,640]{1,0:T(8,128)S(1)}, u32[]{:S(2)}, u32[]{:S(2)}) collective-permute-start(f32[96,640]{1,0:T(8,128)S(1)} %get-tuple-element.109), channel_id=1, source_target_pairs={{0,4},{4,0},{1,5},{5,1},{2,6},{6,2},{3,7},{7,3},{8,12},{12,8},{9,1... | collective-permute-start | bytes 737288 | tf_op jit(solution)/shard_map/ppermute | solution.py:290
  72.0 2.9 %collective-permute-start.18 = (f32[80,640]{1,0:T(8,128)S(1)}, f32[80,640]{1,0:T(8,128)S(1)}, u32[]{:S(2)}, u32[]{:S(2)}) collective-permute-start(f32[80,640]{1,0:T(8,128)S(1)} %get-tuple-element.110), channel_id=1, source_target_pairs={{0,4},{4,0},{1,5},{5,1},{2,6},{6,2},{3,7},{7,3},{8,12},{12,8},{9,1... | collective-permute-start | bytes 614408 | tf_op jit(solution)/shard_map/ppermute | solution.py:290
  74.0 16.7 %collective-permute-start.15 = (f32[2,32,640]{2,1,0:T(8,128)S(1)}, f32[2,32,640]{2,1,0:T(8,128)S(1)}, u32[]{:S(2)}, u32[]{:S(2)}) collective-permute-start(f32[2,32,640]{2,1,0:T(8,128)S(1)} %slice_bitcast_fusion.2), channel_id=1, source_target_pairs={{0,16},{8,24},{16,0},{24,8},{1,17},{9,25},{17,1},{25,9},{2,18},{10... | collective-permute-start | bytes 491528 | tf_op jit(solution)/shard_map/ppermute | solution.py:298
  75.0 9.0 %collective-permute-start.21 = (f32[2,1,32,640]{3,2,1,0:T(8,128)S(1)}, f32[2,1,32,640]{3,2,1,0:T(8,128)S(1)}, u32[]{:S(2)}, u32[]{:S(2)}) collective-permute-start(f32[2,1,32,640]{3,2,1,0:T(8,128)S(1)} %get-tuple-element.113), channel_id=1, source_target_pairs={{0,8},{8,0},{16,24},{24,16},{1,9},{9,1},{17,25},{25,17},{2,10},{10... | collective-permute-start | bytes 491528 | tf_op jit(solution)/shard_map/ppermute | solution.py:298
  76.6 7.4 %collective-permute-start.22 = (f32[2,1,32,640]{3,2,1,0:T(8,128)S(1)}, f32[2,1,32,640]{3,2,1,0:T(8,128)S(1)}, u32[]{:S(2)}, u32[]{:S(2)}) collective-permute-start(f32[2,1,32,640]{3,2,1,0:T(8,128)S(1)} %get-tuple-element.114), channel_id=1, source_target_pairs={{0,16},{8,24},{16,0},{24,8},{1,17},{9,25},{17,1},{25,9},{2,18},{10... | collective-permute-start | bytes 491528 | tf_op jit(solution)/shard_map/ppermute | solution.py:298
  77.2 14.2 %collective-permute-start.16 = (f32[2,32,640]{2,1,0:T(8,128)S(1)}, f32[2,32,640]{2,1,0:T(8,128)S(1)}, u32[]{:S(2)}, u32[]{:S(2)}) collective-permute-start(f32[2,32,640]{2,1,0:T(8,128)S(1)} %slice_bitcast_fusion.1), channel_id=1, source_target_pairs={{0,8},{8,0},{16,24},{24,16},{1,9},{9,1},{17,25},{25,17},{2,10},{10... | collective-permute-start | bytes 491528 | tf_op jit(solution)/shard_map/ppermute | solution.py:298
  85.2 4.2 %collective-permute-start.26 = (f32[128,640]{1,0:T(8,128)S(1)}, f32[128,640]{1,0:T(8,128)S(1)}, u32[]{:S(2)}, u32[]{:S(2)}) collective-permute-start(f32[128,640]{1,0:T(8,128)S(1)} %get-tuple-element.120), channel_id=1, source_target_pairs={{0,4},{4,0},{1,5},{5,1},{2,6},{6,2},{3,7},{7,3},{8,12},{12,8},{9,1... | collective-permute-start | bytes 983048 | tf_op jit(solution)/shard_map/ppermute | solution.py:290
  85.8 5.6 %collective-permute-start.23 = (f32[1,32,640]{2,1,0:T(8,128)S(1)}, f32[1,32,640]{2,1,0:T(8,128)S(1)}, u32[]{:S(2)}, u32[]{:S(2)}) collective-permute-start(f32[1,32,640]{2,1,0:T(8,128)S(1)} %slice_bitcast_fusion.11), channel_id=1, source_target_pairs={{0,16},{8,24},{16,0},{24,8},{1,17},{9,25},{17,1},{25,9},{2,18},{10... | collective-permute-start | bytes 245768 | tf_op jit(solution)/shard_map/ppermute | solution.py:298
  87.1 4.5 %collective-permute-start.24 = (f32[1,32,640]{2,1,0:T(8,128)S(1)}, f32[1,32,640]{2,1,0:T(8,128)S(1)}, u32[]{:S(2)}, u32[]{:S(2)}) collective-permute-start(f32[1,32,640]{2,1,0:T(8,128)S(1)} %slice_bitcast_fusion.10), channel_id=1, source_target_pairs={{0,8},{8,0},{16,24},{24,16},{1,9},{9,1},{17,25},{25,17},{2,10},{10... | collective-permute-start | bytes 245768 | tf_op jit(solution)/shard_map/ppermute | solution.py:298
  89.6 6.1 %collective-permute-start.30 = (f32[2,1,32,640]{3,2,1,0:T(8,128)S(1)}, f32[2,1,32,640]{3,2,1,0:T(8,128)S(1)}, u32[]{:S(2)}, u32[]{:S(2)}) collective-permute-start(f32[2,1,32,640]{3,2,1,0:T(8,128)S(1)} %get-tuple-element.122), channel_id=1, source_target_pairs={{0,16},{8,24},{16,0},{24,8},{1,17},{9,25},{17,1},{25,9},{2,18},{10... | collective-permute-start | bytes 491528 | tf_op jit(solution)/shard_map/ppermute | solution.py:298
  90.7 5.7 %collective-permute-start.28 = (f32[2,1,32,640]{3,2,1,0:T(8,128)S(1)}, f32[2,1,32,640]{3,2,1,0:T(8,128)S(1)}, u32[]{:S(2)}, u32[]{:S(2)}) collective-permute-start(f32[2,1,32,640]{3,2,1,0:T(8,128)S(1)} %get-tuple-element.121), channel_id=1, source_target_pairs={{0,8},{8,0},{16,24},{24,16},{1,9},{9,1},{17,25},{25,17},{2,10},{10... | collective-permute-start | bytes 491528 | tf_op jit(solution)/shard_map/ppermute | solution.py:298
  91.7 12.4 %collective-permute-start.27 = (f32[64,640]{1,0:T(8,128)S(1)}, f32[64,640]{1,0:T(8,128)S(1)}, u32[]{:S(2)}, u32[]{:S(2)}) collective-permute-start(f32[64,640]{1,0:T(8,128)S(1)} %get-tuple-element.133), channel_id=1, source_target_pairs={{0,1},{2,0},{3,2},{1,3},{4,5},{6,4},{7,6},{5,7},{8,9},{10,8},{11,1... | collective-permute-start | bytes 491528 | tf_op jit(solution)/shard_map/ppermute | solution.py:289
  95.6 8.5 %collective-permute-start.33 = (f32[64,640]{1,0:T(8,128)S(1)}, f32[64,640]{1,0:T(8,128)S(1)}, u32[]{:S(2)}, u32[]{:S(2)}) collective-permute-start(f32[64,640]{1,0:T(8,128)S(1)} %maximum_bitcast_fusion.1), channel_id=1, source_target_pairs={{0,2},{2,3},{3,1},{1,0},{4,6},{6,7},{7,5},{5,4},{8,10},{10,11},{11... | collective-permute-start | bytes 491528 | tf_op jit(solution)/shard_map/ppermute | solution.py:289
  95.7 4.5 %collective-permute-start.31 = (f32[1,32,640]{2,1,0:T(8,128)S(1)}, f32[1,32,640]{2,1,0:T(8,128)S(1)}, u32[]{:S(2)}, u32[]{:S(2)}) collective-permute-start(f32[1,32,640]{2,1,0:T(8,128)S(1)} %slice_bitcast_fusion.6), channel_id=1, source_target_pairs={{0,8},{8,0},{16,24},{24,16},{1,9},{9,1},{17,25},{25,17},{2,10},{10... | collective-permute-start | bytes 245768 | tf_op jit(solution)/shard_map/ppermute | solution.py:298
  96.5 4.5 %collective-permute-start.29 = (f32[1,32,640]{2,1,0:T(8,128)S(1)}, f32[1,32,640]{2,1,0:T(8,128)S(1)}, u32[]{:S(2)}, u32[]{:S(2)}) collective-permute-start(f32[1,32,640]{2,1,0:T(8,128)S(1)} %slice_bitcast_fusion.8), channel_id=1, source_target_pairs={{0,16},{8,24},{16,0},{24,8},{1,17},{9,25},{17,1},{25,9},{2,18},{10... | collective-permute-start | bytes 245768 | tf_op jit(solution)/shard_map/ppermute | solution.py:298
  101.0 7.3 %collective-permute-start.32 = (f32[64,640]{1,0:T(8,128)S(1)}, f32[64,640]{1,0:T(8,128)S(1)}, u32[]{:S(2)}, u32[]{:S(2)}) collective-permute-start(f32[64,640]{1,0:T(8,128)S(1)} %maximum_bitcast_fusion), channel_id=1, source_target_pairs={{0,3},{2,1},{3,0},{1,2},{4,7},{6,5},{7,4},{5,6},{8,11},{10,9},{11,... | collective-permute-start | bytes 491528 | tf_op jit(solution)/shard_map/ppermute | solution.py:289
  (12 other events, 93.4 us)

commit v5 on v4

--- a/solution.py
+++ b/solution.py
@@ -310,8 +310,8 @@
     owns = {0: attend(meta, [upper, lower], 0, kt, vv)}
     back, *sent = after(owns[0], *sent)
     owns[planes - 1] = ring(back, -1)
-    sent[0], sent[1], *pieces = after(*sent, *pieces)
     owns[1] = attend(meta, sent, 1, kt, vv)
+    owns[1], *pieces = after(owns[1], *pieces)
     owns[2] = ring(owns[1], 1)
     high, low = prepare_weights(ints(*places), [mine] + pieces)
 

time: 110 us -> 108 us (0.982)
  waiting for transfers between devices: 37.5 us -> 27.2 us
  starting transfers between devices: 36.8 us -> 45.3 us
    ppermute x10, waiting for transfers between devices: 30.7 us -> 21.2 us  [by_heads(): ring = lambda x, step: lax.ppermute(x, 'seq', ring_perm(planes, step))]
    ppermute x10, starting transfers between devices: 17.4 us -> 26.6 us  [by_heads(): ring = lambda x, step: lax.ppermute(x, 'seq', ring_perm(planes, step))]
    ppermute x15, waiting for transfers between devices: 6.69 us -> 5.07 us  [by_heads(): lax.ppermute(x, 'feature', [(i, i ^ e) for i in range(parts)])]
  transfers between devices with their start and end apart: 34 -> 34, of which waited for: 12 -> 13; matrix products, arithmetic and copies ran while one was open for 5% -> 6% of each run, Pallas kernels for 22% -> 22%
where the time goes in v5:
time: 108 us
  starting transfers between devices  45.3 us (42%)
  waiting for transfers between devices  27.2 us (25%)
  Pallas kernels  25.9 us (24%)
  local copies, waits for them, and re-layouts  7.71 us (7%)
    ppermute x10, starting transfers between devices, by_heads(): ring = lambda x, step: lax.ppermute(x, 'seq', ring_perm(planes, step))  26.6 us
    ppermute x10, waiting for transfers between devices, by_heads(): ring = lambda x, step: lax.ppermute(x, 'seq', ring_perm(planes, step))  21.2 us
    ppermute x15, starting transfers between devices, by_heads(): lax.ppermute(x, 'feature', [(i, i ^ e) for i in range(parts)])  16.3 us
    pallas_call x6, Pallas kernels, project(): pl.pallas_call(kernel, out_shape=tuple((jax.ShapeDtypeStruct((b - a, colu...  10.4 us
    pallas_call x2, Pallas kernels, attend(): pl.pallas_call(kernel, out_shape=jax.ShapeDtypeStruct((rows, group * d),...  8.61 us
    ppermute x15, waiting for transfers between devices, by_heads(): lax.ppermute(x, 'feature', [(i, i ^ e) for i in range(parts)])  5.07 us
    transpose x1, local copies, waits for them, and re-layouts, by_heads(): turn = lambda x: lax.dynamic_slice_in_dim(w_out, x * k_rows, k_rows, 0).T  3.69 us
    pallas_call x1, Pallas kernels, prepare_keys(): pl.pallas_call(kernel, out_shape=(jax.ShapeDtypeStruct((3 * d, n * rows),...  2.66 us
  transfers between devices with their start and end apart: 34, of which 13 were waited for; matrix products, arithmetic and copies ran while one was open for 6% of the time, Pallas kernels for 22%

profile of v5, /device:TPU:0, one launch (start us, length us, event | category | flops | bytes accessed | tf_op | source)
XLA Modules:
  0.0 107.6 jit_solution(12913338606925910271)
XLA Ops:
  0.0 1.5 %constant_dynamic-slice_fusion = (f32[256,1,128]{2,1,0:T(1,128)S(1)}, f32[256,1,128]{2,1,0:T(1,128)S(1)}) fusion(f32[256,4,128]{2,1,0:T(4,128)} %param.6, s32[]{:T(128)S(6)} %select_n.139, f32[256,4,128]{2,1,0:T(4,128)} %param.5), kind=kLoop, calls=%fused_computation.32 | loop fusion | bytes 524292 | tf_op jit(solution)/shard_map/jit(dynamic_index_in_dim)/dynamic_slice | solution.py:292
  1.5 3.1 %collective-permute-start.2 = (f32[2,256,128]{2,1,0:T(8,128)S(1)}, f32[2,256,128]{2,1,0:T(8,128)S(1)}, u32[]{:S(2)}, u32[]{:S(2)}) collective-permute-start(f32[2,256,128]{2,1,0:T(8,128)S(1)} %pad_maximum_fusion.refs_0_), channel_id=1, source_target_pairs={{0,1},{2,0},{3,2},{1,3},{4,5},{6,4},{7,6},{5,7},{8,9},{10,8},{11,1... | collective-permute-start | bytes 786440 | tf_op jit(solution)/shard_map/ppermute | solution.py:289
  4.6 2.5 %collective-permute-start.1 = (f32[2,256,128]{2,1,0:T(8,128)S(1)}, f32[2,256,128]{2,1,0:T(8,128)S(1)}, u32[]{:S(2)}, u32[]{:S(2)}) collective-permute-start(f32[2,256,128]{2,1,0:T(8,128)S(1)} %pad_maximum_fusion.refs_0_), channel_id=1, source_target_pairs={{0,3},{2,1},{3,0},{1,2},{4,7},{6,5},{7,4},{5,6},{8,11},{10,9},{11,... | collective-permute-start | bytes 786440 | tf_op jit(solution)/shard_map/ppermute | solution.py:289
  7.1 1.6 %collective-permute-start = (f32[2,256,128]{2,1,0:T(8,128)S(1)}, f32[2,256,128]{2,1,0:T(8,128)S(1)}, u32[]{:S(2)}, u32[]{:S(2)}) collective-permute-start(f32[2,256,128]{2,1,0:T(8,128)S(1)} %pad_maximum_fusion.refs_0_), channel_id=1, source_target_pairs={{0,2},{2,3},{3,1},{1,0},{4,6},{6,7},{7,5},{5,4},{8,10},{10,11},{11... | collective-permute-start | bytes 786440 | tf_op jit(solution)/shard_map/ppermute | solution.py:289
  8.6 3.7 %dynamic-slice_bitcast_fusion = (f32[320,640]{1,0:T(8,128)}, f32[320,640]{1,0:T(8,128)}, f32[320,640]{1,0:T(8,128)}, f32[320,640]{1,0:T(8,128)}) fusion(f32[2560,320]{0,1:T(8,128)} %param.7, s32[]{:T(128)S(6)} %select_n.150, s32[]{:T(128)S(6)} %select_n.148, s32[]{:T(128)S(6)} %select_n.140, s32[]{:T(128)S(6)} %select_n.149), kind=kLoop, calls=%fused_computation | loop fusion | bytes 6553616 | tf_op jit(solution)/shard_map/transpose | solution.py:297
  12.3 2.4 %collective-permute-start.8 = (f32[320,640]{1,0:T(8,128)}, f32[320,640]{1,0:T(8,128)}, u32[]{:S(2)}, u32[]{:S(2)}) collective-permute-start(f32[320,640]{1,0:T(8,128)} %get-tuple-element.127), channel_id=1, source_target_pairs={{0,24},{8,16},{16,8},{24,0},{1,25},{9,17},{17,9},{25,1},{2,26},{10... | collective-permute-start | bytes 2457608 | tf_op jit(solution)/shard_map/ppermute | solution.py:298
  17.8 2.1 %collective-permute-done.1.refs_2_ = f32[2,256,128]{2,1,0:T(8,128)S(1)} collective-permute-done((f32[2,256,128]{2,1,0:T(8,128)S(1)}, f32[2,256,128]{2,1,0:T(8,128)S(1)}, u32[]{:S(2)}, u32[]{:S(2)}) %collective-permute-start.1) | collective-permute-done | bytes 262176 | tf_op jit(solution)/shard_map/ppermute | solution.py:289
  20.0 3.2 %collective-permute-done.refs_1_ = f32[2,256,128]{2,1,0:T(8,128)S(1)} collective-permute-done((f32[2,256,128]{2,1,0:T(8,128)S(1)}, f32[2,256,128]{2,1,0:T(8,128)S(1)}, u32[]{:S(2)}, u32[]{:S(2)}) %collective-permute-start) | collective-permute-done | bytes 262176 | tf_op jit(solution)/shard_map/ppermute | solution.py:289
  23.1 8.5 %collective-permute-start.4 = (f32[3,256,128]{2,1,0:T(8,128)S(1)}, f32[3,256,128]{2,1,0:T(8,128)}, u32[]{:S(2)}, u32[]{:S(2)}) collective-permute-start(f32[3,256,128]{2,1,0:T(8,128)S(1)} %slice.65.refs_1_), channel_id=1, source_target_pairs={{0,2},{2,3},{3,1},{1,0},{4,6},{6,7},{7,5},{5,4},{8,10},{10,11},{11... | collective-permute-start | bytes 1179656 | tf_op jit(solution)/shard_map/ppermute | solution.py:289
  32.4 2.7 %prepare_keys.1 = (bf16[384,1024]{1,0:T(8,128)(2,1)}, bf16[2048,256]{1,0:T(8,128)(2,1)}) custom-call(f32[2,256,128]{2,1,0:T(8,128)} %copy-done.4, f32[2,256,128]{2,1,0:T(8,128)} %copy-done.8, f32[2,256,128]{2,1,0:T(8,128)} %copy-done.7, f32[2,256,128]{2,1,0:T(8,128)} %copy-done.6), custom_call_target="tpu_custom_call" | custom-call | flops 1 | bytes 1 | tf_op jit(solution)/shard_map/prepare_keys/pallas_call | solution.py:83
  35.1 3.7 %attend.2.refs_0_ = f32[256,640]{1,0:T(8,128)} custom-call(s32[4]{0:T(128)} %pad_add_fusion.1.meta_ref, f32[2,256,128]{2,1,0:T(8,128)} %copy-done.5, f32[3,256,128]{2,1,0:T(8,128)} %copy-done.3, bf16[384,1024]{1,0:T(8,128)(2,1)} %get-tuple-element.73.refs_2_, bf16[2048,256]{1,0:T(8,128)(2,1)} %get-tuple-element.74.refs_3_), custom_call_target="tpu_custom_call" | custom-call | flops 1 | bytes 1 | tf_op jit(solution)/shard_map/attend/pallas_call | solution.py:144
  38.7 6.1 %collective-permute-done.3.refs_0_ = f32[2,256,128]{2,1,0:T(8,128)S(1)} collective-permute-done((f32[2,256,128]{2,1,0:T(8,128)S(1)}, f32[2,256,128]{2,1,0:T(8,128)S(1)}, u32[]{:S(2)}, u32[]{:S(2)}) %collective-permute-start.3) | collective-permute-done | bytes 262176 | tf_op jit(solution)/shard_map/ppermute | solution.py:289
  44.9 1.5 %collective-permute-start.5 = (f32[256,640]{1,0:T(8,128)}, f32[256,640]{1,0:T(8,128)}, u32[]{:S(2)}, u32[]{:S(2)}) collective-permute-start(f32[256,640]{1,0:T(8,128)} %attend.2.refs_0_), channel_id=1, source_target_pairs={{0,1},{2,0},{3,2},{1,3},{4,5},{6,4},{7,6},{5,7},{8,9},{10,8},{11,1... | collective-permute-start | bytes 1966088 | tf_op jit(solution)/shard_map/ppermute | solution.py:289
  46.5 5.0 %attend.3.refs_1_ = f32[256,640]{1,0:T(8,128)} custom-call(s32[4]{0:T(128)} %pad_add_fusion.1.meta_ref, f32[2,256,128]{2,1,0:T(8,128)} %copy-done.9, f32[3,256,128]{2,1,0:T(8,128)} %collective-permute-done.4.refs_1_, bf16[384,1024]{1,0:T(8,128)(2,1)} %get-tuple-element.73.refs_2_, bf16[2048,256]{1,0:T(8,128)(2,1)} %get-tuple-element.74.refs_3_), custom_call_target="tpu_custom_call" | custom-call | flops 1 | bytes 1 | tf_op jit(solution)/shard_map/attend/pallas_call | solution.py:144
  52.6 2.2 %prepare_weights.1 = (bf16[2,640,640]{2,1,0:T(8,128)(2,1)S(1)}, bf16[2,640,640]{2,1,0:T(8,128)(2,1)S(1)}) custom-call(s32[8]{0:T(128)S(1)} %stack.88.meta_ref, f32[320,640]{1,0:T(8,128)S(1)} %copy-done.2, f32[320,640]{1,0:T(8,128)} %collective-permute-done.6.refs_1_, f32[320,640]{1,0:T(8,128)} %collective-permute-done.7.refs_2_, ...), custom_call_target="tpu_custom_call" | custom-call | flops 1 | bytes 1 | tf_op jit(solution)/shard_map/prepare_weights/pallas_call | solution.py:177
  54.9 1.9 %project.6 = (f32[128,640]{1,0:T(8,128)S(1)}, f32[128,640]{1,0:T(8,128)S(1)}, f32[128,640]{1,0:T(8,128)S(1)}, f32[128,640]{1,0:T(8,128)S(1)}) custom-call(f32[256,640]{1,0:T(8,128)S(1)} %copy-done, f32[256,640]{1,0:T(8,128)S(1)} %copy-done.1, bf16[2,640,640]{2,1,0:T(8,128)(2,1)S(1)} %get-tuple-element.83.refs_2_.refs_1_, ...), custom_call_target="tpu_custom_call" | custom-call | flops 1 | bytes 1 | tf_op jit(solution)/shard_map/project/pallas_call | solution.py:204
  57.9 1.9 %project.7.kept_ref = f32[512,640]{1,0:T(8,128)S(1)} custom-call(f32[256,640]{1,0:T(8,128)S(1)} %copy-done, f32[256,640]{1,0:T(8,128)S(1)} %copy-done.1, bf16[2,640,640]{2,1,0:T(8,128)(2,1)S(1)} %get-tuple-element.83.refs_2_.refs_1_, bf16[2,640,640]{2,1,0:T(8,128)(2,1)S(1)} %get-tuple-element.84.refs_3_.refs_2_), custom_call_target="tpu_custom_call" | custom-call | flops 1 | bytes 1 | tf_op jit(solution)/shard_map/project/pallas_call | solution.py:204
  59.9 1.7 %collective-permute-done.5.refs_0_ = f32[256,640]{1,0:T(8,128)} collective-permute-done((f32[256,640]{1,0:T(8,128)}, f32[256,640]{1,0:T(8,128)}, u32[]{:S(2)}, u32[]{:S(2)}) %collective-permute-start.5) | collective-permute-done | bytes 655392 | tf_op jit(solution)/shard_map/ppermute | solution.py:289
  61.8 1.6 %collective-permute-start.13 = (f32[2,2,32,640]{3,2,1,0:T(8,128)S(1)}, f32[2,2,32,640]{3,2,1,0:T(8,128)S(1)}, u32[]{:S(2)}, u32[]{:S(2)}) collective-permute-start(f32[2,2,32,640]{3,2,1,0:T(8,128)S(1)} %get-tuple-element.101), channel_id=1, source_target_pairs={{0,8},{8,0},{16,24},{24,16},{1,9},{9,1},{17,25},{25,17},{2,10},{10... | collective-permute-start | bytes 983048 | tf_op jit(solution)/shard_map/ppermute | solution.py:298
  63.4 1.5 %collective-permute-start.14 = (f32[2,2,32,640]{3,2,1,0:T(8,128)S(1)}, f32[2,2,32,640]{3,2,1,0:T(8,128)S(1)}, u32[]{:S(2)}, u32[]{:S(2)}) collective-permute-start(f32[2,2,32,640]{3,2,1,0:T(8,128)S(1)} %get-tuple-element.102), channel_id=1, source_target_pairs={{0,16},{8,24},{16,0},{24,8},{1,17},{9,25},{17,1},{25,9},{2,18},{10... | collective-permute-start | bytes 983048 | tf_op jit(solution)/shard_map/ppermute | solution.py:298
  64.9 1.7 %collective-permute-start.20 = (f32[256,640]{1,0:T(8,128)S(1)}, f32[256,640]{1,0:T(8,128)S(1)}, u32[]{:S(2)}, u32[]{:S(2)}) collective-permute-start(f32[256,640]{1,0:T(8,128)S(1)} %copy-done.1), channel_id=1, source_target_pairs={{0,2},{2,3},{3,1},{1,0},{4,6},{6,7},{7,5},{5,4},{8,10},{10,11},{11... | collective-permute-start | bytes 1966088 | tf_op jit(solution)/shard_map/ppermute | solution.py:289
  66.6 2.2 %project.9 = (f32[96,640]{1,0:T(8,128)S(1)}, f32[80,640]{1,0:T(8,128)S(1)}, f32[80,640]{1,0:T(8,128)S(1)}) custom-call(f32[256,640]{1,0:T(8,128)} %collective-permute-done.5.refs_0_, bf16[2,640,640]{2,1,0:T(8,128)(2,1)S(1)} %get-tuple-element.83.refs_2_.refs_1_, bf16[2,640,640]{2,1,0:T(8,128)(2,1)S(1)} %get-tuple-element.84.refs_3_.refs_2_), custom_call_target="tpu_custom_call" | custom-call | flops 1 | bytes 1 | tf_op jit(solution)/shard_map/project/pallas_call | solution.py:204
  68.9 2.2 %project.8.kept_ref = f32[256,640]{1,0:T(8,128)S(1)} custom-call(f32[256,640]{1,0:T(8,128)} %collective-permute-done.5.refs_0_, bf16[2,640,640]{2,1,0:T(8,128)(2,1)S(1)} %get-tuple-element.83.refs_2_.refs_1_, bf16[2,640,640]{2,1,0:T(8,128)(2,1)S(1)} %get-tuple-element.84.refs_3_.refs_2_), custom_call_target="tpu_custom_call" | custom-call | flops 1 | bytes 1 | tf_op jit(solution)/shard_map/project/pallas_call | solution.py:204
  74.7 1.6 %collective-permute-start.16 = (f32[2,32,640]{2,1,0:T(8,128)S(1)}, f32[2,32,640]{2,1,0:T(8,128)S(1)}, u32[]{:S(2)}, u32[]{:S(2)}) collective-permute-start(f32[2,32,640]{2,1,0:T(8,128)S(1)} %slice_bitcast_fusion.1), channel_id=1, source_target_pairs={{0,8},{8,0},{16,24},{24,16},{1,9},{9,1},{17,25},{25,17},{2,10},{10... | collective-permute-start | bytes 491528 | tf_op jit(solution)/shard_map/ppermute | solution.py:298
  76.2 4.8 %collective-permute-done.20.refs_0_ = f32[256,640]{1,0:T(8,128)S(1)} collective-permute-done((f32[256,640]{1,0:T(8,128)S(1)}, f32[256,640]{1,0:T(8,128)S(1)}, u32[]{:S(2)}, u32[]{:S(2)}) %collective-permute-start.20) | collective-permute-done | bytes 655392 | tf_op jit(solution)/shard_map/ppermute | solution.py:289
  86.5 1.6 %collective-permute-start.28 = (f32[2,1,32,640]{3,2,1,0:T(8,128)S(1)}, f32[2,1,32,640]{3,2,1,0:T(8,128)S(1)}, u32[]{:S(2)}, u32[]{:S(2)}) collective-permute-start(f32[2,1,32,640]{3,2,1,0:T(8,128)S(1)} %get-tuple-element.119), channel_id=1, source_target_pairs={{0,8},{8,0},{16,24},{24,16},{1,9},{9,1},{17,25},{25,17},{2,10},{10... | collective-permute-start | bytes 491528 | tf_op jit(solution)/shard_map/ppermute | solution.py:298
  89.5 1.9 %collective-permute-start.27 = (f32[64,640]{1,0:T(8,128)S(1)}, f32[64,640]{1,0:T(8,128)S(1)}, u32[]{:S(2)}, u32[]{:S(2)}) collective-permute-start(f32[64,640]{1,0:T(8,128)S(1)} %get-tuple-element.131), channel_id=1, source_target_pairs={{0,1},{2,0},{3,2},{1,3},{4,5},{6,4},{7,6},{5,7},{8,9},{10,8},{11,1... | collective-permute-start | bytes 491528 | tf_op jit(solution)/shard_map/ppermute | solution.py:289
  94.9 2.3 %collective-permute-done.29 = f32[1,32,640]{2,1,0:T(8,128)S(1)} collective-permute-done((f32[1,32,640]{2,1,0:T(8,128)S(1)}, f32[1,32,640]{2,1,0:T(8,128)S(1)}, u32[]{:S(2)}, u32[]{:S(2)}) %collective-permute-start.29) | collective-permute-done | bytes 81952 | tf_op jit(solution)/shard_map/ppermute | solution.py:298
  97.2 1.4 %collective-permute-done.31 = f32[1,32,640]{2,1,0:T(8,128)S(1)} collective-permute-done((f32[1,32,640]{2,1,0:T(8,128)S(1)}, f32[1,32,640]{2,1,0:T(8,128)S(1)}, u32[]{:S(2)}, u32[]{:S(2)}) %collective-permute-start.31) | collective-permute-done | bytes 81952 | tf_op jit(solution)/shard_map/ppermute | solution.py:298
  98.6 4.0 %collective-permute-start.32 = (f32[64,640]{1,0:T(8,128)S(1)}, f32[64,640]{1,0:T(8,128)S(1)}, u32[]{:S(2)}, u32[]{:S(2)}) collective-permute-start(f32[64,640]{1,0:T(8,128)S(1)} %maximum_bitcast_fusion), channel_id=1, source_target_pairs={{0,3},{2,1},{3,0},{1,2},{4,7},{6,5},{7,4},{5,6},{8,11},{10,9},{11,... | collective-permute-start | bytes 491528 | tf_op jit(solution)/shard_map/ppermute | solution.py:289
  102.7 3.3 %collective-permute-done.32.refs_2_ = f32[64,640]{1,0:T(8,128)S(1)} collective-permute-done((f32[64,640]{1,0:T(8,128)S(1)}, f32[64,640]{1,0:T(8,128)S(1)}, u32[]{:S(2)}, u32[]{:S(2)}) %collective-permute-start.32) | collective-permute-done | bytes 163872 | tf_op jit(solution)/shard_map/ppermute | solution.py:289
  106.0 1.6 %assemble.1 = f32[64,2560]{1,0:T(8,128)} custom-call(s32[4]{0:T(128)S(1)} %pad_add_fusion.meta_ref, f32[64,640]{1,0:T(8,128)S(1)} %get-tuple-element.132.refs_0_, f32[64,640]{1,0:T(8,128)S(1)} %collective-permute-done.27.refs_1_, f32[64,640]{1,0:T(8,128)S(1)} %collective-permute-done.32.refs_2_, f32[64,640]{1,0:T(8,128)S(1)} %collective-permute-done.33.refs_3_), custom_call_target="tpu_custom_call" | custom-call | flops 1 | bytes 1 | tf_op jit(solution)/shard_map/assemble/pallas_call | solution.py:266
  (100 shorter events, 20.4 us)
Async XLA Ops:
  1.5 15.1 %collective-permute-start.2 = (f32[2,256,128]{2,1,0:T(8,128)S(1)}, f32[2,256,128]{2,1,0:T(8,128)S(1)}, u32[]{:S(2)}, u32[]{:S(2)}) collective-permute-start(f32[2,256,128]{2,1,0:T(8,128)S(1)} %pad_maximum_fusion.refs_0_), channel_id=1, source_target_pairs={{0,1},{2,0},{3,2},{1,3},{4,5},{6,4},{7,6},{5,7},{8,9},{10,8},{11,1... | collective-permute-start | bytes 786440 | tf_op jit(solution)/shard_map/ppermute | solution.py:289
  4.6 15.4 %collective-permute-start.1 = (f32[2,256,128]{2,1,0:T(8,128)S(1)}, f32[2,256,128]{2,1,0:T(8,128)S(1)}, u32[]{:S(2)}, u32[]{:S(2)}) collective-permute-start(f32[2,256,128]{2,1,0:T(8,128)S(1)} %pad_maximum_fusion.refs_0_), channel_id=1, source_target_pairs={{0,3},{2,1},{3,0},{1,2},{4,7},{6,5},{7,4},{5,6},{8,11},{10,9},{11,... | collective-permute-start | bytes 786440 | tf_op jit(solution)/shard_map/ppermute | solution.py:289
  7.1 16.1 %collective-permute-start = (f32[2,256,128]{2,1,0:T(8,128)S(1)}, f32[2,256,128]{2,1,0:T(8,128)S(1)}, u32[]{:S(2)}, u32[]{:S(2)}) collective-permute-start(f32[2,256,128]{2,1,0:T(8,128)S(1)} %pad_maximum_fusion.refs_0_), channel_id=1, source_target_pairs={{0,2},{2,3},{3,1},{1,0},{4,6},{6,7},{7,5},{5,4},{8,10},{10,11},{11... | collective-permute-start | bytes 786440 | tf_op jit(solution)/shard_map/ppermute | solution.py:289
  12.3 39.1 %collective-permute-start.8 = (f32[320,640]{1,0:T(8,128)}, f32[320,640]{1,0:T(8,128)}, u32[]{:S(2)}, u32[]{:S(2)}) collective-permute-start(f32[320,640]{1,0:T(8,128)} %get-tuple-element.127), channel_id=1, source_target_pairs={{0,24},{8,16},{16,8},{24,0},{1,25},{9,17},{17,9},{25,1},{2,26},{10... | collective-permute-start | bytes 2457608 | tf_op jit(solution)/shard_map/ppermute | solution.py:298
  14.8 36.6 %collective-permute-start.6 = (f32[320,640]{1,0:T(8,128)}, f32[320,640]{1,0:T(8,128)}, u32[]{:S(2)}, u32[]{:S(2)}) collective-permute-start(f32[320,640]{1,0:T(8,128)} %get-tuple-element.128), channel_id=1, source_target_pairs={{0,8},{8,0},{16,24},{24,16},{1,9},{9,1},{17,25},{25,17},{2,10},{10... | collective-permute-start | bytes 2457608 | tf_op jit(solution)/shard_map/ppermute | solution.py:298
  16.6 34.8 %collective-permute-start.7 = (f32[320,640]{1,0:T(8,128)}, f32[320,640]{1,0:T(8,128)}, u32[]{:S(2)}, u32[]{:S(2)}) collective-permute-start(f32[320,640]{1,0:T(8,128)} %get-tuple-element.130), channel_id=1, source_target_pairs={{0,16},{8,24},{16,0},{24,8},{1,17},{9,25},{17,1},{25,9},{2,18},{10... | collective-permute-start | bytes 2457608 | tf_op jit(solution)/shard_map/ppermute | solution.py:298
  23.1 21.7 %collective-permute-start.4 = (f32[3,256,128]{2,1,0:T(8,128)S(1)}, f32[3,256,128]{2,1,0:T(8,128)}, u32[]{:S(2)}, u32[]{:S(2)}) collective-permute-start(f32[3,256,128]{2,1,0:T(8,128)S(1)} %slice.65.refs_1_), channel_id=1, source_target_pairs={{0,2},{2,3},{3,1},{1,0},{4,6},{6,7},{7,5},{5,4},{8,10},{10,11},{11... | collective-permute-start | bytes 1179656 | tf_op jit(solution)/shard_map/ppermute | solution.py:289
  31.6 13.2 %collective-permute-start.3 = (f32[2,256,128]{2,1,0:T(8,128)S(1)}, f32[2,256,128]{2,1,0:T(8,128)S(1)}, u32[]{:S(2)}, u32[]{:S(2)}) collective-permute-start(f32[2,256,128]{2,1,0:T(8,128)S(1)} %slice.64.refs_0_), channel_id=1, source_target_pairs={{0,2},{2,3},{3,1},{1,0},{4,6},{6,7},{7,5},{5,4},{8,10},{10,11},{11... | collective-permute-start | bytes 786440 | tf_op jit(solution)/shard_map/ppermute | solution.py:289
  44.9 16.7 %collective-permute-start.5 = (f32[256,640]{1,0:T(8,128)}, f32[256,640]{1,0:T(8,128)}, u32[]{:S(2)}, u32[]{:S(2)}) collective-permute-start(f32[256,640]{1,0:T(8,128)} %attend.2.refs_0_), channel_id=1, source_target_pairs={{0,1},{2,0},{3,2},{1,3},{4,5},{6,4},{7,6},{5,7},{8,9},{10,8},{11,1... | collective-permute-start | bytes 1966088 | tf_op jit(solution)/shard_map/ppermute | solution.py:289
  56.8 3.0 %collective-permute-start.9 = (f32[128,640]{1,0:T(8,128)S(1)}, f32[128,640]{1,0:T(8,128)S(1)}, u32[]{:S(2)}, u32[]{:S(2)}) collective-permute-start(f32[128,640]{1,0:T(8,128)S(1)} %get-tuple-element.85), channel_id=1, source_target_pairs={{0,4},{4,0},{1,5},{5,1},{2,6},{6,2},{3,7},{7,3},{8,12},{12,8},{9,1... | collective-permute-start | bytes 983048 | tf_op jit(solution)/shard_map/ppermute | solution.py:290
  56.9 3.0 %collective-permute-start.10 = (f32[128,640]{1,0:T(8,128)S(1)}, f32[128,640]{1,0:T(8,128)S(1)}, u32[]{:S(2)}, u32[]{:S(2)}) collective-permute-start(f32[128,640]{1,0:T(8,128)S(1)} %get-tuple-element.86), channel_id=1, source_target_pairs={{0,4},{4,0},{1,5},{5,1},{2,6},{6,2},{3,7},{7,3},{8,12},{12,8},{9,1... | collective-permute-start | bytes 983048 | tf_op jit(solution)/shard_map/ppermute | solution.py:290
  57.4 2.5 %collective-permute-start.11 = (f32[128,640]{1,0:T(8,128)S(1)}, f32[128,640]{1,0:T(8,128)S(1)}, u32[]{:S(2)}, u32[]{:S(2)}) collective-permute-start(f32[128,640]{1,0:T(8,128)S(1)} %get-tuple-element.87), channel_id=1, source_target_pairs={{0,4},{4,0},{1,5},{5,1},{2,6},{6,2},{3,7},{7,3},{8,12},{12,8},{9,1... | collective-permute-start | bytes 983048 | tf_op jit(solution)/shard_map/ppermute | solution.py:290
  57.5 2.4 %collective-permute-start.12 = (f32[128,640]{1,0:T(8,128)S(1)}, f32[128,640]{1,0:T(8,128)S(1)}, u32[]{:S(2)}, u32[]{:S(2)}) collective-permute-start(f32[128,640]{1,0:T(8,128)S(1)} %get-tuple-element.88), channel_id=1, source_target_pairs={{0,4},{4,0},{1,5},{5,1},{2,6},{6,2},{3,7},{7,3},{8,12},{12,8},{9,1... | collective-permute-start | bytes 983048 | tf_op jit(solution)/shard_map/ppermute | solution.py:290
  61.8 9.8 %collective-permute-start.13 = (f32[2,2,32,640]{3,2,1,0:T(8,128)S(1)}, f32[2,2,32,640]{3,2,1,0:T(8,128)S(1)}, u32[]{:S(2)}, u32[]{:S(2)}) collective-permute-start(f32[2,2,32,640]{3,2,1,0:T(8,128)S(1)} %get-tuple-element.101), channel_id=1, source_target_pairs={{0,8},{8,0},{16,24},{24,16},{1,9},{9,1},{17,25},{25,17},{2,10},{10... | collective-permute-start | bytes 983048 | tf_op jit(solution)/shard_map/ppermute | solution.py:298
  63.4 8.3 %collective-permute-start.14 = (f32[2,2,32,640]{3,2,1,0:T(8,128)S(1)}, f32[2,2,32,640]{3,2,1,0:T(8,128)S(1)}, u32[]{:S(2)}, u32[]{:S(2)}) collective-permute-start(f32[2,2,32,640]{3,2,1,0:T(8,128)S(1)} %get-tuple-element.102), channel_id=1, source_target_pairs={{0,16},{8,24},{16,0},{24,8},{1,17},{9,25},{17,1},{25,9},{2,18},{10... | collective-permute-start | bytes 983048 | tf_op jit(solution)/shard_map/ppermute | solution.py:298
  64.9 16.1 %collective-permute-start.20 = (f32[256,640]{1,0:T(8,128)S(1)}, f32[256,640]{1,0:T(8,128)S(1)}, u32[]{:S(2)}, u32[]{:S(2)}) collective-permute-start(f32[256,640]{1,0:T(8,128)S(1)} %copy-done.1), channel_id=1, source_target_pairs={{0,2},{2,3},{3,1},{1,0},{4,6},{6,7},{7,5},{5,4},{8,10},{10,11},{11... | collective-permute-start | bytes 1966088 | tf_op jit(solution)/shard_map/ppermute | solution.py:289
  68.8 4.3 %collective-permute-start.17 = (f32[96,640]{1,0:T(8,128)S(1)}, f32[96,640]{1,0:T(8,128)S(1)}, u32[]{:S(2)}, u32[]{:S(2)}) collective-permute-start(f32[96,640]{1,0:T(8,128)S(1)} %get-tuple-element.107), channel_id=1, source_target_pairs={{0,4},{4,0},{1,5},{5,1},{2,6},{6,2},{3,7},{7,3},{8,12},{12,8},{9,1... | collective-permute-start | bytes 737288 | tf_op jit(solution)/shard_map/ppermute | solution.py:290
  71.8 16.2 %collective-permute-start.15 = (f32[2,32,640]{2,1,0:T(8,128)S(1)}, f32[2,32,640]{2,1,0:T(8,128)S(1)}, u32[]{:S(2)}, u32[]{:S(2)}) collective-permute-start(f32[2,32,640]{2,1,0:T(8,128)S(1)} %slice_bitcast_fusion.2), channel_id=1, source_target_pairs={{0,16},{8,24},{16,0},{24,8},{1,17},{9,25},{17,1},{25,9},{2,18},{10... | collective-permute-start | bytes 491528 | tf_op jit(solution)/shard_map/ppermute | solution.py:298
  73.2 7.8 %collective-permute-start.21 = (f32[2,1,32,640]{3,2,1,0:T(8,128)S(1)}, f32[2,1,32,640]{3,2,1,0:T(8,128)S(1)}, u32[]{:S(2)}, u32[]{:S(2)}) collective-permute-start(f32[2,1,32,640]{3,2,1,0:T(8,128)S(1)} %get-tuple-element.111), channel_id=1, source_target_pairs={{0,8},{8,0},{16,24},{24,16},{1,9},{9,1},{17,25},{25,17},{2,10},{10... | collective-permute-start | bytes 491528 | tf_op jit(solution)/shard_map/ppermute | solution.py:298
  73.8 8.1 %collective-permute-start.22 = (f32[2,1,32,640]{3,2,1,0:T(8,128)S(1)}, f32[2,1,32,640]{3,2,1,0:T(8,128)S(1)}, u32[]{:S(2)}, u32[]{:S(2)}) collective-permute-start(f32[2,1,32,640]{3,2,1,0:T(8,128)S(1)} %get-tuple-element.112), channel_id=1, source_target_pairs={{0,16},{8,24},{16,0},{24,8},{1,17},{9,25},{17,1},{25,9},{2,18},{10... | collective-permute-start | bytes 491528 | tf_op jit(solution)/shard_map/ppermute | solution.py:298
  74.7 14.4 %collective-permute-start.16 = (f32[2,32,640]{2,1,0:T(8,128)S(1)}, f32[2,32,640]{2,1,0:T(8,128)S(1)}, u32[]{:S(2)}, u32[]{:S(2)}) collective-permute-start(f32[2,32,640]{2,1,0:T(8,128)S(1)} %slice_bitcast_fusion.1), channel_id=1, source_target_pairs={{0,8},{8,0},{16,24},{24,16},{1,9},{9,1},{17,25},{25,17},{2,10},{10... | collective-permute-start | bytes 491528 | tf_op jit(solution)/shard_map/ppermute | solution.py:298
  83.0 1.7 %collective-permute-start.25 = (f32[128,640]{1,0:T(8,128)S(1)}, f32[128,640]{1,0:T(8,128)S(1)}, u32[]{:S(2)}, u32[]{:S(2)}) collective-permute-start(f32[128,640]{1,0:T(8,128)S(1)} %get-tuple-element.117), channel_id=1, source_target_pairs={{0,4},{4,0},{1,5},{5,1},{2,6},{6,2},{3,7},{7,3},{8,12},{12,8},{9,1... | collective-permute-start | bytes 983048 | tf_op jit(solution)/shard_map/ppermute | solution.py:290
  83.1 3.2 %collective-permute-start.26 = (f32[128,640]{1,0:T(8,128)S(1)}, f32[128,640]{1,0:T(8,128)S(1)}, u32[]{:S(2)}, u32[]{:S(2)}) collective-permute-start(f32[128,640]{1,0:T(8,128)S(1)} %get-tuple-element.118), channel_id=1, source_target_pairs={{0,4},{4,0},{1,5},{5,1},{2,6},{6,2},{3,7},{7,3},{8,12},{12,8},{9,1... | collective-permute-start | bytes 983048 | tf_op jit(solution)/shard_map/ppermute | solution.py:290
  83.7 5.4 %collective-permute-start.23 = (f32[1,32,640]{2,1,0:T(8,128)S(1)}, f32[1,32,640]{2,1,0:T(8,128)S(1)}, u32[]{:S(2)}, u32[]{:S(2)}) collective-permute-start(f32[1,32,640]{2,1,0:T(8,128)S(1)} %slice_bitcast_fusion.11), channel_id=1, source_target_pairs={{0,16},{8,24},{16,0},{24,8},{1,17},{9,25},{17,1},{25,9},{2,18},{10... | collective-permute-start | bytes 245768 | tf_op jit(solution)/shard_map/ppermute | solution.py:298
  84.7 4.7 %collective-permute-start.24 = (f32[1,32,640]{2,1,0:T(8,128)S(1)}, f32[1,32,640]{2,1,0:T(8,128)S(1)}, u32[]{:S(2)}, u32[]{:S(2)}) collective-permute-start(f32[1,32,640]{2,1,0:T(8,128)S(1)} %slice_bitcast_fusion.10), channel_id=1, source_target_pairs={{0,8},{8,0},{16,24},{24,16},{1,9},{9,1},{17,25},{25,17},{2,10},{10... | collective-permute-start | bytes 245768 | tf_op jit(solution)/shard_map/ppermute | solution.py:298
  86.5 6.2 %collective-permute-start.28 = (f32[2,1,32,640]{3,2,1,0:T(8,128)S(1)}, f32[2,1,32,640]{3,2,1,0:T(8,128)S(1)}, u32[]{:S(2)}, u32[]{:S(2)}) collective-permute-start(f32[2,1,32,640]{3,2,1,0:T(8,128)S(1)} %get-tuple-element.119), channel_id=1, source_target_pairs={{0,8},{8,0},{16,24},{24,16},{1,9},{9,1},{17,25},{25,17},{2,10},{10... | collective-permute-start | bytes 491528 | tf_op jit(solution)/shard_map/ppermute | solution.py:298
  88.0 6.0 %collective-permute-start.30 = (f32[2,1,32,640]{3,2,1,0:T(8,128)S(1)}, f32[2,1,32,640]{3,2,1,0:T(8,128)S(1)}, u32[]{:S(2)}, u32[]{:S(2)}) collective-permute-start(f32[2,1,32,640]{3,2,1,0:T(8,128)S(1)} %get-tuple-element.120), channel_id=1, source_target_pairs={{0,16},{8,24},{16,0},{24,8},{1,17},{9,25},{17,1},{25,9},{2,18},{10... | collective-permute-start | bytes 491528 | tf_op jit(solution)/shard_map/ppermute | solution.py:298
  89.5 13.1 %collective-permute-start.27 = (f32[64,640]{1,0:T(8,128)S(1)}, f32[64,640]{1,0:T(8,128)S(1)}, u32[]{:S(2)}, u32[]{:S(2)}) collective-permute-start(f32[64,640]{1,0:T(8,128)S(1)} %get-tuple-element.131), channel_id=1, source_target_pairs={{0,1},{2,0},{3,2},{1,3},{4,5},{6,4},{7,6},{5,7},{8,9},{10,8},{11,1... | collective-permute-start | bytes 491528 | tf_op jit(solution)/shard_map/ppermute | solution.py:289
  91.5 11.2 %collective-permute-start.33 = (f32[64,640]{1,0:T(8,128)S(1)}, f32[64,640]{1,0:T(8,128)S(1)}, u32[]{:S(2)}, u32[]{:S(2)}) collective-permute-start(f32[64,640]{1,0:T(8,128)S(1)} %maximum_bitcast_fusion.1), channel_id=1, source_target_pairs={{0,2},{2,3},{3,1},{1,0},{4,6},{6,7},{7,5},{5,4},{8,10},{10,11},{11... | collective-permute-start | bytes 491528 | tf_op jit(solution)/shard_map/ppermute | solution.py:289
  92.7 4.5 %collective-permute-start.29 = (f32[1,32,640]{2,1,0:T(8,128)S(1)}, f32[1,32,640]{2,1,0:T(8,128)S(1)}, u32[]{:S(2)}, u32[]{:S(2)}) collective-permute-start(f32[1,32,640]{2,1,0:T(8,128)S(1)} %slice_bitcast_fusion.8), channel_id=1, source_target_pairs={{0,16},{8,24},{16,0},{24,8},{1,17},{9,25},{17,1},{25,9},{2,18},{10... | collective-permute-start | bytes 245768 | tf_op jit(solution)/shard_map/ppermute | solution.py:298
  94.1 4.5 %collective-permute-start.31 = (f32[1,32,640]{2,1,0:T(8,128)S(1)}, f32[1,32,640]{2,1,0:T(8,128)S(1)}, u32[]{:S(2)}, u32[]{:S(2)}) collective-permute-start(f32[1,32,640]{2,1,0:T(8,128)S(1)} %slice_bitcast_fusion.6), channel_id=1, source_target_pairs={{0,8},{8,0},{16,24},{24,16},{1,9},{9,1},{17,25},{25,17},{2,10},{10... | collective-permute-start | bytes 245768 | tf_op jit(solution)/shard_map/ppermute | solution.py:298
  98.6 7.4 %collective-permute-start.32 = (f32[64,640]{1,0:T(8,128)S(1)}, f32[64,640]{1,0:T(8,128)S(1)}, u32[]{:S(2)}, u32[]{:S(2)}) collective-permute-start(f32[64,640]{1,0:T(8,128)S(1)} %maximum_bitcast_fusion), channel_id=1, source_target_pairs={{0,3},{2,1},{3,0},{1,2},{4,7},{6,5},{7,4},{5,6},{8,11},{10,9},{11,... | collective-permute-start | bytes 491528 | tf_op jit(solution)/shard_map/ppermute | solution.py:289
  (12 other events, 92.3 us)

commit v6 on v5

--- a/solution.py
+++ b/solution.py
@@ -186,32 +186,54 @@
     )(meta, *pieces)
 
 
-def project(blocks, high, low, half, chunks):
+def share(a_high, a_low, high_ref, low_ref, half):
+    dot = functools.partial(lax.dot_general, dimension_numbers=NT, preferred_element_type=F32)
+    w_high = high_ref[half]
+    return dot(a_high, w_high) + dot(a_low, w_high) + dot(a_high, low_ref[half])
+
+
+def project_given(blocks, high, low, chunks):
     n = len(blocks)
-    rows = n * blocks[0].shape[0]
+    rows, k = n * blocks[0].shape[0], blocks[0].shape[1]
     columns = high.shape[1]
     ends = [-(-rows * i // (16 * chunks)) * 16 for i in range(chunks + 1)]
 
     def kernel(*refs):
         high_ref, low_ref = refs[n : n + 2]
+        *given, a_high_ref, a_low_ref = refs[n + 2 :]
         a_high, a_low = split(jnp.concatenate([ref[...] for ref in refs[:n]], axis=0))
-        dot = functools.partial(lax.dot_general, dimension_numbers=NT, preferred_element_type=F32)
-        w_high = high_ref[half]
-        total = dot(a_high, w_high) + dot(a_low, w_high) + dot(a_high, low_ref[half])
-        for i, ref in enumerate(refs[n + 2 :]):
+        a_high_ref[...], a_low_ref[...] = a_high, a_low
+        total = share(a_high, a_low, high_ref, low_ref, 1)
+        for i, ref in enumerate(given):
             ref[...] = total[ends[i] : ends[i + 1]]
 
     return pl.pallas_call(
         kernel,
         out_shape=tuple(
             jax.ShapeDtypeStruct((b - a, columns), F32) for a, b in zip(ends, ends[1:])
-        ),
+        )
+        + (jax.ShapeDtypeStruct((rows, k), BF16),) * 2,
         in_specs=vmem(n + 2),
-        out_specs=tuple(vmem(chunks)),
+        out_specs=tuple(vmem(chunks + 2)),
         compiler_params=params(),
         cost_estimate=brief(),
-        name="project",
+        name="project_given",
     )(*blocks, high, low)
+
+
+def project_kept(a_high, a_low, high, low):
+    def kernel(a_high_ref, a_low_ref, high_ref, low_ref, out):
+        out[...] = share(a_high_ref[...], a_low_ref[...], high_ref, low_ref, 0)
+
+    return pl.pallas_call(
+        kernel,
+        out_shape=jax.ShapeDtypeStruct((a_high.shape[0], high.shape[1]), F32),
+        in_specs=vmem(4),
+        out_specs=vmem(1)[0],
+        compiler_params=params(),
+        cost_estimate=brief(),
+        name="project_kept",
+    )(a_high, a_low, high, low)
 
 
 def fold(meta, kept, got, blocks, parts, orders):
@@ -317,8 +339,9 @@
 
     exchange = lambda xs: [swap(x) for x in xs]
     both = [owns[0], owns[1]]
-    given = exchange(project(both, high, low, 1, 4))
-    (kept,) = project(both, high, low, 0, 1)
+    *given, a_high, a_low = project_given(both, high, low, 4)
+    given = exchange(given)
+    kept = project_kept(a_high, a_low, high, low)
     owns[3], *given = after(owns[3], *given)
     orders = ((0, (0, 2)), (1, (0, 1)), (0, (1, 3)), (1, (2, 3)))
     add = lambda xs, ys: [x + y for x, y in zip(xs, ys)]
@@ -328,16 +351,18 @@
     *keep_a, up, down = fold(place, kept, given, 2, parts, orders)
     owns[3], up, down, *keep_a = after(owns[3], up, down, *keep_a)
     got_a = first([up, down])
-    given = exchange(project([owns[3]], high, low, 1, 3))
-    (kept,) = project([owns[3]], high, low, 0, 1)
+    *given, a_high, a_low = project_given([owns[3]], high, low, 2)
+    given = exchange(given)
+    kept = project_kept(a_high, a_low, high, low)
     kept, *got_a = after(kept, *got_a)
     keep_a = add(keep_a, got_a)
     *keep_b, up, down = fold(place, kept, given, 1, parts, orders)
     got_b = first([up, down])
     owns[2], *got_b = after(owns[2], *got_b)
     keep_b = add(keep_b, got_b)
-    given = exchange(project([owns[2]], high, low, 1, 2))
-    (kept,) = project([owns[2]], high, low, 0, 1)
+    *given, a_high, a_low = project_given([owns[2]], high, low, 2)
+    given = exchange(given)
+    kept = project_kept(a_high, a_low, high, low)
     *keep_c, up, down = fold(place, kept, given, 1, parts, orders)
     got_a = second(keep_a)
     got_b = second(keep_b)
@@ -389,8 +414,8 @@
     out_specs = P(("seq", "feature"), "kvhead")
 
     def local(queries, keys, values, w_out):
-        parts, groups = mesh.shape["feature"], mesh.shape["kvhead"]
-        body = by_heads if (groups, parts, keys.shape[1]) == (2, 4, parts) else plain
+        sizes = tuple(mesh.shape[a] for a in ("feature", "kvhead", "seq"))
+        body = by_heads if sizes == (4, 2, 4) and keys.shape[1] == 4 else plain
         return body(queries, keys, values, w_out)
 
     return jax.shard_map(local, mesh=mesh, in_specs=in_specs, out_specs=out_specs, check_vma=False)

time: 108 us -> 107 us (level)
  starting transfers between devices: 45.3 us -> 44 us
  waiting for transfers between devices: 27.2 us -> 28.4 us
    ppermute x10, waiting for transfers between devices: 21.2 us -> 23.3 us  [by_heads(): ring = lambda x, step: lax.ppermute(x, 'seq', ring_perm(planes, step))]
    ppermute x10, starting transfers between devices: 26.6 us -> 25.1 us  [by_heads(): ring = lambda x, step: lax.ppermute(x, 'seq', ring_perm(planes, step))]
    pallas_call x6, Pallas kernels: 10.4 us -> 9.28 us  [the longest x3 5.2 us: project_given(): pl.pallas_call(kernel, out_shape=tuple((jax.ShapeDtypeStruct((b - a, colu...]
    ppermute x9 -> x8, starting transfers between devices: 2.36 us -> 2.21 us  [by_heads(): swap = lambda x: lax.ppermute(x, 'kvhead', [(0, 1), (1, 0)])]
  transfers between devices with their start and end apart: 34 -> 33, of which waited for: 13 -> 12; matrix products, arithmetic and copies ran while one was open for 6% -> 7% of each run, Pallas kernels for 22% -> 22%
where the time goes in v6:
time: 107 us
  starting transfers between devices  44 us (41%)
  waiting for transfers between devices  28.4 us (27%)
  Pallas kernels  24.9 us (23%)
  local copies, waits for them, and re-layouts  8.34 us (8%)
    ppermute x10, starting transfers between devices, by_heads(): ring = lambda x, step: lax.ppermute(x, 'seq', ring_perm(planes, step))  25.1 us
    ppermute x10, waiting for transfers between devices, by_heads(): ring = lambda x, step: lax.ppermute(x, 'seq', ring_perm(planes, step))  23.3 us
    ppermute x15, starting transfers between devices, by_heads(): lax.ppermute(x, 'feature', [(i, i ^ e) for i in range(parts)])  16.6 us
    pallas_call x2, Pallas kernels, attend(): pl.pallas_call(kernel, out_shape=jax.ShapeDtypeStruct((rows, group * d),...  8.61 us
    pallas_call x3, Pallas kernels, project_given(): pl.pallas_call(kernel, out_shape=tuple((jax.ShapeDtypeStruct((b - a, colu...  5.2 us
    ppermute x15, waiting for transfers between devices, by_heads(): lax.ppermute(x, 'feature', [(i, i ^ e) for i in range(parts)])  4.63 us
    pallas_call x3, Pallas kernels, project_kept(): pl.pallas_call(kernel, out_shape=jax.ShapeDtypeStruct((a_high.shape[0], h...  4.08 us
    transpose x1, local copies, waits for them, and re-layouts, by_heads(): turn = lambda x: lax.dynamic_slice_in_dim(w_out, x * k_rows, k_rows, 0).T  3.37 us
  transfers between devices with their start and end apart: 33, of which 12 were waited for; matrix products, arithmetic and copies ran while one was open for 7% of the time, Pallas kernels for 22%

profile of v6, /device:TPU:0, one launch (start us, length us, event | category | flops | bytes accessed | tf_op | source)
XLA Modules:
  0.0 107.0 jit_solution(13344284435320370871)
XLA Ops:
  0.0 1.5 %constant_dynamic-slice_fusion = (f32[256,1,128]{2,1,0:T(1,128)S(1)}, f32[256,1,128]{2,1,0:T(1,128)S(1)}) fusion(f32[256,4,128]{2,1,0:T(4,128)} %param.6, s32[]{:T(128)S(6)} %select_n.139, f32[256,4,128]{2,1,0:T(4,128)} %param.5), kind=kLoop, calls=%fused_computation.32 | loop fusion | bytes 524292 | tf_op jit(solution)/shard_map/jit(dynamic_index_in_dim)/dynamic_slice | solution.py:314
  1.5 3.1 %collective-permute-start.2 = (f32[2,256,128]{2,1,0:T(8,128)S(1)}, f32[2,256,128]{2,1,0:T(8,128)S(1)}, u32[]{:S(2)}, u32[]{:S(2)}) collective-permute-start(f32[2,256,128]{2,1,0:T(8,128)S(1)} %pad_maximum_fusion.refs_0_), channel_id=1, source_target_pairs={{0,1},{2,0},{3,2},{1,3},{4,5},{6,4},{7,6},{5,7},{8,9},{10,8},{11,1... | collective-permute-start | bytes 786440 | tf_op jit(solution)/shard_map/ppermute | solution.py:311
  4.6 2.5 %collective-permute-start.1 = (f32[2,256,128]{2,1,0:T(8,128)S(1)}, f32[2,256,128]{2,1,0:T(8,128)S(1)}, u32[]{:S(2)}, u32[]{:S(2)}) collective-permute-start(f32[2,256,128]{2,1,0:T(8,128)S(1)} %pad_maximum_fusion.refs_0_), channel_id=1, source_target_pairs={{0,3},{2,1},{3,0},{1,2},{4,7},{6,5},{7,4},{5,6},{8,11},{10,9},{11,... | collective-permute-start | bytes 786440 | tf_op jit(solution)/shard_map/ppermute | solution.py:311
  7.1 1.6 %collective-permute-start = (f32[2,256,128]{2,1,0:T(8,128)S(1)}, f32[2,256,128]{2,1,0:T(8,128)S(1)}, u32[]{:S(2)}, u32[]{:S(2)}) collective-permute-start(f32[2,256,128]{2,1,0:T(8,128)S(1)} %pad_maximum_fusion.refs_0_), channel_id=1, source_target_pairs={{0,2},{2,3},{3,1},{1,0},{4,6},{6,7},{7,5},{5,4},{8,10},{10,11},{11... | collective-permute-start | bytes 786440 | tf_op jit(solution)/shard_map/ppermute | solution.py:311
  8.6 3.4 %dynamic-slice_bitcast_fusion = (f32[320,640]{1,0:T(8,128)}, f32[320,640]{1,0:T(8,128)}, f32[320,640]{1,0:T(8,128)S(1)}, f32[320,640]{1,0:T(8,128)}) fusion(f32[2560,320]{0,1:T(8,128)} %param.7, s32[]{:T(128)S(6)} %select_n.150, s32[]{:T(128)S(6)} %select_n.148, s32[]{:T(128)S(6)} %select_n.140, s32[]{:T(128)S(6)} %select_n.149), kind=kLoop, calls=%fused_computation | loop fusion | bytes 6553616 | tf_op jit(solution)/shard_map/transpose | solution.py:319
  12.0 2.4 %collective-permute-start.8 = (f32[320,640]{1,0:T(8,128)}, f32[320,640]{1,0:T(8,128)}, u32[]{:S(2)}, u32[]{:S(2)}) collective-permute-start(f32[320,640]{1,0:T(8,128)} %get-tuple-element.137), channel_id=1, source_target_pairs={{0,24},{8,16},{16,8},{24,0},{1,25},{9,17},{17,9},{25,1},{2,26},{10... | collective-permute-start | bytes 2457608 | tf_op jit(solution)/shard_map/ppermute | solution.py:320
  20.0 3.2 %collective-permute-done.refs_1_ = f32[2,256,128]{2,1,0:T(8,128)S(1)} collective-permute-done((f32[2,256,128]{2,1,0:T(8,128)S(1)}, f32[2,256,128]{2,1,0:T(8,128)S(1)}, u32[]{:S(2)}, u32[]{:S(2)}) %collective-permute-start) | collective-permute-done | bytes 262176 | tf_op jit(solution)/shard_map/ppermute | solution.py:311
  23.9 8.5 %collective-permute-start.4 = (f32[3,256,128]{2,1,0:T(8,128)}, f32[3,256,128]{2,1,0:T(8,128)}, u32[]{:S(2)}, u32[]{:S(2)}) collective-permute-start(f32[3,256,128]{2,1,0:T(8,128)} %slice.65.refs_1_), channel_id=1, source_target_pairs={{0,2},{2,3},{3,1},{1,0},{4,6},{6,7},{7,5},{5,4},{8,10},{10,11},{11... | collective-permute-start | bytes 1179656 | tf_op jit(solution)/shard_map/ppermute | solution.py:311
  32.4 2.6 %prepare_keys.1 = (bf16[384,1024]{1,0:T(8,128)(2,1)}, bf16[2048,256]{1,0:T(8,128)(2,1)}) custom-call(f32[2,256,128]{2,1,0:T(8,128)} %copy-done.2, f32[2,256,128]{2,1,0:T(8,128)} %copy-done.5, f32[2,256,128]{2,1,0:T(8,128)} %copy-done.4, f32[2,256,128]{2,1,0:T(8,128)} %copy-done.3), custom_call_target="tpu_custom_call" | custom-call | flops 1 | bytes 1 | tf_op jit(solution)/shard_map/prepare_keys/pallas_call | solution.py:83
  35.1 3.7 %attend.2.refs_0_ = f32[256,640]{1,0:T(8,128)} custom-call(s32[4]{0:T(128)} %pad_add_fusion.1.meta_ref, f32[2,256,128]{2,1,0:T(8,128)} %slice.64.refs_0_, f32[3,256,128]{2,1,0:T(8,128)} %slice.65.refs_1_, bf16[384,1024]{1,0:T(8,128)(2,1)} %get-tuple-element.78.refs_2_, bf16[2048,256]{1,0:T(8,128)(2,1)} %get-tuple-element.79.refs_3_), custom_call_target="tpu_custom_call" | custom-call | flops 1 | bytes 1 | tf_op jit(solution)/shard_map/attend/pallas_call | solution.py:144
  38.7 7.2 %collective-permute-done.3.refs_0_ = f32[2,256,128]{2,1,0:T(8,128)} collective-permute-done((f32[2,256,128]{2,1,0:T(8,128)}, f32[2,256,128]{2,1,0:T(8,128)}, u32[]{:S(2)}, u32[]{:S(2)}) %collective-permute-start.3) | collective-permute-done | bytes 262176 | tf_op jit(solution)/shard_map/ppermute | solution.py:311
  45.9 1.5 %collective-permute-start.5 = (f32[256,640]{1,0:T(8,128)}, f32[256,640]{1,0:T(8,128)}, u32[]{:S(2)}, u32[]{:S(2)}) collective-permute-start(f32[256,640]{1,0:T(8,128)} %attend.2.refs_0_), channel_id=1, source_target_pairs={{0,1},{2,0},{3,2},{1,3},{4,5},{6,4},{7,6},{5,7},{8,9},{10,8},{11,1... | collective-permute-start | bytes 1966088 | tf_op jit(solution)/shard_map/ppermute | solution.py:311
  47.5 4.9 %attend.3.refs_1_ = f32[256,640]{1,0:T(8,128)} custom-call(s32[4]{0:T(128)} %pad_add_fusion.1.meta_ref, f32[2,256,128]{2,1,0:T(8,128)} %collective-permute-done.3.refs_0_, f32[3,256,128]{2,1,0:T(8,128)} %collective-permute-done.4.refs_1_, bf16[384,1024]{1,0:T(8,128)(2,1)} %get-tuple-element.78.refs_2_, bf16[2048,256]{1,0:T(8,128)(2,1)} %get-tuple-element.79.refs_3_), custom_call_target="tpu_custom_call" | custom-call | flops 1 | bytes 1 | tf_op jit(solution)/shard_map/attend/pallas_call | solution.py:144
  52.5 2.3 %prepare_weights.1 = (bf16[2,640,640]{2,1,0:T(8,128)(2,1)S(1)}, bf16[2,640,640]{2,1,0:T(8,128)(2,1)S(1)}) custom-call(s32[8]{0:T(128)S(1)} %stack.88.meta_ref, f32[320,640]{1,0:T(8,128)S(1)} %get-tuple-element.84.refs_0_, f32[320,640]{1,0:T(8,128)} %collective-permute-done.6.refs_1_, f32[320,640]{1,0:T(8,128)} %collective-permute-done.7.refs_2_, ...), custom_call_target="tpu_custom_call" | custom-call | flops 1 | bytes 1 | tf_op jit(solution)/shard_map/prepare_weights/pallas_call | solution.py:177
  54.8 1.9 %project_given.3 = (f32[128,640]{1,0:T(8,128)S(1)}, f32[128,640]{1,0:T(8,128)S(1)}, f32[128,640]{1,0:T(8,128)S(1)}, f32[128,640]{1,0:T(8,128)S(1)}, bf16[512,640...) custom-call(f32[256,640]{1,0:T(8,128)S(1)} %copy-done, f32[256,640]{1,0:T(8,128)S(1)} %copy-done.1, ...), custom_call_target="tpu_custom_call" | custom-call | flops 1 | bytes 1 | tf_op jit(solution)/shard_map/project_given/pallas_call | solution.py:210
  57.9 1.9 %project_kept.3.kept_ref = f32[512,640]{1,0:T(8,128)S(1)} custom-call(bf16[512,640]{1,0:T(8,128)(2,1)S(1)} %get-tuple-element.96.a_high_ref, bf16[512,640]{1,0:T(8,128)(2,1)S(1)} %get-tuple-element.97.a_low_ref, bf16[2,640,640]{2,1,0:T(8,128)(2,1)S(1)} %get-tuple-element.88.refs_2_.high_ref.refs_1_, ...), custom_call_target="tpu_custom_call" | custom-call | flops 1 | bytes 1 | tf_op jit(solution)/shard_map/project_kept/pallas_call | solution.py:228
  59.9 2.8 %collective-permute-done.5.refs_0_ = f32[256,640]{1,0:T(8,128)} collective-permute-done((f32[256,640]{1,0:T(8,128)}, f32[256,640]{1,0:T(8,128)}, u32[]{:S(2)}, u32[]{:S(2)}) %collective-permute-start.5) | collective-permute-done | bytes 655392 | tf_op jit(solution)/shard_map/ppermute | solution.py:311
  62.9 1.6 %collective-permute-start.13 = (f32[2,2,32,640]{3,2,1,0:T(8,128)S(1)}, f32[2,2,32,640]{3,2,1,0:T(8,128)S(1)}, u32[]{:S(2)}, u32[]{:S(2)}) collective-permute-start(f32[2,2,32,640]{3,2,1,0:T(8,128)S(1)} %get-tuple-element.110), channel_id=1, source_target_pairs={{0,8},{8,0},{16,24},{24,16},{1,9},{9,1},{17,25},{25,17},{2,10},{10... | collective-permute-start | bytes 983048 | tf_op jit(solution)/shard_map/ppermute | solution.py:320
  64.4 1.5 %collective-permute-start.14 = (f32[2,2,32,640]{3,2,1,0:T(8,128)S(1)}, f32[2,2,32,640]{3,2,1,0:T(8,128)S(1)}, u32[]{:S(2)}, u32[]{:S(2)}) collective-permute-start(f32[2,2,32,640]{3,2,1,0:T(8,128)S(1)} %get-tuple-element.111), channel_id=1, source_target_pairs={{0,16},{8,24},{16,0},{24,8},{1,17},{9,25},{17,1},{25,9},{2,18},{10... | collective-permute-start | bytes 983048 | tf_op jit(solution)/shard_map/ppermute | solution.py:320
  66.0 1.7 %collective-permute-start.19 = (f32[256,640]{1,0:T(8,128)S(1)}, f32[256,640]{1,0:T(8,128)S(1)}, u32[]{:S(2)}, u32[]{:S(2)}) collective-permute-start(f32[256,640]{1,0:T(8,128)S(1)} %copy-done.1), channel_id=1, source_target_pairs={{0,2},{2,3},{3,1},{1,0},{4,6},{6,7},{7,5},{5,4},{8,10},{10,11},{11... | collective-permute-start | bytes 1966088 | tf_op jit(solution)/shard_map/ppermute | solution.py:311
  67.7 2.2 %project_given.4 = (f32[128,640]{1,0:T(8,128)S(1)}, f32[128,640]{1,0:T(8,128)S(1)}, bf16[256,640]{1,0:T(8,128)(2,1)S(1)}, bf16[256,640]{1,0:T(8,128)(2,1)S(1)}) custom-call(f32[256,640]{1,0:T(8,128)} %collective-permute-done.5.refs_0_, bf16[2,640,640]{2,1,0:T(8,128)(2,1)S(1)} %get-tuple-element.88.refs_2_.high_ref.refs_1_, ...), custom_call_target="tpu_custom_call" | custom-call | flops 1 | bytes 1 | tf_op jit(solution)/shard_map/project_given/pallas_call | solution.py:210
  71.6 1.5 %collective-permute-start.15 = (f32[2,32,640]{2,1,0:T(8,128)S(1)}, f32[2,32,640]{2,1,0:T(8,128)S(1)}, u32[]{:S(2)}, u32[]{:S(2)}) collective-permute-start(f32[2,32,640]{2,1,0:T(8,128)S(1)} %slice_bitcast_fusion.2), channel_id=1, source_target_pairs={{0,16},{8,24},{16,0},{24,8},{1,17},{9,25},{17,1},{25,9},{2,18},{10... | collective-permute-start | bytes 491528 | tf_op jit(solution)/shard_map/ppermute | solution.py:320
  74.5 1.6 %collective-permute-start.16 = (f32[2,32,640]{2,1,0:T(8,128)S(1)}, f32[2,32,640]{2,1,0:T(8,128)S(1)}, u32[]{:S(2)}, u32[]{:S(2)}) collective-permute-start(f32[2,32,640]{2,1,0:T(8,128)S(1)} %slice_bitcast_fusion.1), channel_id=1, source_target_pairs={{0,8},{8,0},{16,24},{24,16},{1,9},{9,1},{17,25},{25,17},{2,10},{10... | collective-permute-start | bytes 491528 | tf_op jit(solution)/shard_map/ppermute | solution.py:320
  76.0 4.9 %collective-permute-done.19.refs_0_ = f32[256,640]{1,0:T(8,128)S(1)} collective-permute-done((f32[256,640]{1,0:T(8,128)S(1)}, f32[256,640]{1,0:T(8,128)S(1)}, u32[]{:S(2)}, u32[]{:S(2)}) %collective-permute-start.19) | collective-permute-done | bytes 655392 | tf_op jit(solution)/shard_map/ppermute | solution.py:311
  85.9 1.6 %collective-permute-start.27 = (f32[2,1,32,640]{3,2,1,0:T(8,128)S(1)}, f32[2,1,32,640]{3,2,1,0:T(8,128)S(1)}, u32[]{:S(2)}, u32[]{:S(2)}) collective-permute-start(f32[2,1,32,640]{3,2,1,0:T(8,128)S(1)} %get-tuple-element.129), channel_id=1, source_target_pairs={{0,8},{8,0},{16,24},{24,16},{1,9},{9,1},{17,25},{25,17},{2,10},{10... | collective-permute-start | bytes 491528 | tf_op jit(solution)/shard_map/ppermute | solution.py:320
  89.0 2.4 %collective-permute-start.26 = (f32[64,640]{1,0:T(8,128)S(1)}, f32[64,640]{1,0:T(8,128)S(1)}, u32[]{:S(2)}, u32[]{:S(2)}) collective-permute-start(f32[64,640]{1,0:T(8,128)S(1)} %get-tuple-element.141), channel_id=1, source_target_pairs={{0,1},{2,0},{3,2},{1,3},{4,5},{6,4},{7,6},{5,7},{8,9},{10,8},{11,1... | collective-permute-start | bytes 491528 | tf_op jit(solution)/shard_map/ppermute | solution.py:311
  92.2 1.3 %collective-permute-start.28 = (f32[1,32,640]{2,1,0:T(8,128)S(1)}, f32[1,32,640]{2,1,0:T(8,128)S(1)}, u32[]{:S(2)}, u32[]{:S(2)}) collective-permute-start(f32[1,32,640]{2,1,0:T(8,128)S(1)} %slice_bitcast_fusion.8), channel_id=1, source_target_pairs={{0,16},{8,24},{16,0},{24,8},{1,17},{9,25},{17,1},{25,9},{2,18},{10... | collective-permute-start | bytes 245768 | tf_op jit(solution)/shard_map/ppermute | solution.py:320
  94.4 2.3 %collective-permute-done.28 = f32[1,32,640]{2,1,0:T(8,128)S(1)} collective-permute-done((f32[1,32,640]{2,1,0:T(8,128)S(1)}, f32[1,32,640]{2,1,0:T(8,128)S(1)}, u32[]{:S(2)}, u32[]{:S(2)}) %collective-permute-start.28) | collective-permute-done | bytes 81952 | tf_op jit(solution)/shard_map/ppermute | solution.py:320
  96.7 1.4 %collective-permute-done.30 = f32[1,32,640]{2,1,0:T(8,128)S(1)} collective-permute-done((f32[1,32,640]{2,1,0:T(8,128)S(1)}, f32[1,32,640]{2,1,0:T(8,128)S(1)}, u32[]{:S(2)}, u32[]{:S(2)}) %collective-permute-start.30) | collective-permute-done | bytes 81952 | tf_op jit(solution)/shard_map/ppermute | solution.py:320
  98.1 3.2 %collective-permute-start.31 = (f32[64,640]{1,0:T(8,128)S(1)}, f32[64,640]{1,0:T(8,128)S(1)}, u32[]{:S(2)}, u32[]{:S(2)}) collective-permute-start(f32[64,640]{1,0:T(8,128)S(1)} %maximum_bitcast_fusion), channel_id=1, source_target_pairs={{0,3},{2,1},{3,0},{1,2},{4,7},{6,5},{7,4},{5,6},{8,11},{10,9},{11,... | collective-permute-start | bytes 491528 | tf_op jit(solution)/shard_map/ppermute | solution.py:311
  101.4 4.0 %collective-permute-done.31.refs_2_ = f32[64,640]{1,0:T(8,128)S(1)} collective-permute-done((f32[64,640]{1,0:T(8,128)S(1)}, f32[64,640]{1,0:T(8,128)S(1)}, u32[]{:S(2)}, u32[]{:S(2)}) %collective-permute-start.31) | collective-permute-done | bytes 163872 | tf_op jit(solution)/shard_map/ppermute | solution.py:311
  105.4 1.6 %assemble.1 = f32[64,2560]{1,0:T(8,128)} custom-call(s32[4]{0:T(128)S(1)} %pad_add_fusion.meta_ref, f32[64,640]{1,0:T(8,128)S(1)} %get-tuple-element.142.refs_0_, f32[64,640]{1,0:T(8,128)S(1)} %collective-permute-done.26.refs_1_, f32[64,640]{1,0:T(8,128)S(1)} %collective-permute-done.31.refs_2_, f32[64,640]{1,0:T(8,128)S(1)} %collective-permute-done.32.refs_3_), custom_call_target="tpu_custom_call" | custom-call | flops 1 | bytes 1 | tf_op jit(solution)/shard_map/assemble/pallas_call | solution.py:288
  (90 shorter events, 18.8 us)
Async XLA Ops:
  1.5 16.1 %collective-permute-start.2 = (f32[2,256,128]{2,1,0:T(8,128)S(1)}, f32[2,256,128]{2,1,0:T(8,128)S(1)}, u32[]{:S(2)}, u32[]{:S(2)}) collective-permute-start(f32[2,256,128]{2,1,0:T(8,128)S(1)} %pad_maximum_fusion.refs_0_), channel_id=1, source_target_pairs={{0,1},{2,0},{3,2},{1,3},{4,5},{6,4},{7,6},{5,7},{8,9},{10,8},{11,1... | collective-permute-start | bytes 786440 | tf_op jit(solution)/shard_map/ppermute | solution.py:311
  4.6 15.4 %collective-permute-start.1 = (f32[2,256,128]{2,1,0:T(8,128)S(1)}, f32[2,256,128]{2,1,0:T(8,128)S(1)}, u32[]{:S(2)}, u32[]{:S(2)}) collective-permute-start(f32[2,256,128]{2,1,0:T(8,128)S(1)} %pad_maximum_fusion.refs_0_), channel_id=1, source_target_pairs={{0,3},{2,1},{3,0},{1,2},{4,7},{6,5},{7,4},{5,6},{8,11},{10,9},{11,... | collective-permute-start | bytes 786440 | tf_op jit(solution)/shard_map/ppermute | solution.py:311
  7.1 16.1 %collective-permute-start = (f32[2,256,128]{2,1,0:T(8,128)S(1)}, f32[2,256,128]{2,1,0:T(8,128)S(1)}, u32[]{:S(2)}, u32[]{:S(2)}) collective-permute-start(f32[2,256,128]{2,1,0:T(8,128)S(1)} %pad_maximum_fusion.refs_0_), channel_id=1, source_target_pairs={{0,2},{2,3},{3,1},{1,0},{4,6},{6,7},{7,5},{5,4},{8,10},{10,11},{11... | collective-permute-start | bytes 786440 | tf_op jit(solution)/shard_map/ppermute | solution.py:311
  12.0 40.5 %collective-permute-start.8 = (f32[320,640]{1,0:T(8,128)}, f32[320,640]{1,0:T(8,128)}, u32[]{:S(2)}, u32[]{:S(2)}) collective-permute-start(f32[320,640]{1,0:T(8,128)} %get-tuple-element.137), channel_id=1, source_target_pairs={{0,24},{8,16},{16,8},{24,0},{1,25},{9,17},{17,9},{25,1},{2,26},{10... | collective-permute-start | bytes 2457608 | tf_op jit(solution)/shard_map/ppermute | solution.py:320
  14.5 38.0 %collective-permute-start.6 = (f32[320,640]{1,0:T(8,128)}, f32[320,640]{1,0:T(8,128)}, u32[]{:S(2)}, u32[]{:S(2)}) collective-permute-start(f32[320,640]{1,0:T(8,128)} %get-tuple-element.138), channel_id=1, source_target_pairs={{0,8},{8,0},{16,24},{24,16},{1,9},{9,1},{17,25},{25,17},{2,10},{10... | collective-permute-start | bytes 2457608 | tf_op jit(solution)/shard_map/ppermute | solution.py:320
  17.6 34.9 %collective-permute-start.7 = (f32[320,640]{1,0:T(8,128)}, f32[320,640]{1,0:T(8,128)}, u32[]{:S(2)}, u32[]{:S(2)}) collective-permute-start(f32[320,640]{1,0:T(8,128)} %get-tuple-element.140), channel_id=1, source_target_pairs={{0,16},{8,24},{16,0},{24,8},{1,17},{9,25},{17,1},{25,9},{2,18},{10... | collective-permute-start | bytes 2457608 | tf_op jit(solution)/shard_map/ppermute | solution.py:320
  23.9 22.1 %collective-permute-start.4 = (f32[3,256,128]{2,1,0:T(8,128)}, f32[3,256,128]{2,1,0:T(8,128)}, u32[]{:S(2)}, u32[]{:S(2)}) collective-permute-start(f32[3,256,128]{2,1,0:T(8,128)} %slice.65.refs_1_), channel_id=1, source_target_pairs={{0,2},{2,3},{3,1},{1,0},{4,6},{6,7},{7,5},{5,4},{8,10},{10,11},{11... | collective-permute-start | bytes 1179656 | tf_op jit(solution)/shard_map/ppermute | solution.py:311
  32.4 13.5 %collective-permute-start.3 = (f32[2,256,128]{2,1,0:T(8,128)}, f32[2,256,128]{2,1,0:T(8,128)}, u32[]{:S(2)}, u32[]{:S(2)}) collective-permute-start(f32[2,256,128]{2,1,0:T(8,128)} %slice.64.refs_0_), channel_id=1, source_target_pairs={{0,2},{2,3},{3,1},{1,0},{4,6},{6,7},{7,5},{5,4},{8,10},{10,11},{11... | collective-permute-start | bytes 786440 | tf_op jit(solution)/shard_map/ppermute | solution.py:311
  45.9 16.7 %collective-permute-start.5 = (f32[256,640]{1,0:T(8,128)}, f32[256,640]{1,0:T(8,128)}, u32[]{:S(2)}, u32[]{:S(2)}) collective-permute-start(f32[256,640]{1,0:T(8,128)} %attend.2.refs_0_), channel_id=1, source_target_pairs={{0,1},{2,0},{3,2},{1,3},{4,5},{6,4},{7,6},{5,7},{8,9},{10,8},{11,1... | collective-permute-start | bytes 1966088 | tf_op jit(solution)/shard_map/ppermute | solution.py:311
  56.8 3.0 %collective-permute-start.9 = (f32[128,640]{1,0:T(8,128)S(1)}, f32[128,640]{1,0:T(8,128)S(1)}, u32[]{:S(2)}, u32[]{:S(2)}) collective-permute-start(f32[128,640]{1,0:T(8,128)S(1)} %get-tuple-element.90), channel_id=1, source_target_pairs={{0,4},{4,0},{1,5},{5,1},{2,6},{6,2},{3,7},{7,3},{8,12},{12,8},{9,1... | collective-permute-start | bytes 983048 | tf_op jit(solution)/shard_map/ppermute | solution.py:312
  56.9 3.0 %collective-permute-start.10 = (f32[128,640]{1,0:T(8,128)S(1)}, f32[128,640]{1,0:T(8,128)S(1)}, u32[]{:S(2)}, u32[]{:S(2)}) collective-permute-start(f32[128,640]{1,0:T(8,128)S(1)} %get-tuple-element.91), channel_id=1, source_target_pairs={{0,4},{4,0},{1,5},{5,1},{2,6},{6,2},{3,7},{7,3},{8,12},{12,8},{9,1... | collective-permute-start | bytes 983048 | tf_op jit(solution)/shard_map/ppermute | solution.py:312
  57.4 2.5 %collective-permute-start.11 = (f32[128,640]{1,0:T(8,128)S(1)}, f32[128,640]{1,0:T(8,128)S(1)}, u32[]{:S(2)}, u32[]{:S(2)}) collective-permute-start(f32[128,640]{1,0:T(8,128)S(1)} %get-tuple-element.92), channel_id=1, source_target_pairs={{0,4},{4,0},{1,5},{5,1},{2,6},{6,2},{3,7},{7,3},{8,12},{12,8},{9,1... | collective-permute-start | bytes 983048 | tf_op jit(solution)/shard_map/ppermute | solution.py:312
  57.4 2.4 %collective-permute-start.12 = (f32[128,640]{1,0:T(8,128)S(1)}, f32[128,640]{1,0:T(8,128)S(1)}, u32[]{:S(2)}, u32[]{:S(2)}) collective-permute-start(f32[128,640]{1,0:T(8,128)S(1)} %get-tuple-element.93), channel_id=1, source_target_pairs={{0,4},{4,0},{1,5},{5,1},{2,6},{6,2},{3,7},{7,3},{8,12},{12,8},{9,1... | collective-permute-start | bytes 983048 | tf_op jit(solution)/shard_map/ppermute | solution.py:312
  62.9 8.7 %collective-permute-start.13 = (f32[2,2,32,640]{3,2,1,0:T(8,128)S(1)}, f32[2,2,32,640]{3,2,1,0:T(8,128)S(1)}, u32[]{:S(2)}, u32[]{:S(2)}) collective-permute-start(f32[2,2,32,640]{3,2,1,0:T(8,128)S(1)} %get-tuple-element.110), channel_id=1, source_target_pairs={{0,8},{8,0},{16,24},{24,16},{1,9},{9,1},{17,25},{25,17},{2,10},{10... | collective-permute-start | bytes 983048 | tf_op jit(solution)/shard_map/ppermute | solution.py:320
  64.4 7.1 %collective-permute-start.14 = (f32[2,2,32,640]{3,2,1,0:T(8,128)S(1)}, f32[2,2,32,640]{3,2,1,0:T(8,128)S(1)}, u32[]{:S(2)}, u32[]{:S(2)}) collective-permute-start(f32[2,2,32,640]{3,2,1,0:T(8,128)S(1)} %get-tuple-element.111), channel_id=1, source_target_pairs={{0,16},{8,24},{16,0},{24,8},{1,17},{9,25},{17,1},{25,9},{2,18},{10... | collective-permute-start | bytes 983048 | tf_op jit(solution)/shard_map/ppermute | solution.py:320
  66.0 15.0 %collective-permute-start.19 = (f32[256,640]{1,0:T(8,128)S(1)}, f32[256,640]{1,0:T(8,128)S(1)}, u32[]{:S(2)}, u32[]{:S(2)}) collective-permute-start(f32[256,640]{1,0:T(8,128)S(1)} %copy-done.1), channel_id=1, source_target_pairs={{0,2},{2,3},{3,1},{1,0},{4,6},{6,7},{7,5},{5,4},{8,10},{10,11},{11... | collective-permute-start | bytes 1966088 | tf_op jit(solution)/shard_map/ppermute | solution.py:311
  69.9 3.3 %collective-permute-start.17 = (f32[128,640]{1,0:T(8,128)S(1)}, f32[128,640]{1,0:T(8,128)S(1)}, u32[]{:S(2)}, u32[]{:S(2)}) collective-permute-start(f32[128,640]{1,0:T(8,128)S(1)} %get-tuple-element.116), channel_id=1, source_target_pairs={{0,4},{4,0},{1,5},{5,1},{2,6},{6,2},{3,7},{7,3},{8,12},{12,8},{9,1... | collective-permute-start | bytes 983048 | tf_op jit(solution)/shard_map/ppermute | solution.py:312
  70.0 3.2 %collective-permute-start.18 = (f32[128,640]{1,0:T(8,128)S(1)}, f32[128,640]{1,0:T(8,128)S(1)}, u32[]{:S(2)}, u32[]{:S(2)}) collective-permute-start(f32[128,640]{1,0:T(8,128)S(1)} %get-tuple-element.117), channel_id=1, source_target_pairs={{0,4},{4,0},{1,5},{5,1},{2,6},{6,2},{3,7},{7,3},{8,12},{12,8},{9,1... | collective-permute-start | bytes 983048 | tf_op jit(solution)/shard_map/ppermute | solution.py:312
  71.6 15.9 %collective-permute-start.15 = (f32[2,32,640]{2,1,0:T(8,128)S(1)}, f32[2,32,640]{2,1,0:T(8,128)S(1)}, u32[]{:S(2)}, u32[]{:S(2)}) collective-permute-start(f32[2,32,640]{2,1,0:T(8,128)S(1)} %slice_bitcast_fusion.2), channel_id=1, source_target_pairs={{0,16},{8,24},{16,0},{24,8},{1,17},{9,25},{17,1},{25,9},{2,18},{10... | collective-permute-start | bytes 491528 | tf_op jit(solution)/shard_map/ppermute | solution.py:320
  73.3 7.7 %collective-permute-start.20 = (f32[2,1,32,640]{3,2,1,0:T(8,128)S(1)}, f32[2,1,32,640]{3,2,1,0:T(8,128)S(1)}, u32[]{:S(2)}, u32[]{:S(2)}) collective-permute-start(f32[2,1,32,640]{3,2,1,0:T(8,128)S(1)} %get-tuple-element.119), channel_id=1, source_target_pairs={{0,8},{8,0},{16,24},{24,16},{1,9},{9,1},{17,25},{25,17},{2,10},{10... | collective-permute-start | bytes 491528 | tf_op jit(solution)/shard_map/ppermute | solution.py:320
  73.9 7.5 %collective-permute-start.21 = (f32[2,1,32,640]{3,2,1,0:T(8,128)S(1)}, f32[2,1,32,640]{3,2,1,0:T(8,128)S(1)}, u32[]{:S(2)}, u32[]{:S(2)}) collective-permute-start(f32[2,1,32,640]{3,2,1,0:T(8,128)S(1)} %get-tuple-element.120), channel_id=1, source_target_pairs={{0,16},{8,24},{16,0},{24,8},{1,17},{9,25},{17,1},{25,9},{2,18},{10... | collective-permute-start | bytes 491528 | tf_op jit(solution)/shard_map/ppermute | solution.py:320
  74.5 14.0 %collective-permute-start.16 = (f32[2,32,640]{2,1,0:T(8,128)S(1)}, f32[2,32,640]{2,1,0:T(8,128)S(1)}, u32[]{:S(2)}, u32[]{:S(2)}) collective-permute-start(f32[2,32,640]{2,1,0:T(8,128)S(1)} %slice_bitcast_fusion.1), channel_id=1, source_target_pairs={{0,8},{8,0},{16,24},{24,16},{1,9},{9,1},{17,25},{25,17},{2,10},{10... | collective-permute-start | bytes 491528 | tf_op jit(solution)/shard_map/ppermute | solution.py:320
  82.5 3.2 %collective-permute-start.25 = (f32[128,640]{1,0:T(8,128)S(1)}, f32[128,640]{1,0:T(8,128)S(1)}, u32[]{:S(2)}, u32[]{:S(2)}) collective-permute-start(f32[128,640]{1,0:T(8,128)S(1)} %get-tuple-element.128), channel_id=1, source_target_pairs={{0,4},{4,0},{1,5},{5,1},{2,6},{6,2},{3,7},{7,3},{8,12},{12,8},{9,1... | collective-permute-start | bytes 983048 | tf_op jit(solution)/shard_map/ppermute | solution.py:312
  83.1 5.4 %collective-permute-start.22 = (f32[1,32,640]{2,1,0:T(8,128)S(1)}, f32[1,32,640]{2,1,0:T(8,128)S(1)}, u32[]{:S(2)}, u32[]{:S(2)}) collective-permute-start(f32[1,32,640]{2,1,0:T(8,128)S(1)} %slice_bitcast_fusion.11), channel_id=1, source_target_pairs={{0,16},{8,24},{16,0},{24,8},{1,17},{9,25},{17,1},{25,9},{2,18},{10... | collective-permute-start | bytes 245768 | tf_op jit(solution)/shard_map/ppermute | solution.py:320
  84.2 4.7 %collective-permute-start.23 = (f32[1,32,640]{2,1,0:T(8,128)S(1)}, f32[1,32,640]{2,1,0:T(8,128)S(1)}, u32[]{:S(2)}, u32[]{:S(2)}) collective-permute-start(f32[1,32,640]{2,1,0:T(8,128)S(1)} %slice_bitcast_fusion.10), channel_id=1, source_target_pairs={{0,8},{8,0},{16,24},{24,16},{1,9},{9,1},{17,25},{25,17},{2,10},{10... | collective-permute-start | bytes 245768 | tf_op jit(solution)/shard_map/ppermute | solution.py:320
  85.9 6.3 %collective-permute-start.27 = (f32[2,1,32,640]{3,2,1,0:T(8,128)S(1)}, f32[2,1,32,640]{3,2,1,0:T(8,128)S(1)}, u32[]{:S(2)}, u32[]{:S(2)}) collective-permute-start(f32[2,1,32,640]{3,2,1,0:T(8,128)S(1)} %get-tuple-element.129), channel_id=1, source_target_pairs={{0,8},{8,0},{16,24},{24,16},{1,9},{9,1},{17,25},{25,17},{2,10},{10... | collective-permute-start | bytes 491528 | tf_op jit(solution)/shard_map/ppermute | solution.py:320
  87.5 6.1 %collective-permute-start.29 = (f32[2,1,32,640]{3,2,1,0:T(8,128)S(1)}, f32[2,1,32,640]{3,2,1,0:T(8,128)S(1)}, u32[]{:S(2)}, u32[]{:S(2)}) collective-permute-start(f32[2,1,32,640]{3,2,1,0:T(8,128)S(1)} %get-tuple-element.130), channel_id=1, source_target_pairs={{0,16},{8,24},{16,0},{24,8},{1,17},{9,25},{17,1},{25,9},{2,18},{10... | collective-permute-start | bytes 491528 | tf_op jit(solution)/shard_map/ppermute | solution.py:320
  89.0 12.3 %collective-permute-start.26 = (f32[64,640]{1,0:T(8,128)S(1)}, f32[64,640]{1,0:T(8,128)S(1)}, u32[]{:S(2)}, u32[]{:S(2)}) collective-permute-start(f32[64,640]{1,0:T(8,128)S(1)} %get-tuple-element.141), channel_id=1, source_target_pairs={{0,1},{2,0},{3,2},{1,3},{4,5},{6,4},{7,6},{5,7},{8,9},{10,8},{11,1... | collective-permute-start | bytes 491528 | tf_op jit(solution)/shard_map/ppermute | solution.py:311
  91.5 9.9 %collective-permute-start.32 = (f32[64,640]{1,0:T(8,128)S(1)}, f32[64,640]{1,0:T(8,128)S(1)}, u32[]{:S(2)}, u32[]{:S(2)}) collective-permute-start(f32[64,640]{1,0:T(8,128)S(1)} %maximum_bitcast_fusion.1), channel_id=1, source_target_pairs={{0,2},{2,3},{3,1},{1,0},{4,6},{6,7},{7,5},{5,4},{8,10},{10,11},{11... | collective-permute-start | bytes 491528 | tf_op jit(solution)/shard_map/ppermute | solution.py:311
  92.2 4.5 %collective-permute-start.28 = (f32[1,32,640]{2,1,0:T(8,128)S(1)}, f32[1,32,640]{2,1,0:T(8,128)S(1)}, u32[]{:S(2)}, u32[]{:S(2)}) collective-permute-start(f32[1,32,640]{2,1,0:T(8,128)S(1)} %slice_bitcast_fusion.8), channel_id=1, source_target_pairs={{0,16},{8,24},{16,0},{24,8},{1,17},{9,25},{17,1},{25,9},{2,18},{10... | collective-permute-start | bytes 245768 | tf_op jit(solution)/shard_map/ppermute | solution.py:320
  93.6 4.5 %collective-permute-start.30 = (f32[1,32,640]{2,1,0:T(8,128)S(1)}, f32[1,32,640]{2,1,0:T(8,128)S(1)}, u32[]{:S(2)}, u32[]{:S(2)}) collective-permute-start(f32[1,32,640]{2,1,0:T(8,128)S(1)} %slice_bitcast_fusion.6), channel_id=1, source_target_pairs={{0,8},{8,0},{16,24},{24,16},{1,9},{9,1},{17,25},{25,17},{2,10},{10... | collective-permute-start | bytes 245768 | tf_op jit(solution)/shard_map/ppermute | solution.py:320
  98.1 7.3 %collective-permute-start.31 = (f32[64,640]{1,0:T(8,128)S(1)}, f32[64,640]{1,0:T(8,128)S(1)}, u32[]{:S(2)}, u32[]{:S(2)}) collective-permute-start(f32[64,640]{1,0:T(8,128)S(1)} %maximum_bitcast_fusion), channel_id=1, source_target_pairs={{0,3},{2,1},{3,0},{1,2},{4,7},{6,5},{7,4},{5,6},{8,11},{10,9},{11,... | collective-permute-start | bytes 491528 | tf_op jit(solution)/shard_map/ppermute | solution.py:311
  (7 other events, 26.4 us)

commit v7 on v6

--- a/solution.py
+++ b/solution.py
@@ -354,9 +354,9 @@
     *given, a_high, a_low = project_given([owns[3]], high, low, 2)
     given = exchange(given)
     kept = project_kept(a_high, a_low, high, low)
-    kept, *got_a = after(kept, *got_a)
+    *keep_b, up, down = fold(place, kept, given, 1, parts, orders)
+    up, *got_a = after(up, *got_a)
     keep_a = add(keep_a, got_a)
-    *keep_b, up, down = fold(place, kept, given, 1, parts, orders)
     got_b = first([up, down])
     owns[2], *got_b = after(owns[2], *got_b)
     keep_b = add(keep_b, got_b)

time: 107 us -> 111 us (1.037)
  waiting for transfers between devices: 28.4 us -> 32.9 us
    ppermute x15, waiting for transfers between devices: 4.63 us -> 9.16 us  [by_heads(): lax.ppermute(x, 'feature', [(i, i ^ e) for i in range(parts)])]
    ppermute x10, starting transfers between devices: 25.1 us -> 23.8 us  [by_heads(): ring = lambda x, step: lax.ppermute(x, 'seq', ring_perm(planes, step))]
  transfers between devices with their start and end apart: 33 -> 33, of which waited for: 12 -> 12; matrix products, arithmetic and copies ran while one was open for 7% -> 6% of each run, Pallas kernels for 22% -> 19%
where the time goes in v7:
time: 111 us
  starting transfers between devices  43.6 us (39%)
  waiting for transfers between devices  32.9 us (30%)
  Pallas kernels  24.9 us (22%)
  local copies, waits for them, and re-layouts  8.34 us (8%)
    ppermute x10, starting transfers between devices, by_heads(): ring = lambda x, step: lax.ppermute(x, 'seq', ring_perm(planes, step))  23.8 us
    ppermute x10, waiting for transfers between devices, by_heads(): ring = lambda x, step: lax.ppermute(x, 'seq', ring_perm(planes, step))  23.7 us
    ppermute x15, starting transfers between devices, by_heads(): lax.ppermute(x, 'feature', [(i, i ^ e) for i in range(parts)])  17.6 us
    ppermute x15, waiting for transfers between devices, by_heads(): lax.ppermute(x, 'feature', [(i, i ^ e) for i in range(parts)])  9.16 us
    pallas_call x2, Pallas kernels, attend(): pl.pallas_call(kernel, out_shape=jax.ShapeDtypeStruct((rows, group * d),...  8.61 us
    pallas_call x3, Pallas kernels, project_given(): pl.pallas_call(kernel, out_shape=tuple((jax.ShapeDtypeStruct((b - a, colu...  5.2 us
    pallas_call x3, Pallas kernels, project_kept(): pl.pallas_call(kernel, out_shape=jax.ShapeDtypeStruct((a_high.shape[0], h...  4.09 us
    transpose x1, local copies, waits for them, and re-layouts, by_heads(): turn = lambda x: lax.dynamic_slice_in_dim(w_out, x * k_rows, k_rows, 0).T  3.37 us
  transfers between devices with their start and end apart: 33, of which 12 were waited for; matrix products, arithmetic and copies ran while one was open for 6% of the time, Pallas kernels for 19%

profile of v7, /device:TPU:0, one launch (start us, length us, event | category | flops | bytes accessed | tf_op | source)
XLA Modules:
  0.0 111.1 jit_solution(5162750419590542845)
XLA Ops:
  0.0 1.5 %constant_dynamic-slice_fusion = (f32[256,1,128]{2,1,0:T(1,128)S(1)}, f32[256,1,128]{2,1,0:T(1,128)S(1)}) fusion(f32[256,4,128]{2,1,0:T(4,128)} %param.6, s32[]{:T(128)S(6)} %select_n.139, f32[256,4,128]{2,1,0:T(4,128)} %param.5), kind=kLoop, calls=%fused_computation.32 | loop fusion | bytes 524292 | tf_op jit(solution)/shard_map/jit(dynamic_index_in_dim)/dynamic_slice | solution.py:314
  1.5 3.1 %collective-permute-start.2 = (f32[2,256,128]{2,1,0:T(8,128)S(1)}, f32[2,256,128]{2,1,0:T(8,128)S(1)}, u32[]{:S(2)}, u32[]{:S(2)}) collective-permute-start(f32[2,256,128]{2,1,0:T(8,128)S(1)} %pad_maximum_fusion.refs_0_), channel_id=1, source_target_pairs={{0,1},{2,0},{3,2},{1,3},{4,5},{6,4},{7,6},{5,7},{8,9},{10,8},{11,1... | collective-permute-start | bytes 786440 | tf_op jit(solution)/shard_map/ppermute | solution.py:311
  4.6 2.5 %collective-permute-start.1 = (f32[2,256,128]{2,1,0:T(8,128)S(1)}, f32[2,256,128]{2,1,0:T(8,128)S(1)}, u32[]{:S(2)}, u32[]{:S(2)}) collective-permute-start(f32[2,256,128]{2,1,0:T(8,128)S(1)} %pad_maximum_fusion.refs_0_), channel_id=1, source_target_pairs={{0,3},{2,1},{3,0},{1,2},{4,7},{6,5},{7,4},{5,6},{8,11},{10,9},{11,... | collective-permute-start | bytes 786440 | tf_op jit(solution)/shard_map/ppermute | solution.py:311
  7.1 1.6 %collective-permute-start = (f32[2,256,128]{2,1,0:T(8,128)S(1)}, f32[2,256,128]{2,1,0:T(8,128)S(1)}, u32[]{:S(2)}, u32[]{:S(2)}) collective-permute-start(f32[2,256,128]{2,1,0:T(8,128)S(1)} %pad_maximum_fusion.refs_0_), channel_id=1, source_target_pairs={{0,2},{2,3},{3,1},{1,0},{4,6},{6,7},{7,5},{5,4},{8,10},{10,11},{11... | collective-permute-start | bytes 786440 | tf_op jit(solution)/shard_map/ppermute | solution.py:311
  8.6 3.4 %dynamic-slice_bitcast_fusion = (f32[320,640]{1,0:T(8,128)}, f32[320,640]{1,0:T(8,128)}, f32[320,640]{1,0:T(8,128)S(1)}, f32[320,640]{1,0:T(8,128)}) fusion(f32[2560,320]{0,1:T(8,128)} %param.7, s32[]{:T(128)S(6)} %select_n.150, s32[]{:T(128)S(6)} %select_n.148, s32[]{:T(128)S(6)} %select_n.140, s32[]{:T(128)S(6)} %select_n.149), kind=kLoop, calls=%fused_computation | loop fusion | bytes 6553616 | tf_op jit(solution)/shard_map/transpose | solution.py:319
  12.0 2.4 %collective-permute-start.8 = (f32[320,640]{1,0:T(8,128)}, f32[320,640]{1,0:T(8,128)}, u32[]{:S(2)}, u32[]{:S(2)}) collective-permute-start(f32[320,640]{1,0:T(8,128)} %get-tuple-element.137), channel_id=1, source_target_pairs={{0,24},{8,16},{16,8},{24,0},{1,25},{9,17},{17,9},{25,1},{2,26},{10... | collective-permute-start | bytes 2457608 | tf_op jit(solution)/shard_map/ppermute | solution.py:320
  20.0 3.2 %collective-permute-done.refs_1_ = f32[2,256,128]{2,1,0:T(8,128)S(1)} collective-permute-done((f32[2,256,128]{2,1,0:T(8,128)S(1)}, f32[2,256,128]{2,1,0:T(8,128)S(1)}, u32[]{:S(2)}, u32[]{:S(2)}) %collective-permute-start) | collective-permute-done | bytes 262176 | tf_op jit(solution)/shard_map/ppermute | solution.py:311
  23.9 8.5 %collective-permute-start.4 = (f32[3,256,128]{2,1,0:T(8,128)}, f32[3,256,128]{2,1,0:T(8,128)}, u32[]{:S(2)}, u32[]{:S(2)}) collective-permute-start(f32[3,256,128]{2,1,0:T(8,128)} %slice.65.refs_1_), channel_id=1, source_target_pairs={{0,2},{2,3},{3,1},{1,0},{4,6},{6,7},{7,5},{5,4},{8,10},{10,11},{11... | collective-permute-start | bytes 1179656 | tf_op jit(solution)/shard_map/ppermute | solution.py:311
  32.4 2.6 %prepare_keys.1 = (bf16[384,1024]{1,0:T(8,128)(2,1)}, bf16[2048,256]{1,0:T(8,128)(2,1)}) custom-call(f32[2,256,128]{2,1,0:T(8,128)} %copy-done.2, f32[2,256,128]{2,1,0:T(8,128)} %copy-done.5, f32[2,256,128]{2,1,0:T(8,128)} %copy-done.4, f32[2,256,128]{2,1,0:T(8,128)} %copy-done.3), custom_call_target="tpu_custom_call" | custom-call | flops 1 | bytes 1 | tf_op jit(solution)/shard_map/prepare_keys/pallas_call | solution.py:83
  35.1 3.7 %attend.2.refs_0_ = f32[256,640]{1,0:T(8,128)} custom-call(s32[4]{0:T(128)} %pad_add_fusion.1.meta_ref, f32[2,256,128]{2,1,0:T(8,128)} %slice.64.refs_0_, f32[3,256,128]{2,1,0:T(8,128)} %slice.65.refs_1_, bf16[384,1024]{1,0:T(8,128)(2,1)} %get-tuple-element.78.refs_2_, bf16[2048,256]{1,0:T(8,128)(2,1)} %get-tuple-element.79.refs_3_), custom_call_target="tpu_custom_call" | custom-call | flops 1 | bytes 1 | tf_op jit(solution)/shard_map/attend/pallas_call | solution.py:144
  38.7 7.2 %collective-permute-done.3.refs_0_ = f32[2,256,128]{2,1,0:T(8,128)} collective-permute-done((f32[2,256,128]{2,1,0:T(8,128)}, f32[2,256,128]{2,1,0:T(8,128)}, u32[]{:S(2)}, u32[]{:S(2)}) %collective-permute-start.3) | collective-permute-done | bytes 262176 | tf_op jit(solution)/shard_map/ppermute | solution.py:311
  45.9 1.5 %collective-permute-start.5 = (f32[256,640]{1,0:T(8,128)}, f32[256,640]{1,0:T(8,128)}, u32[]{:S(2)}, u32[]{:S(2)}) collective-permute-start(f32[256,640]{1,0:T(8,128)} %attend.2.refs_0_), channel_id=1, source_target_pairs={{0,1},{2,0},{3,2},{1,3},{4,5},{6,4},{7,6},{5,7},{8,9},{10,8},{11,1... | collective-permute-start | bytes 1966088 | tf_op jit(solution)/shard_map/ppermute | solution.py:311
  47.5 4.9 %attend.3.refs_1_ = f32[256,640]{1,0:T(8,128)} custom-call(s32[4]{0:T(128)} %pad_add_fusion.1.meta_ref, f32[2,256,128]{2,1,0:T(8,128)} %collective-permute-done.3.refs_0_, f32[3,256,128]{2,1,0:T(8,128)} %collective-permute-done.4.refs_1_, bf16[384,1024]{1,0:T(8,128)(2,1)} %get-tuple-element.78.refs_2_, bf16[2048,256]{1,0:T(8,128)(2,1)} %get-tuple-element.79.refs_3_), custom_call_target="tpu_custom_call" | custom-call | flops 1 | bytes 1 | tf_op jit(solution)/shard_map/attend/pallas_call | solution.py:144
  52.5 2.3 %prepare_weights.1 = (bf16[2,640,640]{2,1,0:T(8,128)(2,1)S(1)}, bf16[2,640,640]{2,1,0:T(8,128)(2,1)S(1)}) custom-call(s32[8]{0:T(128)S(1)} %stack.88.meta_ref, f32[320,640]{1,0:T(8,128)S(1)} %get-tuple-element.84.refs_0_, f32[320,640]{1,0:T(8,128)} %collective-permute-done.6.refs_1_, f32[320,640]{1,0:T(8,128)} %collective-permute-done.7.refs_2_, ...), custom_call_target="tpu_custom_call" | custom-call | flops 1 | bytes 1 | tf_op jit(solution)/shard_map/prepare_weights/pallas_call | solution.py:177
  54.8 1.9 %project_given.3 = (f32[128,640]{1,0:T(8,128)S(1)}, f32[128,640]{1,0:T(8,128)S(1)}, f32[128,640]{1,0:T(8,128)S(1)}, f32[128,640]{1,0:T(8,128)S(1)}, bf16[512,640...) custom-call(f32[256,640]{1,0:T(8,128)S(1)} %copy-done, f32[256,640]{1,0:T(8,128)S(1)} %copy-done.1, ...), custom_call_target="tpu_custom_call" | custom-call | flops 1 | bytes 1 | tf_op jit(solution)/shard_map/project_given/pallas_call | solution.py:210
  57.9 1.9 %project_kept.3.kept_ref = f32[512,640]{1,0:T(8,128)S(1)} custom-call(bf16[512,640]{1,0:T(8,128)(2,1)S(1)} %get-tuple-element.96.a_high_ref, bf16[512,640]{1,0:T(8,128)(2,1)S(1)} %get-tuple-element.97.a_low_ref, bf16[2,640,640]{2,1,0:T(8,128)(2,1)S(1)} %get-tuple-element.88.refs_2_.high_ref.refs_1_, ...), custom_call_target="tpu_custom_call" | custom-call | flops 1 | bytes 1 | tf_op jit(solution)/shard_map/project_kept/pallas_call | solution.py:228
  59.9 2.8 %collective-permute-done.5.refs_0_ = f32[256,640]{1,0:T(8,128)} collective-permute-done((f32[256,640]{1,0:T(8,128)}, f32[256,640]{1,0:T(8,128)}, u32[]{:S(2)}, u32[]{:S(2)}) %collective-permute-start.5) | collective-permute-done | bytes 655392 | tf_op jit(solution)/shard_map/ppermute | solution.py:311
  62.9 2.2 %project_given.4 = (f32[128,640]{1,0:T(8,128)S(1)}, f32[128,640]{1,0:T(8,128)S(1)}, bf16[256,640]{1,0:T(8,128)(2,1)S(1)}, bf16[256,640]{1,0:T(8,128)(2,1)S(1)}) custom-call(f32[256,640]{1,0:T(8,128)} %collective-permute-done.5.refs_0_, bf16[2,640,640]{2,1,0:T(8,128)(2,1)S(1)} %get-tuple-element.88.refs_2_.high_ref.refs_1_, ...), custom_call_target="tpu_custom_call" | custom-call | flops 1 | bytes 1 | tf_op jit(solution)/shard_map/project_given/pallas_call | solution.py:210
  65.6 1.5 %collective-permute-start.15 = (f32[2,2,32,640]{3,2,1,0:T(8,128)S(1)}, f32[2,2,32,640]{3,2,1,0:T(8,128)S(1)}, u32[]{:S(2)}, u32[]{:S(2)}) collective-permute-start(f32[2,2,32,640]{3,2,1,0:T(8,128)S(1)} %get-tuple-element.113), channel_id=1, source_target_pairs={{0,8},{8,0},{16,24},{24,16},{1,9},{9,1},{17,25},{25,17},{2,10},{10... | collective-permute-start | bytes 983048 | tf_op jit(solution)/shard_map/ppermute | solution.py:320
  67.1 1.5 %collective-permute-start.16 = (f32[2,2,32,640]{3,2,1,0:T(8,128)S(1)}, f32[2,2,32,640]{3,2,1,0:T(8,128)S(1)}, u32[]{:S(2)}, u32[]{:S(2)}) collective-permute-start(f32[2,2,32,640]{3,2,1,0:T(8,128)S(1)} %get-tuple-element.114), channel_id=1, source_target_pairs={{0,16},{8,24},{16,0},{24,8},{1,17},{9,25},{17,1},{25,9},{2,18},{10... | collective-permute-start | bytes 983048 | tf_op jit(solution)/shard_map/ppermute | solution.py:320
  68.6 1.7 %collective-permute-start.19 = (f32[256,640]{1,0:T(8,128)S(1)}, f32[256,640]{1,0:T(8,128)S(1)}, u32[]{:S(2)}, u32[]{:S(2)}) collective-permute-start(f32[256,640]{1,0:T(8,128)S(1)} %copy-done.1), channel_id=1, source_target_pairs={{0,2},{2,3},{3,1},{1,0},{4,6},{6,7},{7,5},{5,4},{8,10},{10,11},{11... | collective-permute-start | bytes 1966088 | tf_op jit(solution)/shard_map/ppermute | solution.py:311
  71.6 3.7 %collective-permute-done.15 = f32[2,2,32,640]{3,2,1,0:T(8,128)S(1)} collective-permute-done((f32[2,2,32,640]{3,2,1,0:T(8,128)S(1)}, f32[2,2,32,640]{3,2,1,0:T(8,128)S(1)}, u32[]{:S(2)}, u32[]{:S(2)}) %collective-permute-start.15) | collective-permute-done | bytes 327712 | tf_op jit(solution)/shard_map/ppermute | solution.py:320
  76.6 1.6 %collective-permute-start.17 = (f32[2,32,640]{2,1,0:T(8,128)S(1)}, f32[2,32,640]{2,1,0:T(8,128)S(1)}, u32[]{:S(2)}, u32[]{:S(2)}) collective-permute-start(f32[2,32,640]{2,1,0:T(8,128)S(1)} %slice_bitcast_fusion.2), channel_id=1, source_target_pairs={{0,16},{8,24},{16,0},{24,8},{1,17},{9,25},{17,1},{25,9},{2,18},{10... | collective-permute-start | bytes 491528 | tf_op jit(solution)/shard_map/ppermute | solution.py:320
  79.3 1.6 %collective-permute-start.18 = (f32[2,32,640]{2,1,0:T(8,128)S(1)}, f32[2,32,640]{2,1,0:T(8,128)S(1)}, u32[]{:S(2)}, u32[]{:S(2)}) collective-permute-start(f32[2,32,640]{2,1,0:T(8,128)S(1)} %slice_bitcast_fusion.1), channel_id=1, source_target_pairs={{0,8},{8,0},{16,24},{24,16},{1,9},{9,1},{17,25},{25,17},{2,10},{10... | collective-permute-start | bytes 491528 | tf_op jit(solution)/shard_map/ppermute | solution.py:320
  80.8 4.0 %collective-permute-done.19.refs_0_ = f32[256,640]{1,0:T(8,128)S(1)} collective-permute-done((f32[256,640]{1,0:T(8,128)S(1)}, f32[256,640]{1,0:T(8,128)S(1)}, u32[]{:S(2)}, u32[]{:S(2)}) %collective-permute-start.19) | collective-permute-done | bytes 655392 | tf_op jit(solution)/shard_map/ppermute | solution.py:311
  86.9 1.6 %collective-permute-start.22 = (f32[1,32,640]{2,1,0:T(8,128)S(1)}, f32[1,32,640]{2,1,0:T(8,128)S(1)}, u32[]{:S(2)}, u32[]{:S(2)}) collective-permute-start(f32[1,32,640]{2,1,0:T(8,128)S(1)} %slice_bitcast_fusion.11), channel_id=1, source_target_pairs={{0,16},{8,24},{16,0},{24,8},{1,17},{9,25},{17,1},{25,9},{2,18},{10... | collective-permute-start | bytes 245768 | tf_op jit(solution)/shard_map/ppermute | solution.py:320
  90.4 1.5 %collective-permute-start.27 = (f32[2,1,32,640]{3,2,1,0:T(8,128)S(1)}, f32[2,1,32,640]{3,2,1,0:T(8,128)S(1)}, u32[]{:S(2)}, u32[]{:S(2)}) collective-permute-start(f32[2,1,32,640]{3,2,1,0:T(8,128)S(1)} %get-tuple-element.129), channel_id=1, source_target_pairs={{0,8},{8,0},{16,24},{24,16},{1,9},{9,1},{17,25},{25,17},{2,10},{10... | collective-permute-start | bytes 491528 | tf_op jit(solution)/shard_map/ppermute | solution.py:320
  94.2 2.5 %collective-permute-start.32 = (f32[64,640]{1,0:T(8,128)S(1)}, f32[64,640]{1,0:T(8,128)S(1)}, u32[]{:S(2)}, u32[]{:S(2)}) collective-permute-start(f32[64,640]{1,0:T(8,128)S(1)} %maximum_bitcast_fusion.1), channel_id=1, source_target_pairs={{0,2},{2,3},{3,1},{1,0},{4,6},{6,7},{7,5},{5,4},{8,10},{10,11},{11... | collective-permute-start | bytes 491528 | tf_op jit(solution)/shard_map/ppermute | solution.py:311
  99.0 2.2 %collective-permute-done.28 = f32[1,32,640]{2,1,0:T(8,128)S(1)} collective-permute-done((f32[1,32,640]{2,1,0:T(8,128)S(1)}, f32[1,32,640]{2,1,0:T(8,128)S(1)}, u32[]{:S(2)}, u32[]{:S(2)}) %collective-permute-start.28) | collective-permute-done | bytes 81952 | tf_op jit(solution)/shard_map/ppermute | solution.py:320
  102.2 1.8 %collective-permute-start.31 = (f32[64,640]{1,0:T(8,128)S(1)}, f32[64,640]{1,0:T(8,128)S(1)}, u32[]{:S(2)}, u32[]{:S(2)}) collective-permute-start(f32[64,640]{1,0:T(8,128)S(1)} %maximum_bitcast_fusion), channel_id=1, source_target_pairs={{0,3},{2,1},{3,0},{1,2},{4,7},{6,5},{7,4},{5,6},{8,11},{10,9},{11,... | collective-permute-start | bytes 491528 | tf_op jit(solution)/shard_map/ppermute | solution.py:311
  104.1 5.4 %collective-permute-done.31.refs_2_ = f32[64,640]{1,0:T(8,128)S(1)} collective-permute-done((f32[64,640]{1,0:T(8,128)S(1)}, f32[64,640]{1,0:T(8,128)S(1)}, u32[]{:S(2)}, u32[]{:S(2)}) %collective-permute-start.31) | collective-permute-done | bytes 163872 | tf_op jit(solution)/shard_map/ppermute | solution.py:311
  109.5 1.6 %assemble.1 = f32[64,2560]{1,0:T(8,128)} custom-call(s32[4]{0:T(128)S(1)} %pad_add_fusion.meta_ref, f32[64,640]{1,0:T(8,128)S(1)} %get-tuple-element.142.refs_0_, f32[64,640]{1,0:T(8,128)S(1)} %collective-permute-done.26.refs_1_, f32[64,640]{1,0:T(8,128)S(1)} %collective-permute-done.31.refs_2_, f32[64,640]{1,0:T(8,128)S(1)} %collective-permute-done.32.refs_3_), custom_call_target="tpu_custom_call" | custom-call | flops 1 | bytes 1 | tf_op jit(solution)/shard_map/assemble/pallas_call | solution.py:288
  (90 shorter events, 21.4 us)
Async XLA Ops:
  1.5 16.1 %collective-permute-start.2 = (f32[2,256,128]{2,1,0:T(8,128)S(1)}, f32[2,256,128]{2,1,0:T(8,128)S(1)}, u32[]{:S(2)}, u32[]{:S(2)}) collective-permute-start(f32[2,256,128]{2,1,0:T(8,128)S(1)} %pad_maximum_fusion.refs_0_), channel_id=1, source_target_pairs={{0,1},{2,0},{3,2},{1,3},{4,5},{6,4},{7,6},{5,7},{8,9},{10,8},{11,1... | collective-permute-start | bytes 786440 | tf_op jit(solution)/shard_map/ppermute | solution.py:311
  4.6 15.4 %collective-permute-start.1 = (f32[2,256,128]{2,1,0:T(8,128)S(1)}, f32[2,256,128]{2,1,0:T(8,128)S(1)}, u32[]{:S(2)}, u32[]{:S(2)}) collective-permute-start(f32[2,256,128]{2,1,0:T(8,128)S(1)} %pad_maximum_fusion.refs_0_), channel_id=1, source_target_pairs={{0,3},{2,1},{3,0},{1,2},{4,7},{6,5},{7,4},{5,6},{8,11},{10,9},{11,... | collective-permute-start | bytes 786440 | tf_op jit(solution)/shard_map/ppermute | solution.py:311
  7.1 16.1 %collective-permute-start = (f32[2,256,128]{2,1,0:T(8,128)S(1)}, f32[2,256,128]{2,1,0:T(8,128)S(1)}, u32[]{:S(2)}, u32[]{:S(2)}) collective-permute-start(f32[2,256,128]{2,1,0:T(8,128)S(1)} %pad_maximum_fusion.refs_0_), channel_id=1, source_target_pairs={{0,2},{2,3},{3,1},{1,0},{4,6},{6,7},{7,5},{5,4},{8,10},{10,11},{11... | collective-permute-start | bytes 786440 | tf_op jit(solution)/shard_map/ppermute | solution.py:311
  12.0 40.5 %collective-permute-start.8 = (f32[320,640]{1,0:T(8,128)}, f32[320,640]{1,0:T(8,128)}, u32[]{:S(2)}, u32[]{:S(2)}) collective-permute-start(f32[320,640]{1,0:T(8,128)} %get-tuple-element.137), channel_id=1, source_target_pairs={{0,24},{8,16},{16,8},{24,0},{1,25},{9,17},{17,9},{25,1},{2,26},{10... | collective-permute-start | bytes 2457608 | tf_op jit(solution)/shard_map/ppermute | solution.py:320
  14.5 38.0 %collective-permute-start.6 = (f32[320,640]{1,0:T(8,128)}, f32[320,640]{1,0:T(8,128)}, u32[]{:S(2)}, u32[]{:S(2)}) collective-permute-start(f32[320,640]{1,0:T(8,128)} %get-tuple-element.138), channel_id=1, source_target_pairs={{0,8},{8,0},{16,24},{24,16},{1,9},{9,1},{17,25},{25,17},{2,10},{10... | collective-permute-start | bytes 2457608 | tf_op jit(solution)/shard_map/ppermute | solution.py:320
  17.6 34.9 %collective-permute-start.7 = (f32[320,640]{1,0:T(8,128)}, f32[320,640]{1,0:T(8,128)}, u32[]{:S(2)}, u32[]{:S(2)}) collective-permute-start(f32[320,640]{1,0:T(8,128)} %get-tuple-element.140), channel_id=1, source_target_pairs={{0,16},{8,24},{16,0},{24,8},{1,17},{9,25},{17,1},{25,9},{2,18},{10... | collective-permute-start | bytes 2457608 | tf_op jit(solution)/shard_map/ppermute | solution.py:320
  23.9 22.1 %collective-permute-start.4 = (f32[3,256,128]{2,1,0:T(8,128)}, f32[3,256,128]{2,1,0:T(8,128)}, u32[]{:S(2)}, u32[]{:S(2)}) collective-permute-start(f32[3,256,128]{2,1,0:T(8,128)} %slice.65.refs_1_), channel_id=1, source_target_pairs={{0,2},{2,3},{3,1},{1,0},{4,6},{6,7},{7,5},{5,4},{8,10},{10,11},{11... | collective-permute-start | bytes 1179656 | tf_op jit(solution)/shard_map/ppermute | solution.py:311
  32.4 13.5 %collective-permute-start.3 = (f32[2,256,128]{2,1,0:T(8,128)}, f32[2,256,128]{2,1,0:T(8,128)}, u32[]{:S(2)}, u32[]{:S(2)}) collective-permute-start(f32[2,256,128]{2,1,0:T(8,128)} %slice.64.refs_0_), channel_id=1, source_target_pairs={{0,2},{2,3},{3,1},{1,0},{4,6},{6,7},{7,5},{5,4},{8,10},{10,11},{11... | collective-permute-start | bytes 786440 | tf_op jit(solution)/shard_map/ppermute | solution.py:311
  45.9 16.7 %collective-permute-start.5 = (f32[256,640]{1,0:T(8,128)}, f32[256,640]{1,0:T(8,128)}, u32[]{:S(2)}, u32[]{:S(2)}) collective-permute-start(f32[256,640]{1,0:T(8,128)} %attend.2.refs_0_), channel_id=1, source_target_pairs={{0,1},{2,0},{3,2},{1,3},{4,5},{6,4},{7,6},{5,7},{8,9},{10,8},{11,1... | collective-permute-start | bytes 1966088 | tf_op jit(solution)/shard_map/ppermute | solution.py:311
  56.8 3.0 %collective-permute-start.9 = (f32[128,640]{1,0:T(8,128)S(1)}, f32[128,640]{1,0:T(8,128)S(1)}, u32[]{:S(2)}, u32[]{:S(2)}) collective-permute-start(f32[128,640]{1,0:T(8,128)S(1)} %get-tuple-element.90), channel_id=1, source_target_pairs={{0,4},{4,0},{1,5},{5,1},{2,6},{6,2},{3,7},{7,3},{8,12},{12,8},{9,1... | collective-permute-start | bytes 983048 | tf_op jit(solution)/shard_map/ppermute | solution.py:312
  56.9 3.0 %collective-permute-start.10 = (f32[128,640]{1,0:T(8,128)S(1)}, f32[128,640]{1,0:T(8,128)S(1)}, u32[]{:S(2)}, u32[]{:S(2)}) collective-permute-start(f32[128,640]{1,0:T(8,128)S(1)} %get-tuple-element.91), channel_id=1, source_target_pairs={{0,4},{4,0},{1,5},{5,1},{2,6},{6,2},{3,7},{7,3},{8,12},{12,8},{9,1... | collective-permute-start | bytes 983048 | tf_op jit(solution)/shard_map/ppermute | solution.py:312
  57.4 2.5 %collective-permute-start.11 = (f32[128,640]{1,0:T(8,128)S(1)}, f32[128,640]{1,0:T(8,128)S(1)}, u32[]{:S(2)}, u32[]{:S(2)}) collective-permute-start(f32[128,640]{1,0:T(8,128)S(1)} %get-tuple-element.92), channel_id=1, source_target_pairs={{0,4},{4,0},{1,5},{5,1},{2,6},{6,2},{3,7},{7,3},{8,12},{12,8},{9,1... | collective-permute-start | bytes 983048 | tf_op jit(solution)/shard_map/ppermute | solution.py:312
  57.4 2.4 %collective-permute-start.12 = (f32[128,640]{1,0:T(8,128)S(1)}, f32[128,640]{1,0:T(8,128)S(1)}, u32[]{:S(2)}, u32[]{:S(2)}) collective-permute-start(f32[128,640]{1,0:T(8,128)S(1)} %get-tuple-element.93), channel_id=1, source_target_pairs={{0,4},{4,0},{1,5},{5,1},{2,6},{6,2},{3,7},{7,3},{8,12},{12,8},{9,1... | collective-permute-start | bytes 983048 | tf_op jit(solution)/shard_map/ppermute | solution.py:312
  65.1 6.4 %collective-permute-start.13 = (f32[128,640]{1,0:T(8,128)S(1)}, f32[128,640]{1,0:T(8,128)S(1)}, u32[]{:S(2)}, u32[]{:S(2)}) collective-permute-start(f32[128,640]{1,0:T(8,128)S(1)} %get-tuple-element.110), channel_id=1, source_target_pairs={{0,4},{4,0},{1,5},{5,1},{2,6},{6,2},{3,7},{7,3},{8,12},{12,8},{9,1... | collective-permute-start | bytes 983048 | tf_op jit(solution)/shard_map/ppermute | solution.py:312
  65.1 6.3 %collective-permute-start.14 = (f32[128,640]{1,0:T(8,128)S(1)}, f32[128,640]{1,0:T(8,128)S(1)}, u32[]{:S(2)}, u32[]{:S(2)}) collective-permute-start(f32[128,640]{1,0:T(8,128)S(1)} %get-tuple-element.111), channel_id=1, source_target_pairs={{0,4},{4,0},{1,5},{5,1},{2,6},{6,2},{3,7},{7,3},{8,12},{12,8},{9,1... | collective-permute-start | bytes 983048 | tf_op jit(solution)/shard_map/ppermute | solution.py:312
  65.6 9.7 %collective-permute-start.15 = (f32[2,2,32,640]{3,2,1,0:T(8,128)S(1)}, f32[2,2,32,640]{3,2,1,0:T(8,128)S(1)}, u32[]{:S(2)}, u32[]{:S(2)}) collective-permute-start(f32[2,2,32,640]{3,2,1,0:T(8,128)S(1)} %get-tuple-element.113), channel_id=1, source_target_pairs={{0,8},{8,0},{16,24},{24,16},{1,9},{9,1},{17,25},{25,17},{2,10},{10... | collective-permute-start | bytes 983048 | tf_op jit(solution)/shard_map/ppermute | solution.py:320
  67.1 9.4 %collective-permute-start.16 = (f32[2,2,32,640]{3,2,1,0:T(8,128)S(1)}, f32[2,2,32,640]{3,2,1,0:T(8,128)S(1)}, u32[]{:S(2)}, u32[]{:S(2)}) collective-permute-start(f32[2,2,32,640]{3,2,1,0:T(8,128)S(1)} %get-tuple-element.114), channel_id=1, source_target_pairs={{0,16},{8,24},{16,0},{24,8},{1,17},{9,25},{17,1},{25,9},{2,18},{10... | collective-permute-start | bytes 983048 | tf_op jit(solution)/shard_map/ppermute | solution.py:320
  68.6 16.2 %collective-permute-start.19 = (f32[256,640]{1,0:T(8,128)S(1)}, f32[256,640]{1,0:T(8,128)S(1)}, u32[]{:S(2)}, u32[]{:S(2)}) collective-permute-start(f32[256,640]{1,0:T(8,128)S(1)} %copy-done.1), channel_id=1, source_target_pairs={{0,2},{2,3},{3,1},{1,0},{4,6},{6,7},{7,5},{5,4},{8,10},{10,11},{11... | collective-permute-start | bytes 1966088 | tf_op jit(solution)/shard_map/ppermute | solution.py:311
  76.6 15.2 %collective-permute-start.17 = (f32[2,32,640]{2,1,0:T(8,128)S(1)}, f32[2,32,640]{2,1,0:T(8,128)S(1)}, u32[]{:S(2)}, u32[]{:S(2)}) collective-permute-start(f32[2,32,640]{2,1,0:T(8,128)S(1)} %slice_bitcast_fusion.2), channel_id=1, source_target_pairs={{0,16},{8,24},{16,0},{24,8},{1,17},{9,25},{17,1},{25,9},{2,18},{10... | collective-permute-start | bytes 491528 | tf_op jit(solution)/shard_map/ppermute | solution.py:320
  78.2 6.6 %collective-permute-start.20 = (f32[2,1,32,640]{3,2,1,0:T(8,128)S(1)}, f32[2,1,32,640]{3,2,1,0:T(8,128)S(1)}, u32[]{:S(2)}, u32[]{:S(2)}) collective-permute-start(f32[2,1,32,640]{3,2,1,0:T(8,128)S(1)} %get-tuple-element.119), channel_id=1, source_target_pairs={{0,8},{8,0},{16,24},{24,16},{1,9},{9,1},{17,25},{25,17},{2,10},{10... | collective-permute-start | bytes 491528 | tf_op jit(solution)/shard_map/ppermute | solution.py:320
  78.7 6.5 %collective-permute-start.21 = (f32[2,1,32,640]{3,2,1,0:T(8,128)S(1)}, f32[2,1,32,640]{3,2,1,0:T(8,128)S(1)}, u32[]{:S(2)}, u32[]{:S(2)}) collective-permute-start(f32[2,1,32,640]{3,2,1,0:T(8,128)S(1)} %get-tuple-element.120), channel_id=1, source_target_pairs={{0,16},{8,24},{16,0},{24,8},{1,17},{9,25},{17,1},{25,9},{2,18},{10... | collective-permute-start | bytes 491528 | tf_op jit(solution)/shard_map/ppermute | solution.py:320
  79.3 13.5 %collective-permute-start.18 = (f32[2,32,640]{2,1,0:T(8,128)S(1)}, f32[2,32,640]{2,1,0:T(8,128)S(1)}, u32[]{:S(2)}, u32[]{:S(2)}) collective-permute-start(f32[2,32,640]{2,1,0:T(8,128)S(1)} %slice_bitcast_fusion.1), channel_id=1, source_target_pairs={{0,8},{8,0},{16,24},{24,16},{1,9},{9,1},{17,25},{25,17},{2,10},{10... | collective-permute-start | bytes 491528 | tf_op jit(solution)/shard_map/ppermute | solution.py:320
  86.4 3.9 %collective-permute-start.25 = (f32[128,640]{1,0:T(8,128)S(1)}, f32[128,640]{1,0:T(8,128)S(1)}, u32[]{:S(2)}, u32[]{:S(2)}) collective-permute-start(f32[128,640]{1,0:T(8,128)S(1)} %get-tuple-element.128), channel_id=1, source_target_pairs={{0,4},{4,0},{1,5},{5,1},{2,6},{6,2},{3,7},{7,3},{8,12},{12,8},{9,1... | collective-permute-start | bytes 983048 | tf_op jit(solution)/shard_map/ppermute | solution.py:312
  86.9 5.9 %collective-permute-start.22 = (f32[1,32,640]{2,1,0:T(8,128)S(1)}, f32[1,32,640]{2,1,0:T(8,128)S(1)}, u32[]{:S(2)}, u32[]{:S(2)}) collective-permute-start(f32[1,32,640]{2,1,0:T(8,128)S(1)} %slice_bitcast_fusion.11), channel_id=1, source_target_pairs={{0,16},{8,24},{16,0},{24,8},{1,17},{9,25},{17,1},{25,9},{2,18},{10... | collective-permute-start | bytes 245768 | tf_op jit(solution)/shard_map/ppermute | solution.py:320
  88.5 4.9 %collective-permute-start.23 = (f32[1,32,640]{2,1,0:T(8,128)S(1)}, f32[1,32,640]{2,1,0:T(8,128)S(1)}, u32[]{:S(2)}, u32[]{:S(2)}) collective-permute-start(f32[1,32,640]{2,1,0:T(8,128)S(1)} %slice_bitcast_fusion.10), channel_id=1, source_target_pairs={{0,8},{8,0},{16,24},{24,16},{1,9},{9,1},{17,25},{25,17},{2,10},{10... | collective-permute-start | bytes 245768 | tf_op jit(solution)/shard_map/ppermute | solution.py:320
  90.4 6.3 %collective-permute-start.27 = (f32[2,1,32,640]{3,2,1,0:T(8,128)S(1)}, f32[2,1,32,640]{3,2,1,0:T(8,128)S(1)}, u32[]{:S(2)}, u32[]{:S(2)}) collective-permute-start(f32[2,1,32,640]{3,2,1,0:T(8,128)S(1)} %get-tuple-element.129), channel_id=1, source_target_pairs={{0,8},{8,0},{16,24},{24,16},{1,9},{9,1},{17,25},{25,17},{2,10},{10... | collective-permute-start | bytes 491528 | tf_op jit(solution)/shard_map/ppermute | solution.py:320
  91.8 5.8 %collective-permute-start.29 = (f32[2,1,32,640]{3,2,1,0:T(8,128)S(1)}, f32[2,1,32,640]{3,2,1,0:T(8,128)S(1)}, u32[]{:S(2)}, u32[]{:S(2)}) collective-permute-start(f32[2,1,32,640]{3,2,1,0:T(8,128)S(1)} %get-tuple-element.130), channel_id=1, source_target_pairs={{0,16},{8,24},{16,0},{24,8},{1,17},{9,25},{17,1},{25,9},{2,18},{10... | collective-permute-start | bytes 491528 | tf_op jit(solution)/shard_map/ppermute | solution.py:320
  93.6 10.5 %collective-permute-start.26 = (f32[64,640]{1,0:T(8,128)S(1)}, f32[64,640]{1,0:T(8,128)S(1)}, u32[]{:S(2)}, u32[]{:S(2)}) collective-permute-start(f32[64,640]{1,0:T(8,128)S(1)} %get-tuple-element.141), channel_id=1, source_target_pairs={{0,1},{2,0},{3,2},{1,3},{4,5},{6,4},{7,6},{5,7},{8,9},{10,8},{11,1... | collective-permute-start | bytes 491528 | tf_op jit(solution)/shard_map/ppermute | solution.py:311
  94.2 9.9 %collective-permute-start.32 = (f32[64,640]{1,0:T(8,128)S(1)}, f32[64,640]{1,0:T(8,128)S(1)}, u32[]{:S(2)}, u32[]{:S(2)}) collective-permute-start(f32[64,640]{1,0:T(8,128)S(1)} %maximum_bitcast_fusion.1), channel_id=1, source_target_pairs={{0,2},{2,3},{3,1},{1,0},{4,6},{6,7},{7,5},{5,4},{8,10},{10,11},{11... | collective-permute-start | bytes 491528 | tf_op jit(solution)/shard_map/ppermute | solution.py:311
  96.7 4.5 %collective-permute-start.28 = (f32[1,32,640]{2,1,0:T(8,128)S(1)}, f32[1,32,640]{2,1,0:T(8,128)S(1)}, u32[]{:S(2)}, u32[]{:S(2)}) collective-permute-start(f32[1,32,640]{2,1,0:T(8,128)S(1)} %slice_bitcast_fusion.8), channel_id=1, source_target_pairs={{0,16},{8,24},{16,0},{24,8},{1,17},{9,25},{17,1},{25,9},{2,18},{10... | collective-permute-start | bytes 245768 | tf_op jit(solution)/shard_map/ppermute | solution.py:320
  97.6 4.5 %collective-permute-start.30 = (f32[1,32,640]{2,1,0:T(8,128)S(1)}, f32[1,32,640]{2,1,0:T(8,128)S(1)}, u32[]{:S(2)}, u32[]{:S(2)}) collective-permute-start(f32[1,32,640]{2,1,0:T(8,128)S(1)} %slice_bitcast_fusion.6), channel_id=1, source_target_pairs={{0,8},{8,0},{16,24},{24,16},{1,9},{9,1},{17,25},{25,17},{2,10},{10... | collective-permute-start | bytes 245768 | tf_op jit(solution)/shard_map/ppermute | solution.py:320
  102.2 7.3 %collective-permute-start.31 = (f32[64,640]{1,0:T(8,128)S(1)}, f32[64,640]{1,0:T(8,128)S(1)}, u32[]{:S(2)}, u32[]{:S(2)}) collective-permute-start(f32[64,640]{1,0:T(8,128)S(1)} %maximum_bitcast_fusion), channel_id=1, source_target_pairs={{0,3},{2,1},{3,0},{1,2},{4,7},{6,5},{7,4},{5,6},{8,11},{10,9},{11,... | collective-permute-start | bytes 491528 | tf_op jit(solution)/shard_map/ppermute | solution.py:311
  (7 other events, 26.9 us)
